TPU v7x, 32 devices: a whole 2x2x4 slice. The times are simulated.
32 devices in a mesh: row: 4 (over z), col: 8 (over y, x, core).
Axes of the slice: x: 2, y: 2, z: 4, core: 2. Of those that a mesh axis runs over, the one named last changes fastest.
Arguments:
- inputs: bfloat16 [512, 8192], P('row', 'col'), may hold values from -6 to 6
- grad_out: bfloat16 [512, 8192], P('row', 'col'), may hold values from -0.1796875 to 0.1796875
- gate_pre: bfloat16 [512, 28672], P('col', 'row'), may hold values from -6 to 6
- up_pre: bfloat16 [512, 28672], P('col', 'row'), may hold values from -6 to 6
- w_gate: bfloat16 [8192, 28672], P('col', 'row'), may hold values from -0.25 to 0.25
- w_up: bfloat16 [8192, 28672], P('col', 'row'), may hold values from -0.25 to 0.25
- w_down: bfloat16 [28672, 8192], P('row', 'col'), may hold values from -0.03125 to 0.03125
Outputs:
- grad_inputs: bfloat16 [512, 8192], P('row', 'col')
- grad_gate: bfloat16 [8192, 28672], P('col', 'row')
- grad_up: bfloat16 [8192, 28672], P('col', 'row')
- grad_down: bfloat16 [28672, 8192], P('row', 'col')
All inputs are finite; a program needn't handle non-finite values.
Results may differ from a plain program's by a relative error of at most 0.005.
Values may be sent and summed in bfloat16 or wider, within the bound.
No kernel may reach another device: no remote copies, remote signals or barrier semaphores. Data moves between devices by JAX's collectives and lax.ppermute only.
A program may use at most 192 MiB of HBM per device.

v0:
```python
import jax
import jax.numpy as jnp
from jax import lax
from jax.sharding import PartitionSpec as P


def swiglu_back(gate_pre, up_pre, hidden_grad):
    gate_wide = gate_pre.astype(jnp.float32)
    up_wide = up_pre.astype(jnp.float32)
    logistic = jax.nn.sigmoid(gate_wide)
    swished = gate_wide * logistic
    hidden = (swished * up_wide).astype(jnp.bfloat16)
    up_grad = (hidden_grad * swished).astype(jnp.bfloat16)
    gate_grad = (hidden_grad * up_wide * logistic * (1.0 + gate_wide * (1.0 - logistic))).astype(
        jnp.bfloat16
    )
    return (hidden, gate_grad, up_grad)


def on_device(inputs, grad_out, gate_pre, up_pre, w_gate, w_up, w_down):
    last_last = (((1,), (1,)), ((), ()))
    first_first = (((0,), (0,)), ((), ()))
    inputs_all, grad_out_all = (
        lax.all_gather(inputs, "row", axis=0, tiled=True),
        lax.all_gather(grad_out, "row", axis=0, tiled=True),
    )
    hidden_grad = lax.psum_scatter(
        lax.dot_general(grad_out_all, w_down, last_last, preferred_element_type=jnp.float32),
        "col",
        scatter_dimension=0,
        tiled=True,
    )
    hidden, gate_grad, up_grad = swiglu_back(gate_pre, up_pre, hidden_grad)
    hidden_all, gate_grad_all, up_grad_all = (
        lax.all_gather(hidden, "col", axis=0, tiled=True),
        lax.all_gather(gate_grad, "col", axis=0, tiled=True),
        lax.all_gather(up_grad, "col", axis=0, tiled=True),
    )
    grad_down = lax.dot_general(
        hidden_all, grad_out_all, first_first, preferred_element_type=jnp.float32
    ).astype(jnp.bfloat16)
    grad_gate = lax.dot_general(
        inputs_all, gate_grad_all, first_first, preferred_element_type=jnp.float32
    ).astype(jnp.bfloat16)
    grad_up = lax.dot_general(
        inputs_all, up_grad_all, first_first, preferred_element_type=jnp.float32
    ).astype(jnp.bfloat16)
    summed = lax.dot_general(gate_grad_all, w_gate, last_last, preferred_element_type=jnp.float32)
    grad_inputs = lax.psum_scatter(
        summed + lax.dot_general(up_grad_all, w_up, last_last, preferred_element_type=jnp.float32),
        "row",
        scatter_dimension=0,
        tiled=True,
    ).astype(jnp.bfloat16)
    return (grad_inputs, grad_gate, grad_up, grad_down)


def solution(mesh):
    placed = (
        P("row", "col"),
        P("row", "col"),
        P("col", "row"),
        P("col", "row"),
        P("col", "row"),
        P("col", "row"),
        P("row", "col"),
    )
    return jax.shard_map(
        on_device,
        mesh=mesh,
        in_specs=placed,
        out_specs=(P("row", "col"), P("col", "row"), P("col", "row"), P("row", "col")),
        check_vma=False,
    )
```

profile of v0, /device:TPU:0, one launch (start us, length us, event | category | flops | bytes accessed | tf_op | source)
XLA Modules:
  0.0 399.6 jit_solution(8280445584553674023)
XLA Ops:
  7.2 0.0 all-gather.6.cloned.1.call-start
  7.2 0.7 all-gather.6.cloned.1.call-update
  7.9 0.0 reduce-scatter.3.cloned.1.call-start
  7.9 32.3 %all-gather.6.cloned.1.call-done = bf16[512,1024]{1,0:T(8,128)(2,1)} async-done(((bf16[128,1024]{1,0:T(8,128)(2,1)}), bf16[512,1024]{1,0:T(8,128)(2,1)}) %all-gather.6.cloned.1.call-update) | async-done | bytes 1048592 | tf_op jit(solution)/shard_map/all_gather | solution.py:25
  40.2 14.4 %fusion.8 = f32[512,7168]{1,0:T(8,128)} fusion(bf16[512,1024]{1,0:T(8,128)(2,1)} %all-gather.6.cloned.1.call-done, bf16[7168,1024]{1,0:T(8,128)(2,1)} %param.13), kind=kOutput, calls=%fused_computation.18 | convolution fusion | flops 7516192768 | bytes 30408704 | tf_op jit(solution)/shard_map/dot_general | solution.py:28
  54.7 0.0 copy-start
  54.7 0.0 copy-start.1
  54.7 0.0 reduce-scatter.3.cloned.1.call-update
  54.7 0.0 all-gather.8.cloned.1.call-start
  54.7 103.1 %reduce-scatter.3.cloned.1.call-done = f32[64,7168]{1,0:T(8,128)} async-done(((f32[512,7168]{1,0:T(8,128)}), f32[64,7168]{1,0:T(8,128)}) %reduce-scatter.3.cloned.1.call-update) | async-done | bytes 1835024 | tf_op jit(solution)/shard_map/reduce_scatter | solution.py:27
  157.9 0.0 copy-done
  157.9 0.0 copy-done.1
  157.9 3.9 multiply_convert_fusion
  161.8 0.0 all-gather.8.cloned.1.call-update
  161.8 0.0 all-gather.10.cloned.1.call-start
  161.8 0.5 all-gather.10.cloned.1.call-update
  162.4 0.0 all-gather.12.cloned.1.call-start
  162.4 0.5 all-gather.12.cloned.1.call-update
  163.0 0.0 all-gather.14.cloned.1.call-start
  163.0 0.5 all-gather.14.cloned.1.call-update
  163.5 0.2 reduce-scatter.5.cloned.1.call-start
  163.8 48.1 %all-gather.8.cloned.1.call-done = bf16[512,7168]{1,0:T(8,128)(2,1)} async-done(((bf16[64,7168]{1,0:T(8,128)(2,1)}), bf16[512,7168]{1,0:T(8,128)(2,1)}) %all-gather.8.cloned.1.call-update) | async-done | bytes 7340048 | tf_op jit(solution)/shard_map/all_gather | solution.py:36
  211.9 13.2 %fusion.9 = f32[512,1024]{1,0:T(8,128)S(1)} fusion(bf16[512,7168]{1,0:T(8,128)(2,1)} %all-gather.8.cloned.1.call-done, bf16[1024,7168]{1,0:T(8,128)(2,1)} %param.11), kind=kOutput, calls=%fused_computation.19 | convolution fusion | flops 7516192768 | bytes 24117248 | tf_op jit(solution)/shard_map/dot_general | solution.py:48
  225.1 39.1 %all-gather.10.cloned.1.call-done = bf16[512,7168]{1,0:T(8,128)(2,1)} async-done(((bf16[64,7168]{1,0:T(8,128)(2,1)}), bf16[512,7168]{1,0:T(8,128)(2,1)}) %all-gather.10.cloned.1.call-update) | async-done | bytes 7340048 | tf_op jit(solution)/shard_map/all_gather | solution.py:37
  264.2 14.2 %convolution_add_fusion = f32[512,1024]{1,0:T(8,128)} fusion(f32[512,1024]{1,0:T(8,128)S(1)} %fusion.9, bf16[512,7168]{1,0:T(8,128)(2,1)} %all-gather.10.cloned.1.call-done, bf16[1024,7168]{1,0:T(8,128)(2,1)} %param.12), kind=kOutput, calls=%fused_computation.17 | convolution fusion | flops 7516717056 | bytes 26214400 | tf_op jit(solution)/shard_map/dot_general | solution.py:50
  278.4 0.0 reduce-scatter.5.cloned.1.call-update
  278.4 15.2 %all-gather.12.cloned.1.call-done = bf16[512,1024]{1,0:T(8,128)(2,1)} async-done(((bf16[128,1024]{1,0:T(8,128)(2,1)}), bf16[512,1024]{1,0:T(8,128)(2,1)}) %all-gather.12.cloned.1.call-update) | async-done | bytes 1048592 | tf_op jit(solution)/shard_map/all_gather | solution.py:24
  293.6 13.5 %convert_bitcast_fusion.1 = bf16[1024,7168]{0,1:T(8,128)(2,1)} fusion(bf16[512,7168]{1,0:T(8,128)(2,1)} %all-gather.8.cloned.1.call-done, bf16[512,1024]{1,0:T(8,128)(2,1)} %all-gather.12.cloned.1.call-done), kind=kOutput, calls=%fused_computation.1 | convolution fusion | flops 7523532800 | bytes 23068672 | tf_op jit(solution)/shard_map/dot_general | solution.py:42
  307.0 0.0 copy-start.3
  307.0 19.8 %copy.11 = bf16[1024,7168]{1,0:T(8,128)(2,1)} copy(bf16[1024,7168]{0,1:T(8,128)(2,1)} %convert_bitcast_fusion.1) | data formatting | bytes 29360128
  326.8 0.0 copy-done.3
  326.8 14.3 %convert_bitcast_fusion = bf16[1024,7168]{0,1:T(8,128)(2,1)} fusion(bf16[512,7168]{1,0:T(8,128)(2,1)} %all-gather.10.cloned.1.call-done, bf16[512,1024]{1,0:T(8,128)(2,1)S(1)} %copy-done.3), kind=kOutput, calls=%fused_computation | convolution fusion | flops 7523532800 | bytes 23068672 | tf_op jit(solution)/shard_map/dot_general | solution.py:45
  341.1 0.0 copy-start.2
  341.1 20.0 %copy.12 = bf16[1024,7168]{1,0:T(8,128)(2,1)} copy(bf16[1024,7168]{0,1:T(8,128)(2,1)} %convert_bitcast_fusion) | data formatting | bytes 29360128
  361.2 0.0 all-gather.14.cloned.1.call-done
  361.2 0.0 copy-done.2
  361.2 14.3 %convolution_convert_fusion = bf16[7168,1024]{1,0:T(8,128)(2,1)} fusion(bf16[512,7168]{1,0:T(8,128)(2,1)} %all-gather.14.cloned.1.call-done, bf16[512,1024]{1,0:T(8,128)(2,1)S(1)} %copy-done.2), kind=kOutput, calls=%fused_computation.2 | convolution fusion | flops 7523532800 | bytes 23068672 | tf_op jit(solution)/shard_map/dot_general | solution.py:39
  375.4 15.6 %reduce-scatter.5.cloned.1.call-done = f32[128,1024]{1,0:T(8,128)} async-done(((f32[512,1024]{1,0:T(8,128)}), f32[128,1024]{1,0:T(8,128)}) %reduce-scatter.5.cloned.1.call-update) | async-done | bytes 524304 | tf_op jit(solution)/shard_map/reduce_scatter | solution.py:49
  391.0 1.8 convert_element_type.37
Async XLA Ops:
  7.2 33.1 %all-gather.6.cloned.1.call-start = ((), (), s32[]{:S(2)}) async-start(), calls=%async_computation.2 | async-start | bytes 1310720 | tf_op jit(solution)/shard_map/all_gather | solution.py:25
  7.9 150.0 %reduce-scatter.3.cloned.1.call-start = ((), (), s32[]{:S(2)}) async-start(), calls=%async_computation.3 | async-start | bytes 16515072 | tf_op jit(solution)/shard_map/reduce_scatter | solution.py:27
  54.7 103.2 %copy-start = (bf16[64,7168]{1,0:T(8,128)(2,1)S(1)}, bf16[64,7168]{1,0:T(8,128)(2,1)}, u32[]{:S(2)}) copy-start(bf16[64,7168]{1,0:T(8,128)(2,1)} %param.9) | copy-start | bytes 2752516
  54.7 103.2 %copy-start.1 = (bf16[64,7168]{1,0:T(8,128)(2,1)S(1)}, bf16[64,7168]{1,0:T(8,128)(2,1)}, u32[]{:S(2)}) copy-start(bf16[64,7168]{1,0:T(8,128)(2,1)} %param.10) | copy-start | bytes 2752516
  54.7 157.2 %all-gather.8.cloned.1.call-start = ((), (), s32[]{:S(2)}) async-start(), calls=%async_computation.4 | async-start | bytes 8257536 | tf_op jit(solution)/shard_map/all_gather | solution.py:36
  161.8 102.4 %all-gather.10.cloned.1.call-start = ((), (), s32[]{:S(2)}) async-start(), calls=%async_computation.5 | async-start | bytes 8257536 | tf_op jit(solution)/shard_map/all_gather | solution.py:37
  162.4 131.2 %all-gather.12.cloned.1.call-start = ((), (), s32[]{:S(2)}) async-start(), calls=%async_computation.7 | async-start | bytes 1310720 | tf_op jit(solution)/shard_map/all_gather | solution.py:24
  163.0 198.2 %all-gather.14.cloned.1.call-start = ((), (), s32[]{:S(2)}) async-start(), calls=%async_computation.8 | async-start | bytes 8257536 | tf_op jit(solution)/shard_map/all_gather | solution.py:35
  163.5 227.5 %reduce-scatter.5.cloned.1.call-start = ((), (), s32[]{:S(2)}) async-start(), calls=%async_computation.6 | async-start | bytes 2621440 | tf_op jit(solution)/shard_map/reduce_scatter | solution.py:49
  307.0 19.8 %copy-start.3 = (bf16[512,1024]{1,0:T(8,128)(2,1)S(1)}, bf16[512,1024]{1,0:T(8,128)(2,1)}, u32[]{:S(2)}) copy-start(bf16[512,1024]{1,0:T(8,128)(2,1)} %all-gather.12.cloned.1.call-done) | copy-start | bytes 3145732
  341.1 20.0 %copy-start.2 = (bf16[512,1024]{1,0:T(8,128)(2,1)S(1)}, bf16[512,1024]{1,0:T(8,128)(2,1)}, u32[]{:S(2)}) copy-start(bf16[512,1024]{1,0:T(8,128)(2,1)} %all-gather.6.cloned.1.call-done) | copy-start | bytes 3145732
Sparse Core Ops, SparseCore 0:
  9.6 30.6 all-gather.5
  54.8 103.0 reduce-scatter.2
  161.9 49.9 all-gather.7
  214.2 49.9 all-gather.9
  265.6 27.9 all-gather.11
  295.3 49.4 all-gather.13
  347.1 43.8 reduce-scatter.4
where the time goes:
time: 401 us; the launch traced here: 400 us
  waiting for transfers between devices  256 us (64%)
  matrix products  83.8 us (21%)
  local copies, waits for them, and re-layouts  39.8 us (10%)
  between operations  14.1 us (4%)
  other arithmetic  5.66 us (1%)
    reduce_scatter x1, waiting for transfers between devices, on_device(): lax.psum_scatter(lax.dot_general(grad_out_all, w_down, last_last, preferr...  103 us
    all_gather x1, waiting for transfers between devices, on_device(): lax.all_gather(gate_grad, 'col', axis=0, tiled=True)  48.1 us
    unnamed x10, local copies, waits for them, and re-layouts  39.8 us
    all_gather x1, waiting for transfers between devices, on_device(): lax.all_gather(up_grad, 'col', axis=0, tiled=True)  39.1 us
    all_gather x1, waiting for transfers between devices, on_device(): lax.all_gather(grad_out, 'row', axis=0, tiled=True)  32.3 us
    reduce_scatter x1, waiting for transfers between devices, on_device(): lax.psum_scatter(summed + lax.dot_general(up_grad_all, w_up, last_last, p...  15.6 us
    all_gather x1, waiting for transfers between devices, on_device(): lax.all_gather(inputs, 'row', axis=0, tiled=True)  15.2 us
    dot_general x1, matrix products, on_device(): lax.dot_general(grad_out_all, w_down, last_last, preferred_element_type=j...  14.4 us
  transfers between devices with their start and end apart: 7, of which 6 were waited for; matrix products, arithmetic and copies ran while one was open for 27% of the time, Pallas kernels for 0%

commit v1 on v0

v1 whole, which is shorter than its diff:
```python
import functools

import jax
import jax.numpy as jnp
from jax import lax
from jax.experimental import pallas as pl
from jax.experimental.pallas import tpu as pltpu
from jax.sharding import PartitionSpec as P

BF16, F32 = jnp.bfloat16, jnp.float32
VMEM_BYTES = 56 * 1024 * 1024


def dot(a, b, a_dim, b_dim):
    return lax.dot_general(a, b, (((a_dim,), (b_dim,)), ((), ())), preferred_element_type=F32)


def logistic_of(wide):
    return 0.5 + 0.5 * jnp.tanh(0.5 * wide)


def swiglu_back(gate_pre, up_pre, hidden_grad):
    gate_wide = gate_pre.astype(F32)
    up_wide = up_pre.astype(F32)
    logistic = logistic_of(gate_wide)
    swished = gate_wide * logistic
    up_grad = (hidden_grad * swished).astype(BF16)
    gate_grad = (hidden_grad * up_wide * logistic * (1.0 + gate_wide * (1.0 - logistic))).astype(BF16)
    return gate_grad, up_grad


def hidden_of(gate_pre, up_pre):
    gate_wide = gate_pre.astype(F32)
    return (gate_wide * logistic_of(gate_wide) * up_pre.astype(F32)).astype(BF16)


def params():
    return pltpu.CompilerParams(vmem_limit_bytes=VMEM_BYTES)


def after(array, before):
    return lax.optimization_barrier((array, before))[0]


def whole_block(shape):
    return pl.BlockSpec(shape, lambda *_: (0,) * len(shape))


def swap(array, bit):
    return lax.ppermute(array, "col", [(i, i ^ bit) for i in range(8)])


def onward(array, rows, step):
    return lax.ppermute(array, "row", [(i, (i + step) % rows) for i in range(rows)])


def token_block(place, col):
    return (((place << 1) & 7) | (place >> 2)) ^ col


def place_of(block, col):
    offset = block ^ col
    return (offset >> 1) + 4 * (offset & 1)


def arrange(where, blocks):
    rows, (count, features) = len(blocks), blocks[0].shape
    tokens = rows * count
    part = tokens // 8

    def kernel(where_ref, *refs):
        *ins, out = refs
        row, col = where_ref[0], where_ref[1]
        for step, ref in enumerate(ins):
            owner = lax.rem(row + (rows - step), rows)
            for at in range(8 // rows):
                start = pl.multiple_of(place_of(owner * (8 // rows) + at, col) * part, part)
                out[pl.ds(start, part), :] = ref[at * part : (at + 1) * part, :]

    return pl.pallas_call(
        kernel,
        out_shape=jax.ShapeDtypeStruct((tokens, features), BF16),
        in_specs=[pl.BlockSpec(memory_space=pltpu.SMEM)] + [pl.BlockSpec(memory_space=pltpu.VMEM)] * rows,
        out_specs=pl.BlockSpec(memory_space=pltpu.VMEM),
        compiler_params=params(),
        name="arrange",
    )(where, *blocks)


def reorder(where, natural):
    tokens, features = natural.shape
    part = tokens // 8

    def kernel(where_ref, x, out):
        for place in range(8):
            start = pl.multiple_of(token_block(place, where_ref[1]) * part, part)
            out[place * part : (place + 1) * part, :] = x[pl.ds(start, part), :]

    return pl.pallas_call(
        kernel,
        out_shape=jax.ShapeDtypeStruct((tokens, features), BF16),
        in_specs=[pl.BlockSpec(memory_space=pltpu.SMEM), pl.BlockSpec(memory_space=pltpu.VMEM)],
        out_specs=pl.BlockSpec(memory_space=pltpu.VMEM),
        compiler_params=params(),
        name="reorder",
    )(where, natural)


def sum_rows(blocks):
    def kernel(own, *refs):
        *ins, out = refs
        total = own[...]
        for ref in ins:
            total = total + ref[...].astype(F32)
        out[...] = total.astype(BF16)

    return pl.pallas_call(
        kernel,
        out_shape=jax.ShapeDtypeStruct(blocks[0].shape, BF16),
        compiler_params=params(),
        name="sum_rows",
    )(*blocks)


def partial_hidden_grad(here, there, w_here, w_there, start, size, tile):
    tokens, features = here.shape
    part = tokens // 4

    def kernel(x, y, w, v, own, for_x, for_y, for_far):
        product = dot(x[...], w[...], 1, 1) + dot(y[...], v[...], 1, 1)
        own[...] = product[:part]
        for_x[...] = product[part : 2 * part].astype(BF16)
        for_y[...] = product[2 * part : 3 * part].astype(BF16)
        for_far[...] = product[3 * part :].astype(BF16)

    column = pl.BlockSpec((part, tile), lambda i: (0, i))
    weights = pl.BlockSpec((tile, features), lambda i: (i + start // tile, 0))
    sent = jax.ShapeDtypeStruct((part, size), BF16)
    return pl.pallas_call(
        kernel,
        grid=(size // tile,),
        in_specs=[whole_block((tokens, features))] * 2 + [weights] * 2,
        out_specs=[column] * 4,
        out_shape=[jax.ShapeDtypeStruct((part, size), F32), sent, sent, sent],
        compiler_params=params(),
        name="partial_hidden_grad",
    )(here, there, w_here, w_there)


def total_hidden_grad(own, *received):
    def kernel(a, b, c, d, out):
        out[...] = (a[...] + b[...].astype(F32) + c[...].astype(F32) + d[...].astype(F32)).astype(BF16)

    return pl.pallas_call(
        kernel,
        out_shape=jax.ShapeDtypeStruct(own.shape, BF16),
        compiler_params=params(),
        name="total_hidden_grad",
    )(own, *received)


def spread_whole(block, over_x_first):
    at_x, at_y = swap(block, 2), swap(block, 4)
    return block, at_x, at_y, swap(at_x, 4) if over_x_first else swap(at_y, 2)


def unpack(block):
    part = block.shape[0] // 8
    gate = jnp.concatenate([block[2 * i * part : (2 * i + 1) * part] for i in range(4)], axis=0)
    up = jnp.concatenate([block[(2 * i + 1) * part : (2 * i + 2) * part] for i in range(4)], axis=0)
    return gate, up


def grad_down_part(stored, grad_out_all, grad_down, hidden_units, inside, start, size, tile):
    tokens, features = grad_out_all.shape

    def kernel(p0, p1, x, *rest):
        out = rest[-1]
        hidden = jnp.concatenate([hidden_of(*unpack(p0[...])), hidden_of(*unpack(p1[...]))], axis=0)
        out[...] = dot(hidden, x[...], 0, 0).astype(BF16)

    block = pl.BlockSpec((tokens, tile), lambda i: (0, i + inside // tile))
    earlier = [] if grad_down is None else [grad_down]
    return pl.pallas_call(
        kernel,
        grid=(size // tile,),
        in_specs=[block] * 2
        + [whole_block((tokens, features))]
        + [pl.BlockSpec(memory_space=pl.ANY)] * len(earlier),
        out_specs=pl.BlockSpec((tile, features), lambda i: (i + start // tile, 0)),
        out_shape=jax.ShapeDtypeStruct((hidden_units, features), BF16),
        input_output_aliases={3: 0} if earlier else {},
        compiler_params=params(),
        name="grad_down_part",
    )(*stored, grad_out_all, *earlier)


def both_gradients(where, hidden_grad, p0, p1):
    part = hidden_grad.shape[0] // 8
    rows = []
    for place in range(8):
        start = pl.multiple_of(token_block(place, where[1]) * part, part)
        rows.append(hidden_grad[pl.ds(start, part), :])
    a0, b0 = swiglu_back(*unpack(p0[...]), jnp.concatenate(rows[:4], axis=0).astype(F32))
    a1, b1 = swiglu_back(*unpack(p1[...]), jnp.concatenate(rows[4:], axis=0).astype(F32))
    return jnp.concatenate([a0, a1], axis=0), jnp.concatenate([b0, b1], axis=0)


def first_part(where, hidden_grad, stored, inputs_all, w_gate, w_up, size, tile):
    tokens, features = inputs_all.shape

    def kernel(where_ref, h, p0, p1, x, wg, wu, grad_gate, grad_up, total):
        gate_grad, up_grad = both_gradients(where_ref, h, p0, p1)
        grad_gate[...] = dot(x[...], gate_grad, 0, 0).astype(BF16)
        grad_up[...] = dot(x[...], up_grad, 0, 0).astype(BF16)
        more = dot(gate_grad, wg[...], 1, 1) + dot(up_grad, wu[...], 1, 1)

        @pl.when(pl.program_id(0) == 0)
        def _():
            total[...] = more

        @pl.when(pl.program_id(0) > 0)
        def _():
            total[...] += more

    block = pl.BlockSpec((tokens, tile), lambda i: (0, i))
    column = pl.BlockSpec((features, tile), lambda i: (0, i))
    weights = jax.ShapeDtypeStruct(w_gate.shape, BF16)
    return pl.pallas_call(
        kernel,
        grid=(size // tile,),
        in_specs=[pl.BlockSpec(memory_space=pltpu.SMEM)]
        + [block] * 3
        + [whole_block((tokens, features)), column, column],
        out_specs=[column, column, whole_block((tokens, features))],
        out_shape=[weights, weights, jax.ShapeDtypeStruct((tokens, features), F32)],
        compiler_params=params(),
        name="first_part",
    )(where, hidden_grad, *stored, inputs_all, w_gate, w_up)


def input_part(where, rows, hidden_grad, stored, w_gate, w_up, total, start, size, tile):
    tokens, features = total.shape
    part = tokens // 8
    steps = size // tile
    strip = features // steps

    def kernel(where_ref, h, p0, p1, wg, wu, before, gate_out, up_out, *rest):
        *outs, carry = rest
        gate_grad, up_grad = both_gradients(where_ref, h, p0, p1)
        gate_out[...] = gate_grad
        up_out[...] = up_grad
        more = dot(gate_grad, wg[...], 1, 1) + dot(up_grad, wu[...], 1, 1)
        step = pl.program_id(0)

        @pl.when(step == 0)
        def _():
            carry[...] = more

        @pl.when(step > 0)
        def _():
            carry[...] += more

        carry[:, pl.ds(pl.multiple_of(step * strip, strip), strip)] += before[...]

        @pl.when(step == steps - 1)
        def _():
            row, col = where_ref[0], where_ref[1]
            for ahead, out in enumerate(outs):
                owner = lax.rem(row + ahead, rows)
                for at in range(8 // rows):
                    place = pl.multiple_of(place_of(owner * (8 // rows) + at, col) * part, part)
                    out[at * part : (at + 1) * part, :] = carry[pl.ds(place, part), :].astype(out.dtype)

    block = pl.BlockSpec((tokens, tile), lambda i: (0, i))
    column = pl.BlockSpec((features, tile), lambda i: (0, i + start // tile))
    made = jax.ShapeDtypeStruct((tokens, size), BF16)
    shape = (tokens // rows, features)
    return pl.pallas_call(
        kernel,
        grid=(steps,),
        in_specs=[pl.BlockSpec(memory_space=pltpu.SMEM)]
        + [block] * 3
        + [column, column, pl.BlockSpec((tokens, strip), lambda i: (0, i))],
        out_specs=[block, block] + [whole_block(shape)] * rows,
        out_shape=[made, made]
        + [jax.ShapeDtypeStruct(shape, F32)]
        + [jax.ShapeDtypeStruct(shape, BF16)] * (rows - 1),
        scratch_shapes=[pltpu.VMEM((tokens, features), F32)],
        compiler_params=params(),
        name="input_part",
    )(where, hidden_grad, *stored, w_gate, w_up, total)


def weight_part(gate_grad, up_grad, inputs_all, grad_gate, grad_up, start, tile):
    tokens, features = inputs_all.shape
    size = gate_grad.shape[1]

    def kernel(a, b, x, _, __, gate_out, up_out):
        gate_out[...] = dot(x[...], a[...], 0, 0).astype(BF16)
        up_out[...] = dot(x[...], b[...], 0, 0).astype(BF16)

    block = pl.BlockSpec((tokens, tile), lambda i: (0, i))
    column = pl.BlockSpec((features, tile), lambda i: (0, i + start // tile))
    weights = jax.ShapeDtypeStruct(grad_gate.shape, BF16)
    return pl.pallas_call(
        kernel,
        grid=(size // tile,),
        in_specs=[block, block, whole_block((tokens, features))] + [pl.BlockSpec(memory_space=pl.ANY)] * 2,
        out_specs=[column, column],
        out_shape=[weights, weights],
        input_output_aliases={3: 0, 4: 1},
        compiler_params=params(),
        name="weight_part",
    )(gate_grad, up_grad, inputs_all, grad_gate, grad_up)


def pack(pieces):
    size = pieces[0].shape[1]
    tile = size // 2
    rows = [piece.shape[0] for piece in pieces]

    def kernel(*refs):
        *ins, out = refs
        start = 0
        for ref, count in zip(ins, rows):
            out[start : start + count, :] = ref[...]
            start += count

    return pl.pallas_call(
        kernel,
        grid=(2,),
        in_specs=[pl.BlockSpec((count, tile), lambda i: (0, i)) for count in rows],
        out_specs=pl.BlockSpec((sum(rows), tile), lambda i: (0, i)),
        out_shape=jax.ShapeDtypeStruct((sum(rows), size), BF16),
        compiler_params=params(),
        name="pack",
    )(*pieces)


def both_cores(pieces):
    mine = pack(pieces)
    return mine, swap(mine, 1)


def on_square(rows, inputs, grad_out, gate_pre, up_pre, w_gate, w_up, w_down):
    hidden_units = w_gate.shape[1]
    unit = 1024
    cut = 3 * unit
    chunks = ((0, cut), (cut, hidden_units - cut))
    part = gate_pre.shape[0]
    tokens = 8 * part
    where = jnp.stack([lax.axis_index("row"), lax.axis_index("col")]).astype(jnp.int32)

    def stack(at):
        start, size = chunks[at]
        return jnp.concatenate([gate_pre[:, start : start + size], up_pre[:, start : start + size]], axis=0)

    def hidden_part(at, before):
        start, size = chunks[at]
        own, *sent = partial_hidden_grad(after(here, before), grad_out_there, w_down, w_there, start, size, unit)
        return own, sent

    def send_hidden(sent):
        return [swap(block, bits) for block, bits in zip(sent, (2, 4, 6))]

    def down(at, grad_down, before):
        start, size = chunks[at]
        return grad_down_part(
            stored[at], after(grad_out_all, before), grad_down, hidden_units, 0, start, size, unit
        )

    stored = {}
    grad_out_all = arrange(where, [grad_out] + [onward(grad_out, rows, step) for step in range(1, rows)])
    w_there = swap(w_down, 1)
    both0, both1 = stack(0), stack(1)
    x0, y0 = swap(both0, 2), swap(both0, 4)
    far0 = [swap(x0[:part], 4), swap(y0[part:], 2)]
    x1, y1 = swap(both1, 2), swap(both1, 4)
    here = grad_out_all[: tokens // 2]
    grad_out_there = swap(grad_out_all[tokens // 2 :], 1)
    inputs_all = lax.all_gather(after(inputs, here), "row", axis=0, tiled=True)

    own0, sent0 = hidden_part(0, here)
    got0 = send_hidden(sent0)
    own1, sent1 = hidden_part(1, own0)
    x0, y0, *far0 = [after(piece, own1) for piece in (x0, y0, *far0)]
    stored[0] = both_cores([both0, x0, y0, *far0])
    x1, y1 = after(x1, stored[0][0]), after(y1, stored[0][0])
    far1 = [swap(x1[:part], 4), swap(y1[part:], 2)]
    hidden0 = total_hidden_grad(after(own0, (x1, y1)), *got0)
    hidden0_all = lax.all_gather(hidden0, "col", axis=0, tiled=True)
    got1 = send_hidden(sent1)
    inputs_all = reorder(where, after(inputs_all, hidden0))
    grad_down = down(0, None, inputs_all)
    hidden1 = total_hidden_grad(after(own1, grad_down), *got1)
    hidden1_all = lax.all_gather(hidden1, "col", axis=0, tiled=True)
    stored[1] = both_cores([after(piece, hidden1) for piece in (both1, x1, y1, *far1)])
    grad_gate, grad_up, total = first_part(
        where, hidden0_all, stored[0], after(inputs_all, stored[1][0]), w_gate, w_up, cut, unit // 2
    )
    gate_grad, up_grad, *sums = input_part(
        where, rows, hidden1_all, stored[1], w_gate, w_up, total, *chunks[1], unit // 2
    )
    sums = [sums[0]] + [onward(block, rows, ahead) for ahead, block in enumerate(sums) if ahead]
    grad_gate, grad_up = weight_part(gate_grad, up_grad, inputs_all, grad_gate, grad_up, cut, unit // 2)
    grad_down = down(1, grad_down, grad_up)
    grad_inputs = sum_rows([after(sums[0], grad_down)] + sums[1:])
    return grad_inputs, grad_gate, grad_up, grad_down


def on_any(inputs, grad_out, gate_pre, up_pre, w_gate, w_up, w_down):
    inputs_all = lax.all_gather(inputs, "row", axis=0, tiled=True)
    grad_out_all = lax.all_gather(grad_out, "row", axis=0, tiled=True)
    gate_all = lax.all_gather(gate_pre, "col", axis=0, tiled=True)
    up_all = lax.all_gather(up_pre, "col", axis=0, tiled=True)
    hidden_grad = lax.psum_scatter(dot(grad_out_all, w_down, 1, 1), "col", scatter_dimension=0, tiled=True)
    gate_grad, up_grad = swiglu_back(gate_pre, up_pre, hidden_grad)
    gate_grad = lax.all_gather(gate_grad, "col", axis=0, tiled=True)
    up_grad = lax.all_gather(up_grad, "col", axis=0, tiled=True)
    grad_down = dot(hidden_of(gate_all, up_all), grad_out_all, 0, 0).astype(BF16)
    grad_gate = dot(inputs_all, gate_grad, 0, 0).astype(BF16)
    grad_up = dot(inputs_all, up_grad, 0, 0).astype(BF16)
    total = dot(gate_grad, w_gate, 1, 1) + dot(up_grad, w_up, 1, 1)
    grad_inputs = lax.psum_scatter(total, "row", scatter_dimension=0, tiled=True).astype(BF16)
    return grad_inputs, grad_gate, grad_up, grad_down


def solution(mesh):
    rows, cols = mesh.shape["row"], mesh.shape["col"]
    plan = functools.partial(on_square, rows) if (rows, cols) == (4, 8) else on_any
    placed = (
        P("row", "col"),
        P("row", "col"),
        P("col", "row"),
        P("col", "row"),
        P("col", "row"),
        P("col", "row"),
        P("row", "col"),
    )
    return jax.shard_map(
        plan,
        mesh=mesh,
        in_specs=placed,
        out_specs=(P("row", "col"), P("col", "row"), P("col", "row"), P("row", "col")),
        check_vma=False,
    )
```

time: 401 us -> 255 us (0.64)
  waiting for transfers between devices: 256 us -> 80.2 us
  Pallas kernels: 0 us -> 114 us
  matrix products: 83.8 us -> 0 us
  starting transfers between devices: 0.45 us -> 32.3 us
  local copies, waits for them, and re-layouts: 39.8 us -> 13.9 us
  other arithmetic: 5.66 us -> 0.7 us
    all_gather x5 -> x3, waiting for transfers between devices: 135 us -> 9.19 us  [the longest x1 9.17 us: on_square(): hidden1_all = lax.all_gather(hidden1, 'col', axis=0, tiled=True)]
    reduce_scatter x2 -> x0, waiting for transfers between devices: 119 us -> none  [the longest x1 103 us: on_device(): lax.psum_scatter(lax.dot_general(grad_out_all, w_down, last_last, preferr...]
    pallas_call x0 -> x14, Pallas kernels: none -> 114 us  [the longest x1 22.6 us: first_part(): pl.pallas_call(kernel, grid=(size // tile,), in_specs=[pl.BlockSpec(memor...]
    dot_general x6 -> x0, matrix products: 83.8 us -> none  [the longest x1 14.4 us: on_device(): lax.dot_general(grad_out_all, w_down, last_last, preferred_element_type=j...]
    ppermute x0 -> x24, waiting for transfers between devices: none -> 71 us  [the longest x18 60.4 us: swap(): return lax.ppermute(array, 'col', [(i, i ^ bit) for i in range(8)])]
    ppermute x0 -> x24, starting transfers between devices: none -> 32.2 us  [the longest x18 19.3 us: swap(): return lax.ppermute(array, 'col', [(i, i ^ bit) for i in range(8)])]
    unnamed x10 -> x38, local copies, waits for them, and re-layouts: 39.8 us -> 8.38 us
    convert_element_type x2 -> x0, other arithmetic: 5.66 us -> none  [the longest x1 3.88 us: swiglu_back(): up_grad = (hidden_grad * swished).astype(jnp.bfloat16)]
  transfers between devices with their start and end apart: 7 -> 27, of which waited for: 6 -> 8; matrix products, arithmetic and copies ran while one was open for 27% -> 2% of each run, Pallas kernels for 0% -> 36%
where the time goes in v1:
time: 255 us
  Pallas kernels  114 us (45%)
  waiting for transfers between devices  80.2 us (31%)
  starting transfers between devices  32.3 us (13%)
  between operations  14 us (5%)
  local copies, waits for them, and re-layouts  13.9 us (5%)
    ppermute x18, waiting for transfers between devices, swap(): return lax.ppermute(array, 'col', [(i, i ^ bit) for i in range(8)])  60.4 us
    pallas_call x1, Pallas kernels, first_part(): pl.pallas_call(kernel, grid=(size // tile,), in_specs=[pl.BlockSpec(memor...  22.6 us
    pallas_call x2, Pallas kernels, grad_down_part(): pl.pallas_call(kernel, grid=(size // tile,), in_specs=[block] * 2 + [whol...  19.8 us
    pallas_call x1, Pallas kernels, input_part(): pl.pallas_call(kernel, grid=(steps,), in_specs=[pl.BlockSpec(memory_space...  19.6 us
    ppermute x18, starting transfers between devices, swap(): return lax.ppermute(array, 'col', [(i, i ^ bit) for i in range(8)])  19.3 us
    pallas_call x2, Pallas kernels, partial_hidden_grad(): pl.pallas_call(kernel, grid=(size // tile,), in_specs=[whole_block((token...  18.4 us
    pallas_call x1, Pallas kernels, weight_part(): pl.pallas_call(kernel, grid=(size // tile,), in_specs=[block, block, whol...  14 us
    ppermute x6, starting transfers between devices, onward(): lax.ppermute(array, 'row', [(i, (i + step) % rows) for i in range(rows)])  12.9 us
  transfers between devices with their start and end apart: 27, of which 8 were waited for; matrix products, arithmetic and copies ran while one was open for 2% of the time, Pallas kernels for 36%

profile of v1, /device:TPU:0, one launch (start us, length us, event | category | flops | bytes accessed | tf_op | source)
XLA Modules:
  0.0 254.7 jit_solution(1043809689999951894)
XLA Ops:
  7.7 3.7 %collective-permute-start.1 = (bf16[128,1024]{1,0:T(8,128)(2,1)}, bf16[128,1024]{1,0:T(8,128)(2,1)}, u32[]{:S(2)}, u32[]{:S(2)}) collective-permute-start(bf16[128,1024]{1,0:T(8,128)(2,1)} %refs_0_.1), channel_id=1, source_target_pairs={{0,16},{8,24},{16,0},{24,8},{1,17},{9,25},{17,1},{25,9},{2,18},{10... | collective-permute-start | bytes 786440 | tf_op jit(solution)/shard_map/ppermute | solution.py:54
  11.4 1.6 collective-permute-start
  13.0 2.2 collective-permute-start.2
  15.2 1.0 slice.32
  16.2 1.0 slice.33
  17.4 1.6 collective-permute-start.6
  19.5 10.6 %collective-permute-done.1.refs_2_ = bf16[128,1024]{1,0:T(8,128)(2,1)} collective-permute-done((bf16[128,1024]{1,0:T(8,128)(2,1)}, bf16[128,1024]{1,0:T(8,128)(2,1)}, u32[]{:S(2)}, u32[]{:S(2)}) %collective-permute-start.1) | collective-permute-done | bytes 262176 | tf_op jit(solution)/shard_map/ppermute | solution.py:54
  30.2 1.8 collective-permute-start.5
  31.9 2.3 arrange.1.x
  34.3 2.2 fusion
  36.8 1.6 collective-permute-start.11
  38.4 1.1 collective-permute-start.10
  39.5 11.1 %collective-permute-done.5.refs_1_ = bf16[128,3072]{1,0:T(8,128)(2,1)S(1)} collective-permute-done((bf16[128,3072]{1,0:T(8,128)(2,1)S(1)}, bf16[128,3072]{1,0:T(8,128)(2,1)S(1)}, u32[]{:S(2)}, u32[]{:S(2)}) %collective-permute-start.5) | collective-permute-done | bytes 786464 | tf_op jit(solution)/shard_map/ppermute | solution.py:50
  50.6 1.8 collective-permute-start.8
  52.4 1.6 collective-permute-start.7
  54.0 8.5 %partial_hidden_grad.2 = (f32[64,3072]{1,0:T(8,128)}, bf16[64,3072]{1,0:T(8,128)(2,1)}, bf16[64,3072]{1,0:T(8,128)(2,1)}, bf16[64,3072]{1,0:T(8,128)(2,1)}) custom-call(bf16[256,1024]{1,0:T(8,128)(2,1)} %get-tuple-element.46.x, bf16[256,1024]{1,0:T(8,128)(2,1)} %copy-done.6, bf16[7168,1024]{1,0:T(8,128)(2,1)} %w.3, bf16[7168,1024]{1,0:T(8,128)(2,1)} %collective-permute-done.4.v), custom_call_target="tpu_custom_call" | custom-call | tf_op jit(solution)/shard_map/partial_hidden_grad/pallas_call | solution.py:139
  63.2 18.3 %collective-permute-done.8.refs_4_ = bf16[64,3072]{1,0:T(8,128)(2,1)S(1)} collective-permute-done((bf16[64,3072]{1,0:T(8,128)(2,1)S(1)}, bf16[64,3072]{1,0:T(8,128)(2,1)S(1)}, u32[]{:S(2)}, u32[]{:S(2)}) %collective-permute-start.8) | collective-permute-done | bytes 393248 | tf_op jit(solution)/shard_map/ppermute | solution.py:50
  81.5 1.8 collective-permute-start.13
  83.3 1.4 collective-permute-start.14
  84.8 9.9 %partial_hidden_grad.3 = (f32[64,4096]{1,0:T(8,128)}, bf16[64,4096]{1,0:T(8,128)(2,1)}, bf16[64,4096]{1,0:T(8,128)(2,1)}, bf16[64,4096]{1,0:T(8,128)(2,1)}) custom-call(bf16[256,1024]{1,0:T(8,128)(2,1)} %get-tuple-element.46.x, bf16[256,1024]{1,0:T(8,128)(2,1)} %copy-done.6, bf16[7168,1024]{1,0:T(8,128)(2,1)} %w.3, bf16[7168,1024]{1,0:T(8,128)(2,1)} %collective-permute-done.4.v), custom_call_target="tpu_custom_call" | custom-call | tf_op jit(solution)/shard_map/partial_hidden_grad/pallas_call | solution.py:139
  94.7 3.2 %pack.2.p0 = bf16[512,3072]{1,0:T(8,128)(2,1)} custom-call(bf16[128,3072]{1,0:T(8,128)(2,1)} %copy-done.2, bf16[128,3072]{1,0:T(8,128)(2,1)} %copy-done.8, bf16[128,3072]{1,0:T(8,128)(2,1)} %copy-done.7, bf16[64,3072]{1,0:T(8,128)(2,1)} %copy-done.14, bf16[64,3072]{1,0:T(8,128)(2,1)} %copy-done.12), custom_call_target="tpu_custom_call" | custom-call | tf_op jit(solution)/shard_map/pack/pallas_call | solution.py:330
  97.9 1.0 copy-done.3
  98.8 1.0 copy-done.4
  101.4 2.4 total_hidden_grad.2
  104.3 1.8 collective-permute-start.16
  106.1 1.4 collective-permute-start.17
  107.5 2.3 reorder.1.x
  109.9 1.7 copy-done
  111.6 9.1 %grad_down_part.2.rest_0_ = bf16[7168,1024]{1,0:T(8,128)(2,1)} custom-call(bf16[512,3072]{1,0:T(8,128)(2,1)} %pack.2.p0, bf16[512,3072]{1,0:T(8,128)(2,1)} %copy-done, bf16[512,1024]{1,0:T(8,128)(2,1)} %arrange.1.x), custom_call_target="tpu_custom_call" | custom-call | tf_op jit(solution)/shard_map/grad_down_part/pallas_call | solution.py:184
  120.6 2.7 %collective-permute-done.15.b = bf16[64,4096]{1,0:T(8,128)(2,1)} collective-permute-done((bf16[64,4096]{1,0:T(8,128)(2,1)}, bf16[64,4096]{1,0:T(8,128)(2,1)}, u32[]{:S(2)}, u32[]{:S(2)}) %collective-permute-start.15) | collective-permute-done | bytes 524320 | tf_op jit(solution)/shard_map/ppermute | solution.py:50
  123.3 10.1 %collective-permute-done.16.c = bf16[64,4096]{1,0:T(8,128)(2,1)} collective-permute-done((bf16[64,4096]{1,0:T(8,128)(2,1)}, bf16[64,4096]{1,0:T(8,128)(2,1)}, u32[]{:S(2)}, u32[]{:S(2)}) %collective-permute-start.16) | collective-permute-done | bytes 524320 | tf_op jit(solution)/shard_map/ppermute | solution.py:50
  133.4 1.6 collective-permute-done.17.d
  135.0 3.2 %total_hidden_grad.3 = bf16[64,4096]{1,0:T(8,128)(2,1)} custom-call(f32[64,4096]{1,0:T(8,128)} %get-tuple-element.61.a, bf16[64,4096]{1,0:T(8,128)(2,1)} %collective-permute-done.15.b, bf16[64,4096]{1,0:T(8,128)(2,1)} %collective-permute-done.16.c, bf16[64,4096]{1,0:T(8,128)(2,1)} %collective-permute-done.17.d), custom_call_target="tpu_custom_call" | custom-call | tf_op jit(solution)/shard_map/total_hidden_grad/pallas_call | solution.py:154
  138.3 1.1 slice.39
  139.8 1.6 collective-permute-start.18
  141.4 16.5 %collective-permute-done.19.refs_4_ = bf16[64,4096]{1,0:T(8,128)(2,1)S(1)} collective-permute-done((bf16[64,4096]{1,0:T(8,128)(2,1)S(1)}, bf16[64,4096]{1,0:T(8,128)(2,1)S(1)}, u32[]{:S(2)}, u32[]{:S(2)}) %collective-permute-start.19) | collective-permute-done | bytes 524320 | tf_op jit(solution)/shard_map/ppermute | solution.py:50
  157.8 0.8 copy-done.9
  158.6 0.8 copy-done.10
  159.4 3.7 %pack.3.p0 = bf16[512,4096]{1,0:T(8,128)(2,1)} custom-call(bf16[128,4096]{1,0:T(8,128)(2,1)} %copy-done.1, bf16[128,4096]{1,0:T(8,128)(2,1)} %copy-done.4, bf16[128,4096]{1,0:T(8,128)(2,1)} %copy-done.3, bf16[64,4096]{1,0:T(8,128)(2,1)} %copy-done.10, bf16[64,4096]{1,0:T(8,128)(2,1)} %copy-done.9), custom_call_target="tpu_custom_call" | custom-call | tf_op jit(solution)/shard_map/pack/pallas_call | solution.py:330
  163.1 22.6 %first_part.1 = (bf16[1024,7168]{1,0:T(8,128)(2,1)}, bf16[1024,7168]{1,0:T(8,128)(2,1)}, f32[512,1024]{1,0:T(8,128)}) custom-call(s32[2]{0:T(128)} %pad_add_fusion.where_ref, bf16[512,3072]{1,0:T(8,128)(2,1)} %all-gather.8.cloned.1.call-done.h, bf16[512,3072]{1,0:T(8,128)(2,1)} %pack.2.p0, bf16[512,3072]{1,0:T(8,128)(2,1)} %copy-done, ...), custom_call_target="tpu_custom_call" | custom-call | tf_op jit(solution)/shard_map/first_part/pallas_call | solution.py:229
  185.7 9.2 %all-gather.6.cloned.1.call-done.h = bf16[512,4096]{1,0:T(8,128)(2,1)} async-done(((bf16[64,4096]{1,0:T(8,128)(2,1)}), bf16[512,4096]{1,0:T(8,128)(2,1)}) %all-gather.6.cloned.1.call-update) | async-done | bytes 4194320 | tf_op jit(solution)/shard_map/all_gather | solution.py:397
  194.9 19.6 %input_part.1 = (bf16[512,4096]{1,0:T(8,128)(2,1)}, bf16[512,4096]{1,0:T(8,128)(2,1)}, f32[128,1024]{1,0:T(8,128)}, bf16[128,1024]{1,0:T(8,128)(2,1)}, bf16[128,...) custom-call(s32[2]{0:T(128)} %pad_add_fusion.where_ref, bf16[512,4096]{1,0:T(8,128)(2,1)} %all-gather.6.cloned.1.call-done.h, ...), custom_call_target="tpu_custom_call" | custom-call | tf_op jit(solution)/shard_map/input_part/pallas_call | solution.py:279
  214.5 1.5 collective-permute-start.21
  216.0 2.4 collective-permute-start.22
  218.4 1.4 collective-permute-start.23
  219.9 14.0 %weight_part.1 = (bf16[1024,7168]{1,0:T(8,128)(2,1)}, bf16[1024,7168]{1,0:T(8,128)(2,1)}) custom-call(bf16[512,4096]{1,0:T(8,128)(2,1)} %get-tuple-element.73.a, bf16[512,4096]{1,0:T(8,128)(2,1)} %get-tuple-element.74.b, bf16[512,1024]{1,0:T(8,128)(2,1)} %reorder.1.x, ...), custom_call_target="tpu_custom_call", output_to_operand_aliasing={{0}: (3, {}), {1}: (4, {})} | custom-call | tf_op jit(solution)/shard_map/weight_part/pallas_call | solution.py:306
  233.9 10.7 %grad_down_part.3 = bf16[7168,1024]{1,0:T(8,128)(2,1)} custom-call(bf16[512,4096]{1,0:T(8,128)(2,1)} %pack.3.p0, bf16[512,4096]{1,0:T(8,128)(2,1)} %collective-permute-done.20.p1, bf16[512,1024]{1,0:T(8,128)(2,1)} %arrange.1.x, bf16[7168,1024]{1,0:T(8,128)(2,1)} %grad_down_part.2.rest_0_), custom_call_target="tpu_custom_call", output_to_operand_aliasing={{}: (3, {})} | custom-call | tf_op jit(solution)/shard_map/grad_down_part/pallas_call | solution.py:184
  246.1 2.1 sum_rows.1
  (75 shorter events, 6.1 us)
Async XLA Ops:
  7.2 100.4 %all-gather.4.cloned.1.call-start = ((), (), s32[]{:S(2)}) async-start(), calls=%async_computation | async-start | bytes 1310720 | tf_op jit(solution)/shard_map/all_gather | solution.py:382
  7.2 46.8 %collective-permute-start.4 = (bf16[7168,1024]{1,0:T(8,128)(2,1)}, bf16[7168,1024]{1,0:T(8,128)(2,1)}, u32[]{:S(2)}, u32[]{:S(2)}) collective-permute-start(bf16[7168,1024]{1,0:T(8,128)(2,1)} %w.3), channel_id=1, source_target_pairs={{0,1},{1,0},{2,3},{3,2},{4,5},{5,4},{6,7},{7,6},{8,9},{9,8},{10,11... | collective-permute-start | bytes 44040200 | tf_op jit(solution)/shard_map/ppermute | solution.py:50
  7.7 22.4 %collective-permute-start.1 = (bf16[128,1024]{1,0:T(8,128)(2,1)}, bf16[128,1024]{1,0:T(8,128)(2,1)}, u32[]{:S(2)}, u32[]{:S(2)}) collective-permute-start(bf16[128,1024]{1,0:T(8,128)(2,1)} %refs_0_.1), channel_id=1, source_target_pairs={{0,16},{8,24},{16,0},{24,8},{1,17},{9,25},{17,1},{25,9},{2,18},{10... | collective-permute-start | bytes 786440 | tf_op jit(solution)/shard_map/ppermute | solution.py:54
  11.4 20.5 %collective-permute-start = (bf16[128,1024]{1,0:T(8,128)(2,1)}, bf16[128,1024]{1,0:T(8,128)(2,1)}, u32[]{:S(2)}, u32[]{:S(2)}) collective-permute-start(bf16[128,1024]{1,0:T(8,128)(2,1)} %refs_0_.1), channel_id=1, source_target_pairs={{0,8},{8,16},{16,24},{24,0},{1,9},{9,17},{17,25},{25,1},{2,10},{10... | collective-permute-start | bytes 786440 | tf_op jit(solution)/shard_map/ppermute | solution.py:54
  13.0 18.9 %collective-permute-start.2 = (bf16[128,1024]{1,0:T(8,128)(2,1)}, bf16[128,1024]{1,0:T(8,128)(2,1)}, u32[]{:S(2)}, u32[]{:S(2)}) collective-permute-start(bf16[128,1024]{1,0:T(8,128)(2,1)} %refs_0_.1), channel_id=1, source_target_pairs={{0,24},{8,0},{16,8},{24,16},{1,25},{9,1},{17,9},{25,17},{2,26},{10... | collective-permute-start | bytes 786440 | tf_op jit(solution)/shard_map/ppermute | solution.py:54
  17.3 19.4 %slice-start = ((bf16[64,7168]{1,0:T(8,128)(2,1)}), bf16[64,4096]{1,0:T(8,128)(2,1)S(1)}, s32[]{:S(2)}) async-start(bf16[64,7168]{1,0:T(8,128)(2,1)} %param.9), calls=%async_computation.3 | async-start | bytes 1048576 | tf_op jit(solution)/shard_map/slice | solution.py:357
  17.3 19.4 %slice-start.1 = ((bf16[64,7168]{1,0:T(8,128)(2,1)}), bf16[64,4096]{1,0:T(8,128)(2,1)S(1)}, s32[]{:S(2)}) async-start(bf16[64,7168]{1,0:T(8,128)(2,1)} %param.10), calls=%async_computation.4 | async-start | bytes 1048576 | tf_op jit(solution)/shard_map/slice | solution.py:357
  17.4 19.4 %copy-start.2 = (bf16[128,3072]{1,0:T(8,128)(2,1)}, bf16[128,3072]{1,0:T(8,128)(2,1)S(1)}, u32[]{:S(2)}) copy-start(bf16[128,3072]{1,0:T(8,128)(2,1)S(1)} %pad_maximum_fusion.1.refs_0_) | copy-start | bytes 2359300
  17.4 21.0 %collective-permute-start.6 = (bf16[128,3072]{1,0:T(8,128)(2,1)S(1)}, bf16[128,3072]{1,0:T(8,128)(2,1)S(1)}, u32[]{:S(2)}, u32[]{:S(2)}) collective-permute-start(bf16[128,3072]{1,0:T(8,128)(2,1)S(1)} %pad_maximum_fusion.1.refs_0_), channel_id=1, source_target_pairs={{0,4},{1,5},{2,6},{3,7},{4,0},{5,1},{6,2},{7,3},{8,12},{9,13},{10,... | collective-permute-start | bytes 2359304 | tf_op jit(solution)/shard_map/ppermute | solution.py:50
  30.2 20.5 %collective-permute-start.5 = (bf16[128,3072]{1,0:T(8,128)(2,1)S(1)}, bf16[128,3072]{1,0:T(8,128)(2,1)S(1)}, u32[]{:S(2)}, u32[]{:S(2)}) collective-permute-start(bf16[128,3072]{1,0:T(8,128)(2,1)S(1)} %pad_maximum_fusion.1.refs_0_), channel_id=1, source_target_pairs={{0,2},{1,3},{2,0},{3,1},{4,6},{5,7},{6,4},{7,5},{8,10},{9,11},{10,... | collective-permute-start | bytes 2359304 | tf_op jit(solution)/shard_map/ppermute | solution.py:50
  36.5 126.6 %all-gather.8.cloned.1.call-start = ((), (), s32[]{:S(2)}) async-start(), calls=%async_computation.2 | async-start | bytes 3538944 | tf_op jit(solution)/shard_map/all_gather | solution.py:392
  36.6 15.8 %collective-permute-start.3 = (bf16[256,1024]{1,0:T(8,128)(2,1)}, bf16[256,1024]{1,0:T(8,128)(2,1)S(1)}, u32[]{:S(2)}, u32[]{:S(2)}) collective-permute-start(bf16[256,1024]{1,0:T(8,128)(2,1)} %get-tuple-element.84), channel_id=1, source_target_pairs={{0,1},{1,0},{2,3},{3,2},{4,5},{5,4},{6,7},{7,6},{8,9},{9,8},{10,11... | collective-permute-start | bytes 1572872 | tf_op jit(solution)/shard_map/ppermute | solution.py:50
  36.8 25.8 %copy-start.1 = (bf16[128,4096]{1,0:T(8,128)(2,1)}, bf16[128,4096]{1,0:T(8,128)(2,1)S(1)}, u32[]{:S(2)}) copy-start(bf16[128,4096]{1,0:T(8,128)(2,1)S(1)} %pad_maximum_fusion.refs_0_) | copy-start | bytes 3145732
  36.8 61.1 %collective-permute-start.11 = (bf16[128,4096]{1,0:T(8,128)(2,1)S(1)}, bf16[128,4096]{1,0:T(8,128)(2,1)S(1)}, u32[]{:S(2)}, u32[]{:S(2)}) collective-permute-start(bf16[128,4096]{1,0:T(8,128)(2,1)S(1)} %pad_maximum_fusion.refs_0_), channel_id=1, source_target_pairs={{0,4},{1,5},{2,6},{3,7},{4,0},{5,1},{6,2},{7,3},{8,12},{9,13},{10,... | collective-permute-start | bytes 3145736 | tf_op jit(solution)/shard_map/ppermute | solution.py:50
  38.4 24.2 %copy-start.7 = (bf16[128,3072]{1,0:T(8,128)(2,1)}, bf16[128,3072]{1,0:T(8,128)(2,1)S(1)}, u32[]{:S(2)}) copy-start(bf16[128,3072]{1,0:T(8,128)(2,1)S(1)} %collective-permute-done.6.refs_2_) | copy-start | bytes 2359300
  38.4 59.5 %collective-permute-start.10 = (bf16[128,4096]{1,0:T(8,128)(2,1)S(1)}, bf16[128,4096]{1,0:T(8,128)(2,1)S(1)}, u32[]{:S(2)}, u32[]{:S(2)}) collective-permute-start(bf16[128,4096]{1,0:T(8,128)(2,1)S(1)} %pad_maximum_fusion.refs_0_), channel_id=1, source_target_pairs={{0,2},{1,3},{2,0},{3,1},{4,6},{5,7},{6,4},{7,5},{8,10},{9,11},{10,... | collective-permute-start | bytes 3145736 | tf_op jit(solution)/shard_map/ppermute | solution.py:50
  50.6 12.0 %copy-start.8 = (bf16[128,3072]{1,0:T(8,128)(2,1)}, bf16[128,3072]{1,0:T(8,128)(2,1)S(1)}, u32[]{:S(2)}) copy-start(bf16[128,3072]{1,0:T(8,128)(2,1)S(1)} %collective-permute-done.5.refs_1_) | copy-start | bytes 2359300
  50.6 30.9 %collective-permute-start.8 = (bf16[64,3072]{1,0:T(8,128)(2,1)S(1)}, bf16[64,3072]{1,0:T(8,128)(2,1)S(1)}, u32[]{:S(2)}, u32[]{:S(2)}) collective-permute-start(bf16[64,3072]{1,0:T(8,128)(2,1)S(1)} %slice.43), channel_id=1, source_target_pairs={{0,2},{1,3},{2,0},{3,1},{4,6},{5,7},{6,4},{7,5},{8,10},{9,11},{10,... | collective-permute-start | bytes 1179656 | tf_op jit(solution)/shard_map/ppermute | solution.py:50
  52.4 1.6 copy-start.6
  52.4 30.9 %collective-permute-start.7 = (bf16[64,3072]{1,0:T(8,128)(2,1)S(1)}, bf16[64,3072]{1,0:T(8,128)(2,1)S(1)}, u32[]{:S(2)}, u32[]{:S(2)}) collective-permute-start(bf16[64,3072]{1,0:T(8,128)(2,1)S(1)} %slice.42), channel_id=1, source_target_pairs={{0,4},{1,5},{2,6},{3,7},{4,0},{5,1},{6,2},{7,3},{8,12},{9,13},{10,... | collective-permute-start | bytes 1179656 | tf_op jit(solution)/shard_map/ppermute | solution.py:50
  62.6 36.2 %collective-permute-start.12 = (bf16[64,3072]{1,0:T(8,128)(2,1)}, bf16[64,3072]{1,0:T(8,128)(2,1)S(1)}, u32[]{:S(2)}, u32[]{:S(2)}) collective-permute-start(bf16[64,3072]{1,0:T(8,128)(2,1)} %get-tuple-element.56), channel_id=1, source_target_pairs={{0,2},{1,3},{2,0},{3,1},{4,6},{5,7},{6,4},{7,5},{8,10},{9,11},{10,... | collective-permute-start | bytes 1179656 | tf_op jit(solution)/shard_map/ppermute | solution.py:50
  81.5 13.1 %copy-start.12 = (bf16[64,3072]{1,0:T(8,128)(2,1)}, bf16[64,3072]{1,0:T(8,128)(2,1)S(1)}, u32[]{:S(2)}) copy-start(bf16[64,3072]{1,0:T(8,128)(2,1)S(1)} %collective-permute-done.8.refs_4_) | copy-start | bytes 1179652
  81.5 18.3 %collective-permute-start.13 = (bf16[64,3072]{1,0:T(8,128)(2,1)}, bf16[64,3072]{1,0:T(8,128)(2,1)S(1)}, u32[]{:S(2)}, u32[]{:S(2)}) collective-permute-start(bf16[64,3072]{1,0:T(8,128)(2,1)} %get-tuple-element.57), channel_id=1, source_target_pairs={{0,4},{1,5},{2,6},{3,7},{4,0},{5,1},{6,2},{7,3},{8,12},{9,13},{10,... | collective-permute-start | bytes 1179656 | tf_op jit(solution)/shard_map/ppermute | solution.py:50
  83.3 11.3 %copy-start.14 = (bf16[64,3072]{1,0:T(8,128)(2,1)}, bf16[64,3072]{1,0:T(8,128)(2,1)S(1)}, u32[]{:S(2)}) copy-start(bf16[64,3072]{1,0:T(8,128)(2,1)S(1)} %collective-permute-done.7.refs_3_) | copy-start | bytes 1179652
  83.3 16.5 %collective-permute-start.14 = (bf16[64,3072]{1,0:T(8,128)(2,1)}, bf16[64,3072]{1,0:T(8,128)(2,1)S(1)}, u32[]{:S(2)}, u32[]{:S(2)}) collective-permute-start(bf16[64,3072]{1,0:T(8,128)(2,1)} %get-tuple-element.58), channel_id=1, source_target_pairs={{0,6},{1,7},{2,4},{3,5},{4,2},{5,3},{6,0},{7,1},{8,14},{9,15},{10,... | collective-permute-start | bytes 1179656 | tf_op jit(solution)/shard_map/ppermute | solution.py:50
  97.8 1.0 copy-start.3
  98.8 1.0 copy-start.4
  99.8 0.7 copy-start.11
  99.8 0.9 copy-start.13
  100.7 0.8 copy-start.15
  103.8 91.0 %all-gather.6.cloned.1.call-start = ((), (), s32[]{:S(2)}) async-start(), calls=%async_computation.1 | async-start | bytes 4718592 | tf_op jit(solution)/shard_map/all_gather | solution.py:397
  103.9 6.0 %collective-permute-start.9 = (bf16[512,3072]{1,0:T(8,128)(2,1)}, bf16[512,3072]{1,0:T(8,128)(2,1)S(1)}, u32[]{:S(2)}, u32[]{:S(2)}) collective-permute-start(bf16[512,3072]{1,0:T(8,128)(2,1)} %pack.2.p0), channel_id=1, source_target_pairs={{0,1},{1,0},{2,3},{3,2},{4,5},{5,4},{6,7},{7,6},{8,9},{9,8},{10,11... | collective-permute-start | bytes 9437192 | tf_op jit(solution)/shard_map/ppermute | solution.py:50
  104.0 19.3 %collective-permute-start.15 = (bf16[64,4096]{1,0:T(8,128)(2,1)}, bf16[64,4096]{1,0:T(8,128)(2,1)}, u32[]{:S(2)}, u32[]{:S(2)}) collective-permute-start(bf16[64,4096]{1,0:T(8,128)(2,1)} %get-tuple-element.62), channel_id=1, source_target_pairs={{0,2},{1,3},{2,0},{3,1},{4,6},{5,7},{6,4},{7,5},{8,10},{9,11},{10,... | collective-permute-start | bytes 1572872 | tf_op jit(solution)/shard_map/ppermute | solution.py:50
  104.3 29.1 %collective-permute-start.16 = (bf16[64,4096]{1,0:T(8,128)(2,1)}, bf16[64,4096]{1,0:T(8,128)(2,1)}, u32[]{:S(2)}, u32[]{:S(2)}) collective-permute-start(bf16[64,4096]{1,0:T(8,128)(2,1)} %get-tuple-element.63), channel_id=1, source_target_pairs={{0,4},{1,5},{2,6},{3,7},{4,0},{5,1},{6,2},{7,3},{8,12},{9,13},{10,... | collective-permute-start | bytes 1572872 | tf_op jit(solution)/shard_map/ppermute | solution.py:50
  106.1 28.9 %collective-permute-start.17 = (bf16[64,4096]{1,0:T(8,128)(2,1)}, bf16[64,4096]{1,0:T(8,128)(2,1)}, u32[]{:S(2)}, u32[]{:S(2)}) collective-permute-start(bf16[64,4096]{1,0:T(8,128)(2,1)} %get-tuple-element.64), channel_id=1, source_target_pairs={{0,6},{1,7},{2,4},{3,5},{4,2},{5,3},{6,0},{7,1},{8,14},{9,15},{10,... | collective-permute-start | bytes 1572872 | tf_op jit(solution)/shard_map/ppermute | solution.py:50
  109.9 1.7 copy-start
  120.6 19.1 %copy-start.5 = (bf16[128,4096]{1,0:T(8,128)(2,1)S(1)}, bf16[128,4096]{1,0:T(8,128)(2,1)}, u32[]{:S(2)}) copy-start(bf16[128,4096]{1,0:T(8,128)(2,1)} %copy-done.4) | copy-start | bytes 3145732
  139.4 18.4 %collective-permute-start.19 = (bf16[64,4096]{1,0:T(8,128)(2,1)S(1)}, bf16[64,4096]{1,0:T(8,128)(2,1)S(1)}, u32[]{:S(2)}, u32[]{:S(2)}) collective-permute-start(bf16[64,4096]{1,0:T(8,128)(2,1)S(1)} %slice.39), channel_id=1, source_target_pairs={{0,2},{1,3},{2,0},{3,1},{4,6},{5,7},{6,4},{7,5},{8,10},{9,11},{10,... | collective-permute-start | bytes 1572872 | tf_op jit(solution)/shard_map/ppermute | solution.py:50
  139.8 18.1 %collective-permute-start.18 = (bf16[64,4096]{1,0:T(8,128)(2,1)S(1)}, bf16[64,4096]{1,0:T(8,128)(2,1)S(1)}, u32[]{:S(2)}, u32[]{:S(2)}) collective-permute-start(bf16[64,4096]{1,0:T(8,128)(2,1)S(1)} %slice.38), channel_id=1, source_target_pairs={{0,4},{1,5},{2,6},{3,7},{4,0},{5,1},{6,2},{7,3},{8,12},{9,13},{10,... | collective-permute-start | bytes 1572872 | tf_op jit(solution)/shard_map/ppermute | solution.py:50
  157.8 0.8 copy-start.9
  158.6 0.8 copy-start.10
  163.1 22.6 %collective-permute-start.20 = (bf16[512,4096]{1,0:T(8,128)(2,1)}, bf16[512,4096]{1,0:T(8,128)(2,1)}, u32[]{:S(2)}, u32[]{:S(2)}) collective-permute-start(bf16[512,4096]{1,0:T(8,128)(2,1)} %pack.3.p0), channel_id=1, source_target_pairs={{0,1},{1,0},{2,3},{3,2},{4,5},{5,4},{6,7},{7,6},{8,9},{9,8},{10,11... | collective-permute-start | bytes 12582920 | tf_op jit(solution)/shard_map/ppermute | solution.py:50
  214.5 30.1 %collective-permute-start.21 = (bf16[128,1024]{1,0:T(8,128)(2,1)}, bf16[128,1024]{1,0:T(8,128)(2,1)S(1)}, u32[]{:S(2)}, u32[]{:S(2)}) collective-permute-start(bf16[128,1024]{1,0:T(8,128)(2,1)} %get-tuple-element.80), channel_id=1, source_target_pairs={{0,8},{8,16},{16,24},{24,0},{1,9},{9,17},{17,25},{25,1},{2,10},{10... | collective-permute-start | bytes 786440 | tf_op jit(solution)/shard_map/ppermute | solution.py:54
  216.0 28.5 %collective-permute-start.22 = (bf16[128,1024]{1,0:T(8,128)(2,1)}, bf16[128,1024]{1,0:T(8,128)(2,1)S(1)}, u32[]{:S(2)}, u32[]{:S(2)}) collective-permute-start(bf16[128,1024]{1,0:T(8,128)(2,1)} %get-tuple-element.81), channel_id=1, source_target_pairs={{0,16},{8,24},{16,0},{24,8},{1,17},{9,25},{17,1},{25,9},{2,18},{10... | collective-permute-start | bytes 786440 | tf_op jit(solution)/shard_map/ppermute | solution.py:54
  218.4 26.2 %collective-permute-start.23 = (bf16[128,1024]{1,0:T(8,128)(2,1)}, bf16[128,1024]{1,0:T(8,128)(2,1)S(1)}, u32[]{:S(2)}, u32[]{:S(2)}) collective-permute-start(bf16[128,1024]{1,0:T(8,128)(2,1)} %get-tuple-element.82), channel_id=1, source_target_pairs={{0,24},{8,0},{16,8},{24,16},{1,25},{9,1},{17,9},{25,17},{2,26},{10... | collective-permute-start | bytes 786440 | tf_op jit(solution)/shard_map/ppermute | solution.py:54
  244.6 0.7 copy-start.16
  244.6 0.8 copy-start.17
  245.4 0.7 copy-start.18
Sparse Core Ops, SparseCore 0:
  36.6 31.7 all-gather.3
  104.0 49.1 all-gather.7
  155.1 39.7 all-gather.5

commit v2 on v1

--- a/solution.py
+++ b/solution.py
@@ -63,44 +63,26 @@
     return (offset >> 1) + 4 * (offset & 1)
 
 
-def arrange(where, blocks):
-    rows, (count, features) = len(blocks), blocks[0].shape
-    tokens = rows * count
-    part = tokens // 8
-
-    def kernel(where_ref, *refs):
-        *ins, out = refs
-        row, col = where_ref[0], where_ref[1]
-        for step, ref in enumerate(ins):
-            owner = lax.rem(row + (rows - step), rows)
-            for at in range(8 // rows):
-                start = pl.multiple_of(place_of(owner * (8 // rows) + at, col) * part, part)
-                out[pl.ds(start, part), :] = ref[at * part : (at + 1) * part, :]
-
-    return pl.pallas_call(
-        kernel,
-        out_shape=jax.ShapeDtypeStruct((tokens, features), BF16),
-        in_specs=[pl.BlockSpec(memory_space=pltpu.SMEM)] + [pl.BlockSpec(memory_space=pltpu.VMEM)] * rows,
-        out_specs=pl.BlockSpec(memory_space=pltpu.VMEM),
-        compiler_params=params(),
-        name="arrange",
-    )(where, *blocks)
-
-
 def reorder(where, natural):
     tokens, features = natural.shape
     part = tokens // 8
 
-    def kernel(where_ref, x, out):
+    def kernel(where_ref, x, out, second):
         for place in range(8):
             start = pl.multiple_of(token_block(place, where_ref[1]) * part, part)
-            out[place * part : (place + 1) * part, :] = x[pl.ds(start, part), :]
-
-    return pl.pallas_call(
-        kernel,
-        out_shape=jax.ShapeDtypeStruct((tokens, features), BF16),
+            rows = x[pl.ds(start, part), :]
+            out[place * part : (place + 1) * part, :] = rows
+            if place >= 4:
+                second[(place - 4) * part : (place - 3) * part, :] = rows
+
+    return pl.pallas_call(
+        kernel,
+        out_shape=[
+            jax.ShapeDtypeStruct((tokens, features), BF16),
+            jax.ShapeDtypeStruct((tokens // 2, features), BF16),
+        ],
         in_specs=[pl.BlockSpec(memory_space=pltpu.SMEM), pl.BlockSpec(memory_space=pltpu.VMEM)],
-        out_specs=pl.BlockSpec(memory_space=pltpu.VMEM),
+        out_specs=[pl.BlockSpec(memory_space=pltpu.VMEM)] * 2,
         compiler_params=params(),
         name="reorder",
     )(where, natural)
@@ -123,7 +105,7 @@
 
 
 def partial_hidden_grad(here, there, w_here, w_there, start, size, tile):
-    tokens, features = here.shape
+    tokens, features = there.shape
     part = tokens // 4
 
     def kernel(x, y, w, v, own, for_x, for_y, for_far):
@@ -371,34 +353,38 @@
         )
 
     stored = {}
-    grad_out_all = arrange(where, [grad_out] + [onward(grad_out, rows, step) for step in range(1, rows)])
+    grad_out_all = lax.all_gather(grad_out, "row", axis=0, tiled=True)
     w_there = swap(w_down, 1)
     both0, both1 = stack(0), stack(1)
     x0, y0 = swap(both0, 2), swap(both0, 4)
-    far0 = [swap(x0[:part], 4), swap(y0[part:], 2)]
+    x0, y0 = after(x0, both1), after(y0, both1)
+    over_y, over_x = x0[:part], y0[part:]
+    far0 = [swap(over_y, 4), swap(over_x, 2)]
+    both1 = after(both1, (over_y, over_x))
     x1, y1 = swap(both1, 2), swap(both1, 4)
-    here = grad_out_all[: tokens // 2]
-    grad_out_there = swap(grad_out_all[tokens // 2 :], 1)
+    grad_out_all, for_peer = reorder(where, after(grad_out_all, (far0, w_there)))
+    here = grad_out_all
+    grad_out_there = swap(for_peer, 1)
     inputs_all = lax.all_gather(after(inputs, here), "row", axis=0, tiled=True)
 
     own0, sent0 = hidden_part(0, here)
     got0 = send_hidden(sent0)
-    own1, sent1 = hidden_part(1, own0)
-    x0, y0, *far0 = [after(piece, own1) for piece in (x0, y0, *far0)]
-    stored[0] = both_cores([both0, x0, y0, *far0])
+    own1, sent1 = hidden_part(1, (own0, x1, y1))
+    got1 = send_hidden(sent1)
+    hidden0 = total_hidden_grad(after(own0, own1), *got0)
+    hidden0_all = lax.all_gather(hidden0, "col", axis=0, tiled=True)
+    stored[0] = both_cores([both0, x0, y0, *[after(piece, hidden0) for piece in far0]])
     x1, y1 = after(x1, stored[0][0]), after(y1, stored[0][0])
-    far1 = [swap(x1[:part], 4), swap(y1[part:], 2)]
-    hidden0 = total_hidden_grad(after(own0, (x1, y1)), *got0)
-    hidden0_all = lax.all_gather(hidden0, "col", axis=0, tiled=True)
-    got1 = send_hidden(sent1)
-    inputs_all = reorder(where, after(inputs_all, hidden0))
-    grad_down = down(0, None, inputs_all)
-    hidden1 = total_hidden_grad(after(own1, grad_down), *got1)
+    over_y, over_x = x1[:part], y1[part:]
+    grad_down = down(0, None, (over_y, over_x))
+    far1 = [swap(over_y, 4), swap(over_x, 2)]
+    inputs_all, _ = reorder(where, after(inputs_all, grad_down))
+    hidden1 = total_hidden_grad(after(own1, inputs_all), *got1)
     hidden1_all = lax.all_gather(hidden1, "col", axis=0, tiled=True)
-    stored[1] = both_cores([after(piece, hidden1) for piece in (both1, x1, y1, *far1)])
     grad_gate, grad_up, total = first_part(
-        where, hidden0_all, stored[0], after(inputs_all, stored[1][0]), w_gate, w_up, cut, unit // 2
+        where, hidden0_all, stored[0], after(inputs_all, hidden1), w_gate, w_up, cut, unit // 2
     )
+    stored[1] = both_cores([after(piece, total) for piece in (both1, x1, y1, *far1)])
     gate_grad, up_grad, *sums = input_part(
         where, rows, hidden1_all, stored[1], w_gate, w_up, total, *chunks[1], unit // 2
     )

time: 255 us -> 235 us (0.922)
  waiting for transfers between devices: 80.2 us -> 70.3 us
  starting transfers between devices: 32.3 us -> 26.3 us
  local copies, waits for them, and re-layouts: 13.9 us -> 9.63 us
    ppermute x6 -> x3, waiting for transfers between devices: 10.6 us -> 0.01 us  [onward(): lax.ppermute(array, 'row', [(i, (i + step) % rows) for i in range(rows)])]
    ppermute x6 -> x3, starting transfers between devices: 12.9 us -> 5.38 us  [onward(): lax.ppermute(array, 'row', [(i, (i + step) % rows) for i in range(rows)])]
    ppermute x18, waiting for transfers between devices: 60.4 us -> 67.4 us  [swap(): return lax.ppermute(array, 'col', [(i, i ^ bit) for i in range(8)])]
    all_gather x1, waiting for transfers between devices: 9.17 us -> 2.71 us  [on_square(): hidden1_all = lax.all_gather(hidden1, 'col', axis=0, tiled=True)]
  transfers between devices with their start and end apart: 27 -> 25, of which waited for: 8 -> 13; matrix products, arithmetic and copies ran while one was open for 2% -> 2% of each run, Pallas kernels for 36% -> 38%
where the time goes in v2:
time: 235 us; the launch traced here: 234 us
  Pallas kernels  113 us (48%)
  waiting for transfers between devices  70.3 us (30%)
  starting transfers between devices  26.3 us (11%)
  between operations  14 us (6%)
  local copies, waits for them, and re-layouts  9.63 us (4%)
    ppermute x18, waiting for transfers between devices, swap(): return lax.ppermute(array, 'col', [(i, i ^ bit) for i in range(8)])  67.4 us
    pallas_call x1, Pallas kernels, first_part(): pl.pallas_call(kernel, grid=(size // tile,), in_specs=[pl.BlockSpec(memor...  21.9 us
    ppermute x18, starting transfers between devices, swap(): return lax.ppermute(array, 'col', [(i, i ^ bit) for i in range(8)])  20.8 us
    pallas_call x1, Pallas kernels, input_part(): pl.pallas_call(kernel, grid=(steps,), in_specs=[pl.BlockSpec(memory_space...  19.6 us
    pallas_call x2, Pallas kernels, grad_down_part(): pl.pallas_call(kernel, grid=(size // tile,), in_specs=[block] * 2 + [whol...  19.5 us
    pallas_call x2, Pallas kernels, partial_hidden_grad(): pl.pallas_call(kernel, grid=(size // tile,), in_specs=[whole_block((token...  18.7 us
    pallas_call x1, Pallas kernels, weight_part(): pl.pallas_call(kernel, grid=(size // tile,), in_specs=[block, block, whol...  14 us
    pallas_call x2, Pallas kernels, pack(): pl.pallas_call(kernel, grid=(2,), in_specs=[pl.BlockSpec((count, tile), l...  7.01 us
  transfers between devices with their start and end apart: 25, of which 13 were waited for; matrix products, arithmetic and copies ran while one was open for 2% of the time, Pallas kernels for 38%

profile of v2, /device:TPU:0, one launch (start us, length us, event | category | flops | bytes accessed | tf_op | source)
XLA Modules:
  0.0 234.1 jit_solution(4753705280916892046)
XLA Ops:
  8.0 1.0 slice.24
  9.0 1.0 slice.25
  10.1 3.0 %collective-permute-start.2 = (bf16[128,3072]{1,0:T(8,128)(2,1)S(1)}, bf16[128,3072]{1,0:T(8,128)(2,1)S(1)}, u32[]{:S(2)}, u32[]{:S(2)}) collective-permute-start(bf16[128,3072]{1,0:T(8,128)(2,1)S(1)} %pad_maximum_fusion.1.refs_0_), channel_id=1, source_target_pairs={{0,4},{1,5},{2,6},{3,7},{4,0},{5,1},{6,2},{7,3},{8,12},{9,13},{10,... | collective-permute-start | bytes 2359304 | tf_op jit(solution)/shard_map/ppermute | solution.py:50
  13.1 1.5 collective-permute-start
  14.7 16.0 %collective-permute-done.2.refs_2_ = bf16[128,3072]{1,0:T(8,128)(2,1)S(1)} collective-permute-done((bf16[128,3072]{1,0:T(8,128)(2,1)S(1)}, bf16[128,3072]{1,0:T(8,128)(2,1)S(1)}, u32[]{:S(2)}, u32[]{:S(2)}) %collective-permute-start.2) | collective-permute-done | bytes 786464 | tf_op jit(solution)/shard_map/ppermute | solution.py:50
  30.8 1.8 collective-permute-start.3
  32.6 0.8 slice.28
  33.6 1.5 collective-permute-start.1
  35.7 5.6 %collective-permute-done.3.refs_4_ = bf16[64,3072]{1,0:T(8,128)(2,1)S(1)} collective-permute-done((bf16[64,3072]{1,0:T(8,128)(2,1)S(1)}, bf16[64,3072]{1,0:T(8,128)(2,1)S(1)}, u32[]{:S(2)}, u32[]{:S(2)}) %collective-permute-start.3) | collective-permute-done | bytes 393248 | tf_op jit(solution)/shard_map/ppermute | solution.py:50
  41.3 2.3 %collective-permute-done.1.refs_3_ = bf16[64,3072]{1,0:T(8,128)(2,1)S(1)} collective-permute-done((bf16[64,3072]{1,0:T(8,128)(2,1)}, bf16[64,3072]{1,0:T(8,128)(2,1)S(1)}, u32[]{:S(2)}, u32[]{:S(2)}) %collective-permute-start.1) | collective-permute-done | bytes 393248 | tf_op jit(solution)/shard_map/ppermute | solution.py:50
  43.7 2.6 %reorder.2 = (bf16[512,1024]{1,0:T(8,128)(2,1)}, bf16[256,1024]{1,0:T(8,128)(2,1)}) custom-call(s32[2]{0:T(128)} %pad_add_fusion.where_ref, bf16[512,1024]{1,0:T(8,128)(2,1)} %all-gather.5.cloned.1.call-done.x), custom_call_target="tpu_custom_call" | custom-call | tf_op jit(solution)/shard_map/reorder/pallas_call | solution.py:78
  46.4 1.6 collective-permute-start.7
  48.0 1.1 collective-permute-start.6
  49.1 2.1 collective-permute-done.5.y
  51.2 0.8 copy-done.6
  52.0 8.4 %partial_hidden_grad.2 = (f32[64,3072]{1,0:T(8,128)}, bf16[64,3072]{1,0:T(8,128)(2,1)}, bf16[64,3072]{1,0:T(8,128)(2,1)}, bf16[64,3072]{1,0:T(8,128)(2,1)}) custom-call(bf16[512,1024]{1,0:T(8,128)(2,1)} %get-tuple-element.88.x, bf16[256,1024]{1,0:T(8,128)(2,1)} %copy-done.6, bf16[7168,1024]{1,0:T(8,128)(2,1)} %w.3, bf16[7168,1024]{1,0:T(8,128)(2,1)} %collective-permute-done.4.v), custom_call_target="tpu_custom_call" | custom-call | tf_op jit(solution)/shard_map/partial_hidden_grad/pallas_call | solution.py:121
  60.4 1.0 collective-permute-start.8
  62.1 1.8 collective-permute-start.10
  64.0 8.6 %collective-permute-done.7.refs_2_ = bf16[128,4096]{1,0:T(8,128)(2,1)S(1)} collective-permute-done((bf16[128,4096]{1,0:T(8,128)(2,1)S(1)}, bf16[128,4096]{1,0:T(8,128)(2,1)S(1)}, u32[]{:S(2)}, u32[]{:S(2)}) %collective-permute-start.7) | collective-permute-done | bytes 1048608 | tf_op jit(solution)/shard_map/ppermute | solution.py:50
  72.6 1.5 collective-permute-done.6.refs_1_
  74.1 10.3 %partial_hidden_grad.3 = (f32[64,4096]{1,0:T(8,128)}, bf16[64,4096]{1,0:T(8,128)(2,1)}, bf16[64,4096]{1,0:T(8,128)(2,1)}, bf16[64,4096]{1,0:T(8,128)(2,1)}) custom-call(bf16[512,1024]{1,0:T(8,128)(2,1)} %get-tuple-element.88.x, bf16[256,1024]{1,0:T(8,128)(2,1)} %copy-done.6, bf16[7168,1024]{1,0:T(8,128)(2,1)} %w.3, bf16[7168,1024]{1,0:T(8,128)(2,1)} %collective-permute-done.4.v), custom_call_target="tpu_custom_call" | custom-call | tf_op jit(solution)/shard_map/partial_hidden_grad/pallas_call | solution.py:121
  84.4 3.1 %collective-permute-done.10.d = bf16[64,3072]{1,0:T(8,128)(2,1)S(1)} collective-permute-done((bf16[64,3072]{1,0:T(8,128)(2,1)}, bf16[64,3072]{1,0:T(8,128)(2,1)S(1)}, u32[]{:S(2)}, u32[]{:S(2)}) %collective-permute-start.10) | collective-permute-done | bytes 393248 | tf_op jit(solution)/shard_map/ppermute | solution.py:50
  87.5 0.8 copy-done.15
  88.3 2.4 %total_hidden_grad.2 = bf16[64,3072]{1,0:T(8,128)(2,1)} custom-call(f32[64,3072]{1,0:T(8,128)} %get-tuple-element.60.a, bf16[64,3072]{1,0:T(8,128)(2,1)} %copy-done.13, bf16[64,3072]{1,0:T(8,128)(2,1)} %copy-done.14, bf16[64,3072]{1,0:T(8,128)(2,1)} %copy-done.15), custom_call_target="tpu_custom_call" | custom-call | tf_op jit(solution)/shard_map/total_hidden_grad/pallas_call | solution.py:136
  90.8 3.3 %pack.2.p0 = bf16[512,3072]{1,0:T(8,128)(2,1)} custom-call(bf16[128,3072]{1,0:T(8,128)(2,1)} %copy-done.2, bf16[128,3072]{1,0:T(8,128)(2,1)} %copy-done.8, bf16[128,3072]{1,0:T(8,128)(2,1)} %copy-done.7, bf16[64,3072]{1,0:T(8,128)(2,1)} %copy-done.12, bf16[64,3072]{1,0:T(8,128)(2,1)} %copy-done.11), custom_call_target="tpu_custom_call" | custom-call | tf_op jit(solution)/shard_map/pack/pallas_call | solution.py:312
  94.0 1.2 collective-permute-start.12
  95.2 1.7 collective-permute-start.13
  97.6 2.3 collective-permute-done.11.p1
  99.9 1.8 copy-done
  101.7 8.8 %grad_down_part.2.rest_0_ = bf16[7168,1024]{1,0:T(8,128)(2,1)} custom-call(bf16[512,3072]{1,0:T(8,128)(2,1)} %pack.2.p0, bf16[512,3072]{1,0:T(8,128)(2,1)} %copy-done, bf16[512,1024]{1,0:T(8,128)(2,1)} %get-tuple-element.88.x), custom_call_target="tpu_custom_call" | custom-call | tf_op jit(solution)/shard_map/grad_down_part/pallas_call | solution.py:166
  110.5 2.5 %reorder.3 = (bf16[512,1024]{1,0:T(8,128)(2,1)}, bf16[256,1024]{1,0:T(8,128)(2,1)}) custom-call(s32[2]{0:T(128)} %pad_add_fusion.where_ref, bf16[512,1024]{1,0:T(8,128)(2,1)} %all-gather.7.cloned.1.call-done.x), custom_call_target="tpu_custom_call" | custom-call | tf_op jit(solution)/shard_map/reorder/pallas_call | solution.py:78
  113.3 8.9 %collective-permute-done.13.c = bf16[64,4096]{1,0:T(8,128)(2,1)} collective-permute-done((bf16[64,4096]{1,0:T(8,128)(2,1)}, bf16[64,4096]{1,0:T(8,128)(2,1)}, u32[]{:S(2)}, u32[]{:S(2)}) %collective-permute-start.13) | collective-permute-done | bytes 524320 | tf_op jit(solution)/shard_map/ppermute | solution.py:50
  122.2 8.7 %collective-permute-done.14.d = bf16[64,4096]{1,0:T(8,128)(2,1)} collective-permute-done((bf16[64,4096]{1,0:T(8,128)(2,1)}, bf16[64,4096]{1,0:T(8,128)(2,1)}, u32[]{:S(2)}, u32[]{:S(2)}) %collective-permute-start.14) | collective-permute-done | bytes 524320 | tf_op jit(solution)/shard_map/ppermute | solution.py:50
  130.9 2.7 %total_hidden_grad.3 = bf16[64,4096]{1,0:T(8,128)(2,1)} custom-call(f32[64,4096]{1,0:T(8,128)} %get-tuple-element.71.a, bf16[64,4096]{1,0:T(8,128)(2,1)} %collective-permute-done.12.b, bf16[64,4096]{1,0:T(8,128)(2,1)} %collective-permute-done.13.c, bf16[64,4096]{1,0:T(8,128)(2,1)} %collective-permute-done.14.d), custom_call_target="tpu_custom_call" | custom-call | tf_op jit(solution)/shard_map/total_hidden_grad/pallas_call | solution.py:136
  133.6 2.2 collective-permute-start.16
  136.4 21.9 %first_part.1 = (bf16[1024,7168]{1,0:T(8,128)(2,1)}, bf16[1024,7168]{1,0:T(8,128)(2,1)}, f32[512,1024]{1,0:T(8,128)}) custom-call(s32[2]{0:T(128)} %pad_add_fusion.where_ref, bf16[512,3072]{1,0:T(8,128)(2,1)} %all-gather.11.cloned.1.call-done.h, bf16[512,3072]{1,0:T(8,128)(2,1)} %pack.2.p0, bf16[512,3072]{1,0:T(8,128)(2,1)} %copy-done, ...), custom_call_target="tpu_custom_call" | custom-call | tf_op jit(solution)/shard_map/first_part/pallas_call | solution.py:211
  158.3 0.8 copy-done.9
  159.1 0.8 copy-done.10
  159.9 3.7 %pack.3.p0 = bf16[512,4096]{1,0:T(8,128)(2,1)} custom-call(bf16[128,4096]{1,0:T(8,128)(2,1)} %copy-done.1, bf16[128,4096]{1,0:T(8,128)(2,1)} %copy-done.4, bf16[128,4096]{1,0:T(8,128)(2,1)} %copy-done.3, bf16[64,4096]{1,0:T(8,128)(2,1)} %copy-done.10, bf16[64,4096]{1,0:T(8,128)(2,1)} %copy-done.9), custom_call_target="tpu_custom_call" | custom-call | tf_op jit(solution)/shard_map/pack/pallas_call | solution.py:312
  163.7 7.9 %collective-permute-done.17.p1 = bf16[512,4096]{1,0:T(8,128)(2,1)} collective-permute-done((bf16[512,4096]{1,0:T(8,128)(2,1)}, bf16[512,4096]{1,0:T(8,128)(2,1)}, u32[]{:S(2)}, u32[]{:S(2)}) %collective-permute-start.17) | collective-permute-done | bytes 4194336 | tf_op jit(solution)/shard_map/ppermute | solution.py:50
  171.5 2.7 %all-gather.9.cloned.1.call-done.h = bf16[512,4096]{1,0:T(8,128)(2,1)} async-done(((bf16[64,4096]{1,0:T(8,128)(2,1)}), bf16[512,4096]{1,0:T(8,128)(2,1)}) %all-gather.9.cloned.1.call-update) | async-done | bytes 4194320 | tf_op jit(solution)/shard_map/all_gather | solution.py:383
  174.2 19.6 %input_part.1 = (bf16[512,4096]{1,0:T(8,128)(2,1)}, bf16[512,4096]{1,0:T(8,128)(2,1)}, f32[128,1024]{1,0:T(8,128)}, bf16[128,1024]{1,0:T(8,128)(2,1)}, bf16[128,...) custom-call(s32[2]{0:T(128)} %pad_add_fusion.where_ref, bf16[512,4096]{1,0:T(8,128)(2,1)} %all-gather.9.cloned.1.call-done.h, ...), custom_call_target="tpu_custom_call" | custom-call | tf_op jit(solution)/shard_map/input_part/pallas_call | solution.py:261
  193.9 1.5 collective-permute-start.18
  195.4 2.4 %collective-permute-start.19 = (bf16[128,1024]{1,0:T(8,128)(2,1)}, bf16[128,1024]{1,0:T(8,128)(2,1)S(1)}, u32[]{:S(2)}, u32[]{:S(2)}) collective-permute-start(bf16[128,1024]{1,0:T(8,128)(2,1)} %get-tuple-element.91), channel_id=1, source_target_pairs={{0,16},{8,24},{16,0},{24,8},{1,17},{9,25},{17,1},{25,9},{2,18},{10... | collective-permute-start | bytes 786440 | tf_op jit(solution)/shard_map/ppermute | solution.py:54
  197.8 1.4 collective-permute-start.20
  199.3 14.0 %weight_part.1 = (bf16[1024,7168]{1,0:T(8,128)(2,1)}, bf16[1024,7168]{1,0:T(8,128)(2,1)}) custom-call(bf16[512,4096]{1,0:T(8,128)(2,1)} %get-tuple-element.83.a, bf16[512,4096]{1,0:T(8,128)(2,1)} %get-tuple-element.84.b, bf16[512,1024]{1,0:T(8,128)(2,1)} %get-tuple-element.75.x, ...), custom_call_target="tpu_custom_call", output_to_operand_aliasing={{0}: (3, {}), {1}: (4, {})} | custom-call | tf_op jit(solution)/shard_map/weight_part/pallas_call | solution.py:288
  213.2 10.7 %grad_down_part.3 = bf16[7168,1024]{1,0:T(8,128)(2,1)} custom-call(bf16[512,4096]{1,0:T(8,128)(2,1)} %pack.3.p0, bf16[512,4096]{1,0:T(8,128)(2,1)} %collective-permute-done.17.p1, bf16[512,1024]{1,0:T(8,128)(2,1)} %get-tuple-element.88.x, bf16[7168,1024]{1,0:T(8,128)(2,1)} %grad_down_part.2.rest_0_), custom_call_target="tpu_custom_call", output_to_operand_aliasing={{}: (3, {})} | custom-call | tf_op jit(solution)/shard_map/grad_down_part/pallas_call | solution.py:166
  225.4 2.1 sum_rows.1
  (71 shorter events, 5.7 us)
Async XLA Ops:
  7.2 7.5 %slice-start = ((bf16[64,7168]{1,0:T(8,128)(2,1)}), bf16[64,4096]{1,0:T(8,128)(2,1)S(1)}, s32[]{:S(2)}) async-start(bf16[64,7168]{1,0:T(8,128)(2,1)} %param.9), calls=%async_computation.4 | async-start | bytes 1048576 | tf_op jit(solution)/shard_map/slice | solution.py:339
  7.2 7.5 %slice-start.1 = ((bf16[64,7168]{1,0:T(8,128)(2,1)}), bf16[64,4096]{1,0:T(8,128)(2,1)S(1)}, s32[]{:S(2)}) async-start(bf16[64,7168]{1,0:T(8,128)(2,1)} %param.10), calls=%async_computation.5 | async-start | bytes 1048576 | tf_op jit(solution)/shard_map/slice | solution.py:339
  7.2 36.5 %all-gather.5.cloned.1.call-start = ((), (), s32[]{:S(2)}) async-start(), calls=%async_computation | async-start | bytes 1310720 | tf_op jit(solution)/shard_map/all_gather | solution.py:356
  7.2 36.5 %collective-permute-start.4 = (bf16[7168,1024]{1,0:T(8,128)(2,1)}, bf16[7168,1024]{1,0:T(8,128)(2,1)}, u32[]{:S(2)}, u32[]{:S(2)}) collective-permute-start(bf16[7168,1024]{1,0:T(8,128)(2,1)} %w.3), channel_id=1, source_target_pairs={{0,1},{1,0},{2,3},{3,2},{4,5},{5,4},{6,7},{7,6},{8,9},{9,8},{10,11... | collective-permute-start | bytes 44040200 | tf_op jit(solution)/shard_map/ppermute | solution.py:50
  7.9 102.6 %all-gather.7.cloned.1.call-start = ((), (), s32[]{:S(2)}) async-start(), calls=%async_computation.1 | async-start | bytes 1310720 | tf_op jit(solution)/shard_map/all_gather | solution.py:368
  10.1 50.3 %copy-start.2 = (bf16[128,3072]{1,0:T(8,128)(2,1)}, bf16[128,3072]{1,0:T(8,128)(2,1)S(1)}, u32[]{:S(2)}) copy-start(bf16[128,3072]{1,0:T(8,128)(2,1)S(1)} %pad_maximum_fusion.1.refs_0_) | copy-start | bytes 2359300
  10.1 20.6 %collective-permute-start.2 = (bf16[128,3072]{1,0:T(8,128)(2,1)S(1)}, bf16[128,3072]{1,0:T(8,128)(2,1)S(1)}, u32[]{:S(2)}, u32[]{:S(2)}) collective-permute-start(bf16[128,3072]{1,0:T(8,128)(2,1)S(1)} %pad_maximum_fusion.1.refs_0_), channel_id=1, source_target_pairs={{0,4},{1,5},{2,6},{3,7},{4,0},{5,1},{6,2},{7,3},{8,12},{9,13},{10,... | collective-permute-start | bytes 2359304 | tf_op jit(solution)/shard_map/ppermute | solution.py:50
  13.1 19.4 %collective-permute-start = (bf16[128,3072]{1,0:T(8,128)(2,1)S(1)}, bf16[128,3072]{1,0:T(8,128)(2,1)S(1)}, u32[]{:S(2)}, u32[]{:S(2)}) collective-permute-start(bf16[128,3072]{1,0:T(8,128)(2,1)S(1)} %pad_maximum_fusion.1.refs_0_), channel_id=1, source_target_pairs={{0,2},{1,3},{2,0},{3,1},{4,6},{5,7},{6,4},{7,5},{8,10},{9,11},{10,... | collective-permute-start | bytes 2359304 | tf_op jit(solution)/shard_map/ppermute | solution.py:50
  14.7 45.7 %copy-start.1 = (bf16[128,4096]{1,0:T(8,128)(2,1)}, bf16[128,4096]{1,0:T(8,128)(2,1)S(1)}, u32[]{:S(2)}) copy-start(bf16[128,4096]{1,0:T(8,128)(2,1)S(1)} %pad_maximum_fusion.refs_0_) | copy-start | bytes 3145732
  30.7 1.8 copy-start.7
  30.8 10.6 %collective-permute-start.3 = (bf16[64,3072]{1,0:T(8,128)(2,1)S(1)}, bf16[64,3072]{1,0:T(8,128)(2,1)S(1)}, u32[]{:S(2)}, u32[]{:S(2)}) collective-permute-start(bf16[64,3072]{1,0:T(8,128)(2,1)S(1)} %slice.29), channel_id=1, source_target_pairs={{0,2},{1,3},{2,0},{3,1},{4,6},{5,7},{6,4},{7,5},{8,10},{9,11},{10,... | collective-permute-start | bytes 1179656 | tf_op jit(solution)/shard_map/ppermute | solution.py:50
  32.6 1.0 copy-start.8
  33.6 10.1 %collective-permute-start.1 = (bf16[64,3072]{1,0:T(8,128)(2,1)}, bf16[64,3072]{1,0:T(8,128)(2,1)S(1)}, u32[]{:S(2)}, u32[]{:S(2)}) collective-permute-start(bf16[64,3072]{1,0:T(8,128)(2,1)} %slice.28), channel_id=1, source_target_pairs={{0,4},{1,5},{2,6},{3,7},{4,0},{5,1},{6,2},{7,3},{8,12},{9,13},{10,... | collective-permute-start | bytes 1179656 | tf_op jit(solution)/shard_map/ppermute | solution.py:50
  41.3 19.1 %copy-start.11 = (bf16[64,3072]{1,0:T(8,128)(2,1)}, bf16[64,3072]{1,0:T(8,128)(2,1)S(1)}, u32[]{:S(2)}) copy-start(bf16[64,3072]{1,0:T(8,128)(2,1)S(1)} %collective-permute-done.3.refs_4_) | copy-start | bytes 1179652
  43.7 2.7 %copy-start.12 = (bf16[64,3072]{1,0:T(8,128)(2,1)}, bf16[64,3072]{1,0:T(8,128)(2,1)S(1)}, u32[]{:S(2)}) copy-start(bf16[64,3072]{1,0:T(8,128)(2,1)S(1)} %collective-permute-done.1.refs_3_) | copy-start | bytes 1179652
  46.4 90.0 %all-gather.11.cloned.1.call-start = ((), (), s32[]{:S(2)}) async-start(), calls=%async_computation.3 | async-start | bytes 3538944 | tf_op jit(solution)/shard_map/all_gather | solution.py:375
  46.4 26.2 %collective-permute-start.7 = (bf16[128,4096]{1,0:T(8,128)(2,1)S(1)}, bf16[128,4096]{1,0:T(8,128)(2,1)S(1)}, u32[]{:S(2)}, u32[]{:S(2)}) collective-permute-start(bf16[128,4096]{1,0:T(8,128)(2,1)S(1)} %pad_maximum_fusion.refs_0_), channel_id=1, source_target_pairs={{0,4},{1,5},{2,6},{3,7},{4,0},{5,1},{6,2},{7,3},{8,12},{9,13},{10,... | collective-permute-start | bytes 3145736 | tf_op jit(solution)/shard_map/ppermute | solution.py:50
  48.0 26.1 %collective-permute-start.6 = (bf16[128,4096]{1,0:T(8,128)(2,1)S(1)}, bf16[128,4096]{1,0:T(8,128)(2,1)S(1)}, u32[]{:S(2)}, u32[]{:S(2)}) collective-permute-start(bf16[128,4096]{1,0:T(8,128)(2,1)S(1)} %pad_maximum_fusion.refs_0_), channel_id=1, source_target_pairs={{0,2},{1,3},{2,0},{3,1},{4,6},{5,7},{6,4},{7,5},{8,10},{9,11},{10,... | collective-permute-start | bytes 3145736 | tf_op jit(solution)/shard_map/ppermute | solution.py:50
  49.0 2.1 collective-permute-start.5
  51.2 0.8 copy-start.6
  60.4 24.0 %collective-permute-start.8 = (bf16[64,3072]{1,0:T(8,128)(2,1)}, bf16[64,3072]{1,0:T(8,128)(2,1)S(1)}, u32[]{:S(2)}, u32[]{:S(2)}) collective-permute-start(bf16[64,3072]{1,0:T(8,128)(2,1)} %get-tuple-element.61), channel_id=1, source_target_pairs={{0,2},{1,3},{2,0},{3,1},{4,6},{5,7},{6,4},{7,5},{8,10},{9,11},{10,... | collective-permute-start | bytes 1179656 | tf_op jit(solution)/shard_map/ppermute | solution.py:50
  61.4 23.0 %collective-permute-start.9 = (bf16[64,3072]{1,0:T(8,128)(2,1)}, bf16[64,3072]{1,0:T(8,128)(2,1)S(1)}, u32[]{:S(2)}, u32[]{:S(2)}) collective-permute-start(bf16[64,3072]{1,0:T(8,128)(2,1)} %get-tuple-element.62), channel_id=1, source_target_pairs={{0,4},{1,5},{2,6},{3,7},{4,0},{5,1},{6,2},{7,3},{8,12},{9,13},{10,... | collective-permute-start | bytes 1179656 | tf_op jit(solution)/shard_map/ppermute | solution.py:50
  62.1 25.4 %collective-permute-start.10 = (bf16[64,3072]{1,0:T(8,128)(2,1)}, bf16[64,3072]{1,0:T(8,128)(2,1)S(1)}, u32[]{:S(2)}, u32[]{:S(2)}) collective-permute-start(bf16[64,3072]{1,0:T(8,128)(2,1)} %get-tuple-element.63), channel_id=1, source_target_pairs={{0,6},{1,7},{2,4},{3,5},{4,2},{5,3},{6,0},{7,1},{8,14},{9,15},{10,... | collective-permute-start | bytes 1179656 | tf_op jit(solution)/shard_map/ppermute | solution.py:50
  72.6 25.0 %copy-start.3 = (bf16[128,4096]{1,0:T(8,128)(2,1)}, bf16[128,4096]{1,0:T(8,128)(2,1)S(1)}, u32[]{:S(2)}) copy-start(bf16[128,4096]{1,0:T(8,128)(2,1)S(1)} %collective-permute-done.7.refs_2_) | copy-start | bytes 3145732
  74.1 10.3 %copy-start.4 = (bf16[128,4096]{1,0:T(8,128)(2,1)}, bf16[128,4096]{1,0:T(8,128)(2,1)S(1)}, u32[]{:S(2)}) copy-start(bf16[128,4096]{1,0:T(8,128)(2,1)S(1)} %collective-permute-done.6.refs_1_) | copy-start | bytes 3145732
  84.4 13.1 %copy-start.5 = (bf16[128,4096]{1,0:T(8,128)(2,1)S(1)}, bf16[128,4096]{1,0:T(8,128)(2,1)}, u32[]{:S(2)}) copy-start(bf16[128,4096]{1,0:T(8,128)(2,1)} %copy-done.4) | copy-start | bytes 3145732
  84.4 3.1 %copy-start.13 = (bf16[64,3072]{1,0:T(8,128)(2,1)}, bf16[64,3072]{1,0:T(8,128)(2,1)S(1)}, u32[]{:S(2)}) copy-start(bf16[64,3072]{1,0:T(8,128)(2,1)S(1)} %collective-permute-done.8.b) | copy-start | bytes 1179652
  84.4 3.1 %copy-start.14 = (bf16[64,3072]{1,0:T(8,128)(2,1)}, bf16[64,3072]{1,0:T(8,128)(2,1)S(1)}, u32[]{:S(2)}) copy-start(bf16[64,3072]{1,0:T(8,128)(2,1)S(1)} %collective-permute-done.9.c) | copy-start | bytes 1179652
  87.5 0.8 copy-start.15
  90.7 83.5 %all-gather.9.cloned.1.call-start = ((), (), s32[]{:S(2)}) async-start(), calls=%async_computation.2 | async-start | bytes 4718592 | tf_op jit(solution)/shard_map/all_gather | solution.py:383
  94.0 5.9 %collective-permute-start.11 = (bf16[512,3072]{1,0:T(8,128)(2,1)}, bf16[512,3072]{1,0:T(8,128)(2,1)S(1)}, u32[]{:S(2)}, u32[]{:S(2)}) collective-permute-start(bf16[512,3072]{1,0:T(8,128)(2,1)} %pack.2.p0), channel_id=1, source_target_pairs={{0,1},{1,0},{2,3},{3,2},{4,5},{5,4},{6,7},{7,6},{8,9},{9,8},{10,11... | collective-permute-start | bytes 9437192 | tf_op jit(solution)/shard_map/ppermute | solution.py:50
  94.0 19.2 %collective-permute-start.12 = (bf16[64,4096]{1,0:T(8,128)(2,1)}, bf16[64,4096]{1,0:T(8,128)(2,1)}, u32[]{:S(2)}, u32[]{:S(2)}) collective-permute-start(bf16[64,4096]{1,0:T(8,128)(2,1)} %get-tuple-element.72), channel_id=1, source_target_pairs={{0,2},{1,3},{2,0},{3,1},{4,6},{5,7},{6,4},{7,5},{8,10},{9,11},{10,... | collective-permute-start | bytes 1572872 | tf_op jit(solution)/shard_map/ppermute | solution.py:50
  95.2 27.0 %collective-permute-start.13 = (bf16[64,4096]{1,0:T(8,128)(2,1)}, bf16[64,4096]{1,0:T(8,128)(2,1)}, u32[]{:S(2)}, u32[]{:S(2)}) collective-permute-start(bf16[64,4096]{1,0:T(8,128)(2,1)} %get-tuple-element.73), channel_id=1, source_target_pairs={{0,4},{1,5},{2,6},{3,7},{4,0},{5,1},{6,2},{7,3},{8,12},{9,13},{10,... | collective-permute-start | bytes 1572872 | tf_op jit(solution)/shard_map/ppermute | solution.py:50
  96.9 34.0 %collective-permute-start.14 = (bf16[64,4096]{1,0:T(8,128)(2,1)}, bf16[64,4096]{1,0:T(8,128)(2,1)}, u32[]{:S(2)}, u32[]{:S(2)}) collective-permute-start(bf16[64,4096]{1,0:T(8,128)(2,1)} %get-tuple-element.74), channel_id=1, source_target_pairs={{0,6},{1,7},{2,4},{3,5},{4,2},{5,3},{6,0},{7,1},{8,14},{9,15},{10,... | collective-permute-start | bytes 1572872 | tf_op jit(solution)/shard_map/ppermute | solution.py:50
  99.9 1.8 copy-start
  133.6 24.7 %collective-permute-start.16 = (bf16[64,4096]{1,0:T(8,128)(2,1)S(1)}, bf16[64,4096]{1,0:T(8,128)(2,1)S(1)}, u32[]{:S(2)}, u32[]{:S(2)}) collective-permute-start(bf16[64,4096]{1,0:T(8,128)(2,1)S(1)} %slice.31), channel_id=1, source_target_pairs={{0,2},{1,3},{2,0},{3,1},{4,6},{5,7},{6,4},{7,5},{8,10},{9,11},{10,... | collective-permute-start | bytes 1572872 | tf_op jit(solution)/shard_map/ppermute | solution.py:50
  135.8 22.5 %collective-permute-start.15 = (bf16[64,4096]{1,0:T(8,128)(2,1)S(1)}, bf16[64,4096]{1,0:T(8,128)(2,1)S(1)}, u32[]{:S(2)}, u32[]{:S(2)}) collective-permute-start(bf16[64,4096]{1,0:T(8,128)(2,1)S(1)} %slice.30), channel_id=1, source_target_pairs={{0,4},{1,5},{2,6},{3,7},{4,0},{5,1},{6,2},{7,3},{8,12},{9,13},{10,... | collective-permute-start | bytes 1572872 | tf_op jit(solution)/shard_map/ppermute | solution.py:50
  158.3 0.8 copy-start.9
  159.1 0.8 copy-start.10
  163.7 7.9 %collective-permute-start.17 = (bf16[512,4096]{1,0:T(8,128)(2,1)}, bf16[512,4096]{1,0:T(8,128)(2,1)}, u32[]{:S(2)}, u32[]{:S(2)}) collective-permute-start(bf16[512,4096]{1,0:T(8,128)(2,1)} %pack.3.p0), channel_id=1, source_target_pairs={{0,1},{1,0},{2,3},{3,2},{4,5},{5,4},{6,7},{7,6},{8,9},{9,8},{10,11... | collective-permute-start | bytes 12582920 | tf_op jit(solution)/shard_map/ppermute | solution.py:50
  193.9 30.1 %collective-permute-start.18 = (bf16[128,1024]{1,0:T(8,128)(2,1)}, bf16[128,1024]{1,0:T(8,128)(2,1)S(1)}, u32[]{:S(2)}, u32[]{:S(2)}) collective-permute-start(bf16[128,1024]{1,0:T(8,128)(2,1)} %get-tuple-element.90), channel_id=1, source_target_pairs={{0,8},{8,16},{16,24},{24,0},{1,9},{9,17},{17,25},{25,1},{2,10},{10... | collective-permute-start | bytes 786440 | tf_op jit(solution)/shard_map/ppermute | solution.py:54
  195.4 28.5 %collective-permute-start.19 = (bf16[128,1024]{1,0:T(8,128)(2,1)}, bf16[128,1024]{1,0:T(8,128)(2,1)S(1)}, u32[]{:S(2)}, u32[]{:S(2)}) collective-permute-start(bf16[128,1024]{1,0:T(8,128)(2,1)} %get-tuple-element.91), channel_id=1, source_target_pairs={{0,16},{8,24},{16,0},{24,8},{1,17},{9,25},{17,1},{25,9},{2,18},{10... | collective-permute-start | bytes 786440 | tf_op jit(solution)/shard_map/ppermute | solution.py:54
  197.8 26.1 %collective-permute-start.20 = (bf16[128,1024]{1,0:T(8,128)(2,1)}, bf16[128,1024]{1,0:T(8,128)(2,1)S(1)}, u32[]{:S(2)}, u32[]{:S(2)}) collective-permute-start(bf16[128,1024]{1,0:T(8,128)(2,1)} %get-tuple-element.92), channel_id=1, source_target_pairs={{0,24},{8,0},{16,8},{24,16},{1,25},{9,1},{17,9},{25,17},{2,26},{10... | collective-permute-start | bytes 786440 | tf_op jit(solution)/shard_map/ppermute | solution.py:54
  223.9 0.7 copy-start.16
  223.9 0.8 copy-start.17
  224.7 0.7 copy-start.18
Sparse Core Ops, SparseCore 0:
  9.6 30.6 all-gather.4
  46.5 28.7 all-gather.6
  90.8 44.2 all-gather.10
  136.8 37.3 all-gather.8

commit v3 on v2

--- a/solution.py
+++ b/solution.py
@@ -127,6 +127,74 @@
         compiler_params=params(),
         name="partial_hidden_grad",
     )(here, there, w_here, w_there)
+
+
+def halved_hidden_grad(here, there, w_here, w_there, start, size, tile):
+    tokens, features = there.shape
+    part = tokens // 4
+    half = part // 2
+
+    def kernel(x, y, w, v, for_x, for_y, keep_x, keep_y):
+        product = dot(x[...], w[...], 1, 1) + dot(y[...], v[...], 1, 1)
+        own, at_x, at_y, far = [product[i * part : (i + 1) * part] for i in range(4)]
+        for_x[:half] = at_x[:half].astype(BF16)
+        for_x[half:] = far[:half].astype(BF16)
+        for_y[:half] = at_y[half:].astype(BF16)
+        for_y[half:] = far[half:].astype(BF16)
+        keep_x[:half] = own[:half]
+        keep_x[half:] = at_y[:half]
+        keep_y[:half] = own[half:]
+        keep_y[half:] = at_x[half:]
+
+    column = pl.BlockSpec((part, tile), lambda i: (0, i))
+    weights = pl.BlockSpec((tile, features), lambda i: (i + start // tile, 0))
+    sent = jax.ShapeDtypeStruct((part, size), BF16)
+    kept = jax.ShapeDtypeStruct((part, size), F32)
+    return pl.pallas_call(
+        kernel,
+        grid=(size // tile,),
+        in_specs=[whole_block((tokens, features))] * 2 + [weights] * 2,
+        out_specs=[column] * 4,
+        out_shape=[sent, sent, kept, kept],
+        compiler_params=params(),
+        name="halved_hidden_grad",
+    )(here, there, w_here, w_there)
+
+
+def pair_sum(keep_x, from_x, keep_y, from_y):
+    part, size = keep_x.shape
+    half = part // 2
+
+    def kernel(a, b, c, d, for_y, for_x, own):
+        upper = a[...] + b[...].astype(F32)
+        lower = c[...] + d[...].astype(F32)
+        own[:half] = upper[:half]
+        own[half:] = lower[:half]
+        for_y[...] = upper[half:].astype(BF16)
+        for_x[...] = lower[half:].astype(BF16)
+
+    sent = jax.ShapeDtypeStruct((half, size), BF16)
+    return pl.pallas_call(
+        kernel,
+        out_shape=[sent, sent, jax.ShapeDtypeStruct((part, size), F32)],
+        compiler_params=params(),
+        name="pair_sum",
+    )(keep_x, from_x, keep_y, from_y)
+
+
+def halves_sum(own, from_y, from_x):
+    half = own.shape[0] // 2
+
+    def kernel(a, b, c, out):
+        out[:half] = (a[:half] + b[...].astype(F32)).astype(BF16)
+        out[half:] = (a[half:] + c[...].astype(F32)).astype(BF16)
+
+    return pl.pallas_call(
+        kernel,
+        out_shape=jax.ShapeDtypeStruct(own.shape, BF16),
+        compiler_params=params(),
+        name="halves_sum",
+    )(own, from_y, from_x)
 
 
 def total_hidden_grad(own, *received):
@@ -274,27 +342,32 @@
     )(where, hidden_grad, *stored, w_gate, w_up, total)
 
 
-def weight_part(gate_grad, up_grad, inputs_all, grad_gate, grad_up, start, tile):
+def weight_part(gate_grad, up_grad, stored, inputs_all, grad_out_all, earlier, start, tile):
     tokens, features = inputs_all.shape
     size = gate_grad.shape[1]
 
-    def kernel(a, b, x, _, __, gate_out, up_out):
+    def kernel(a, b, p0, p1, x, y, *rest):
+        gate_out, up_out, down_out = rest[-3:]
         gate_out[...] = dot(x[...], a[...], 0, 0).astype(BF16)
         up_out[...] = dot(x[...], b[...], 0, 0).astype(BF16)
+        hidden = jnp.concatenate([hidden_of(*unpack(p0[...])), hidden_of(*unpack(p1[...]))], axis=0)
+        down_out[...] = dot(hidden, y[...], 0, 0).astype(BF16)
 
     block = pl.BlockSpec((tokens, tile), lambda i: (0, i))
     column = pl.BlockSpec((features, tile), lambda i: (0, i + start // tile))
-    weights = jax.ShapeDtypeStruct(grad_gate.shape, BF16)
+    row = pl.BlockSpec((tile, features), lambda i: (i + start // tile, 0))
     return pl.pallas_call(
         kernel,
         grid=(size // tile,),
-        in_specs=[block, block, whole_block((tokens, features))] + [pl.BlockSpec(memory_space=pl.ANY)] * 2,
-        out_specs=[column, column],
-        out_shape=[weights, weights],
-        input_output_aliases={3: 0, 4: 1},
+        in_specs=[block] * 4
+        + [whole_block((tokens, features))] * 2
+        + [pl.BlockSpec(memory_space=pl.ANY)] * 3,
+        out_specs=[column, column, row],
+        out_shape=[jax.ShapeDtypeStruct(each.shape, BF16) for each in earlier],
+        input_output_aliases={6: 0, 7: 1, 8: 2},
         compiler_params=params(),
         name="weight_part",
-    )(gate_grad, up_grad, inputs_all, grad_gate, grad_up)
+    )(gate_grad, up_grad, *stored, inputs_all, grad_out_all, *earlier)
 
 
 def pack(pieces):
@@ -369,29 +442,35 @@
 
     own0, sent0 = hidden_part(0, here)
     got0 = send_hidden(sent0)
-    own1, sent1 = hidden_part(1, (own0, x1, y1))
-    got1 = send_hidden(sent1)
-    hidden0 = total_hidden_grad(after(own0, own1), *got0)
+    for_x, for_y, keep_x, keep_y = halved_hidden_grad(
+        after(here, (own0, x1, y1)), grad_out_there, w_down, w_there, *chunks[1], unit
+    )
+    from_x, from_y = swap(for_x, 2), swap(for_y, 4)
+    stored[0] = both_cores([both0, x0, y0, *[after(piece, keep_x) for piece in far0]])
+    hidden0 = total_hidden_grad(after(own0, stored[0][0]), *got0)
     hidden0_all = lax.all_gather(hidden0, "col", axis=0, tiled=True)
-    stored[0] = both_cores([both0, x0, y0, *[after(piece, hidden0) for piece in far0]])
-    x1, y1 = after(x1, stored[0][0]), after(y1, stored[0][0])
+    x1, y1 = after(x1, hidden0), after(y1, hidden0)
     over_y, over_x = x1[:part], y1[part:]
     grad_down = down(0, None, (over_y, over_x))
     far1 = [swap(over_y, 4), swap(over_x, 2)]
-    inputs_all, _ = reorder(where, after(inputs_all, grad_down))
-    hidden1 = total_hidden_grad(after(own1, inputs_all), *got1)
+    for_y, for_x, own1 = pair_sum(after(keep_x, grad_down), from_x, keep_y, from_y)
+    from_y, from_x = swap(for_y, 4), swap(for_x, 2)
+    inputs_all, _ = reorder(where, after(inputs_all, own1))
+    hidden1 = halves_sum(after(own1, inputs_all), from_y, from_x)
     hidden1_all = lax.all_gather(hidden1, "col", axis=0, tiled=True)
     grad_gate, grad_up, total = first_part(
-        where, hidden0_all, stored[0], after(inputs_all, hidden1), w_gate, w_up, cut, unit // 2
+        where, hidden0_all, stored[0], after(inputs_all, hidden1), w_gate, w_up, cut, unit
     )
     stored[1] = both_cores([after(piece, total) for piece in (both1, x1, y1, *far1)])
     gate_grad, up_grad, *sums = input_part(
-        where, rows, hidden1_all, stored[1], w_gate, w_up, total, *chunks[1], unit // 2
+        where, rows, hidden1_all, stored[1], w_gate, w_up, total, *chunks[1], unit
     )
     sums = [sums[0]] + [onward(block, rows, ahead) for ahead, block in enumerate(sums) if ahead]
-    grad_gate, grad_up = weight_part(gate_grad, up_grad, inputs_all, grad_gate, grad_up, cut, unit // 2)
-    grad_down = down(1, grad_down, grad_up)
-    grad_inputs = sum_rows([after(sums[0], grad_down)] + sums[1:])
+    earlier = (grad_gate, grad_up, grad_down)
+    grad_gate, grad_up, grad_down = weight_part(
+        gate_grad, up_grad, stored[1], inputs_all, grad_out_all, earlier, cut, unit
+    )
+    grad_inputs = sum_rows([after(sums[0], grad_up)] + sums[1:])
     return grad_inputs, grad_gate, grad_up, grad_down
 
 

time: 235 us -> 227 us (0.966)
  waiting for transfers between devices: 70.3 us -> 63.8 us
  Pallas kernels: 113 us -> 110 us
    pallas_call x1 -> x4, Pallas kernels: 14 us -> 35.6 us  [the longest x1 19.9 us: weight_part(): pl.pallas_call(kernel, grid=(size // tile,), in_specs=[block] * 4 + [whol...]
    pallas_call x2 -> x1, Pallas kernels: 19.5 us -> 8.86 us  [grad_down_part(): pl.pallas_call(kernel, grid=(size // tile,), in_specs=[block] * 2 + [whol...]
    pallas_call x2 -> x1, Pallas kernels: 18.7 us -> 8.4 us  [partial_hidden_grad(): pl.pallas_call(kernel, grid=(size // tile,), in_specs=[whole_block((token...]
    ppermute x18 -> x19, waiting for transfers between devices: 67.4 us -> 61.7 us  [swap(): return lax.ppermute(array, 'col', [(i, i ^ bit) for i in range(8)])]
    pallas_call x2 -> x1, Pallas kernels: 5.1 us -> 2.38 us  [total_hidden_grad(): pl.pallas_call(kernel, out_shape=jax.ShapeDtypeStruct(own.shape, BF16), c...]
    unnamed x38 -> x46, local copies, waits for them, and re-layouts: 6.65 us -> 8.97 us
    ppermute x18 -> x19, starting transfers between devices: 20.8 us -> 20.4 us  [swap(): return lax.ppermute(array, 'col', [(i, i ^ bit) for i in range(8)])]
  transfers between devices with their start and end apart: 25 -> 26, of which waited for: 13 -> 13; matrix products, arithmetic and copies ran while one was open for 2% -> 2% of each run, Pallas kernels for 38% -> 38%
where the time goes in v3:
time: 227 us; the launch traced here: 226 us
  Pallas kernels  110 us (48%)
  waiting for transfers between devices  63.8 us (28%)
  starting transfers between devices  26.2 us (12%)
  between operations  14 us (6%)
  local copies, waits for them, and re-layouts  11.9 us (5%)
    ppermute x19, waiting for transfers between devices, swap(): return lax.ppermute(array, 'col', [(i, i ^ bit) for i in range(8)])  61.7 us
    pallas_call x1, Pallas kernels, first_part(): pl.pallas_call(kernel, grid=(size // tile,), in_specs=[pl.BlockSpec(memor...  22.2 us
    ppermute x19, starting transfers between devices, swap(): return lax.ppermute(array, 'col', [(i, i ^ bit) for i in range(8)])  20.4 us
    pallas_call x1, Pallas kernels, weight_part(): pl.pallas_call(kernel, grid=(size // tile,), in_specs=[block] * 4 + [whol...  19.9 us
    pallas_call x1, Pallas kernels, input_part(): pl.pallas_call(kernel, grid=(steps,), in_specs=[pl.BlockSpec(memory_space...  18.2 us
    pallas_call x1, Pallas kernels, halved_hidden_grad(): pl.pallas_call(kernel, grid=(size // tile,), in_specs=[whole_block((token...  10.4 us
    unnamed x46, local copies, waits for them, and re-layouts  8.97 us
    pallas_call x1, Pallas kernels, grad_down_part(): pl.pallas_call(kernel, grid=(size // tile,), in_specs=[block] * 2 + [whol...  8.86 us
  transfers between devices with their start and end apart: 26, of which 13 were waited for; matrix products, arithmetic and copies ran while one was open for 2% of the time, Pallas kernels for 38%

profile of v3, /device:TPU:0, one launch (start us, length us, event | category | flops | bytes accessed | tf_op | source)
XLA Modules:
  0.0 226.5 jit_solution(10937006228527875000)
XLA Ops:
  8.0 1.0 slice.24
  9.0 1.0 slice.25
  10.1 3.0 %collective-permute-start.2 = (bf16[128,3072]{1,0:T(8,128)(2,1)S(1)}, bf16[128,3072]{1,0:T(8,128)(2,1)S(1)}, u32[]{:S(2)}, u32[]{:S(2)}) collective-permute-start(bf16[128,3072]{1,0:T(8,128)(2,1)S(1)} %pad_maximum_fusion.1.refs_0_), channel_id=1, source_target_pairs={{0,4},{1,5},{2,6},{3,7},{4,0},{5,1},{6,2},{7,3},{8,12},{9,13},{10,... | collective-permute-start | bytes 2359304 | tf_op jit(solution)/shard_map/ppermute | solution.py:50
  13.1 1.5 collective-permute-start
  14.7 16.0 %collective-permute-done.2.refs_2_ = bf16[128,3072]{1,0:T(8,128)(2,1)S(1)} collective-permute-done((bf16[128,3072]{1,0:T(8,128)(2,1)S(1)}, bf16[128,3072]{1,0:T(8,128)(2,1)S(1)}, u32[]{:S(2)}, u32[]{:S(2)}) %collective-permute-start.2) | collective-permute-done | bytes 786464 | tf_op jit(solution)/shard_map/ppermute | solution.py:50
  30.8 1.8 collective-permute-start.3
  32.6 0.8 slice.28
  33.6 1.5 collective-permute-start.1
  35.7 5.6 %collective-permute-done.3.refs_4_ = bf16[64,3072]{1,0:T(8,128)(2,1)S(1)} collective-permute-done((bf16[64,3072]{1,0:T(8,128)(2,1)S(1)}, bf16[64,3072]{1,0:T(8,128)(2,1)S(1)}, u32[]{:S(2)}, u32[]{:S(2)}) %collective-permute-start.3) | collective-permute-done | bytes 393248 | tf_op jit(solution)/shard_map/ppermute | solution.py:50
  41.3 2.4 %collective-permute-done.1.refs_3_ = bf16[64,3072]{1,0:T(8,128)(2,1)S(1)} collective-permute-done((bf16[64,3072]{1,0:T(8,128)(2,1)}, bf16[64,3072]{1,0:T(8,128)(2,1)S(1)}, u32[]{:S(2)}, u32[]{:S(2)}) %collective-permute-start.1) | collective-permute-done | bytes 393248 | tf_op jit(solution)/shard_map/ppermute | solution.py:50
  43.7 2.6 %reorder.2 = (bf16[512,1024]{1,0:T(8,128)(2,1)}, bf16[256,1024]{1,0:T(8,128)(2,1)}) custom-call(s32[2]{0:T(128)} %pad_add_fusion.where_ref, bf16[512,1024]{1,0:T(8,128)(2,1)} %all-gather.5.cloned.1.call-done.x), custom_call_target="tpu_custom_call" | custom-call | tf_op jit(solution)/shard_map/reorder/pallas_call | solution.py:78
  46.4 1.6 collective-permute-start.7
  48.0 1.1 collective-permute-start.6
  49.1 2.1 collective-permute-done.5.y
  51.2 0.8 copy-done.6
  52.0 8.4 %partial_hidden_grad.1 = (f32[64,3072]{1,0:T(8,128)}, bf16[64,3072]{1,0:T(8,128)(2,1)}, bf16[64,3072]{1,0:T(8,128)(2,1)}, bf16[64,3072]{1,0:T(8,128)(2,1)}) custom-call(bf16[512,1024]{1,0:T(8,128)(2,1)} %get-tuple-element.71.x.y, bf16[256,1024]{1,0:T(8,128)(2,1)} %copy-done.6, bf16[7168,1024]{1,0:T(8,128)(2,1)} %w.3, bf16[7168,1024]{1,0:T(8,128)(2,1)} %collective-permute-done.4.v), custom_call_target="tpu_custom_call" | custom-call | tf_op jit(solution)/shard_map/partial_hidden_grad/pallas_call | solution.py:121
  60.4 1.1 collective-permute-start.9
  62.2 1.8 collective-permute-start.11
  64.0 8.6 %collective-permute-done.7.refs_2_ = bf16[128,4096]{1,0:T(8,128)(2,1)S(1)} collective-permute-done((bf16[128,4096]{1,0:T(8,128)(2,1)S(1)}, bf16[128,4096]{1,0:T(8,128)(2,1)S(1)}, u32[]{:S(2)}, u32[]{:S(2)}) %collective-permute-start.7) | collective-permute-done | bytes 1048608 | tf_op jit(solution)/shard_map/ppermute | solution.py:50
  72.6 1.5 collective-permute-done.6.refs_1_
  74.1 10.4 %halved_hidden_grad.1 = (bf16[64,4096]{1,0:T(8,128)(2,1)}, bf16[64,4096]{1,0:T(8,128)(2,1)}, f32[64,4096]{1,0:T(8,128)}, f32[64,4096]{1,0:T(8,128)}) custom-call(bf16[512,1024]{1,0:T(8,128)(2,1)} %get-tuple-element.71.x.y, bf16[256,1024]{1,0:T(8,128)(2,1)} %copy-done.6, bf16[7168,1024]{1,0:T(8,128)(2,1)} %w.3, bf16[7168,1024]{1,0:T(8,128)(2,1)} %collective-permute-done.4.v), custom_call_target="tpu_custom_call" | custom-call | tf_op jit(solution)/shard_map/halved_hidden_grad/pallas_call | solution.py:153
  84.6 3.3 %pack.2.p0 = bf16[512,3072]{1,0:T(8,128)(2,1)} custom-call(bf16[128,3072]{1,0:T(8,128)(2,1)} %copy-done.2, bf16[128,3072]{1,0:T(8,128)(2,1)} %copy-done.8, bf16[128,3072]{1,0:T(8,128)(2,1)} %copy-done.7, bf16[64,3072]{1,0:T(8,128)(2,1)} %copy-done.14, bf16[64,3072]{1,0:T(8,128)(2,1)} %copy-done.13), custom_call_target="tpu_custom_call" | custom-call | tf_op jit(solution)/shard_map/pack/pallas_call | solution.py:385
  89.5 2.4 %total_hidden_grad.1 = bf16[64,3072]{1,0:T(8,128)(2,1)} custom-call(f32[64,3072]{1,0:T(8,128)} %get-tuple-element.65.a, bf16[64,3072]{1,0:T(8,128)(2,1)} %copy-done.15, bf16[64,3072]{1,0:T(8,128)(2,1)} %copy-done.16, bf16[64,3072]{1,0:T(8,128)(2,1)} %copy-done.17), custom_call_target="tpu_custom_call" | custom-call | tf_op jit(solution)/shard_map/total_hidden_grad/pallas_call | solution.py:204
  92.2 1.1 collective-permute-start.12
  94.0 4.1 %collective-permute-done.8.p1 = bf16[512,3072]{1,0:T(8,128)(2,1)S(1)} collective-permute-done((bf16[512,3072]{1,0:T(8,128)(2,1)}, bf16[512,3072]{1,0:T(8,128)(2,1)S(1)}, u32[]{:S(2)}, u32[]{:S(2)}) %collective-permute-start.8) | collective-permute-done | bytes 3145760 | tf_op jit(solution)/shard_map/ppermute | solution.py:50
  98.1 1.7 copy-done
  99.8 8.9 %grad_down_part.1.rest_2_ = bf16[7168,1024]{1,0:T(8,128)(2,1)} custom-call(bf16[512,3072]{1,0:T(8,128)(2,1)} %pack.2.p0, bf16[512,3072]{1,0:T(8,128)(2,1)} %copy-done, bf16[512,1024]{1,0:T(8,128)(2,1)} %get-tuple-element.71.x.y), custom_call_target="tpu_custom_call" | custom-call | tf_op jit(solution)/shard_map/grad_down_part/pallas_call | solution.py:234
  108.7 2.3 %collective-permute-done.12.b = bf16[64,4096]{1,0:T(8,128)(2,1)S(1)} collective-permute-done((bf16[64,4096]{1,0:T(8,128)(2,1)}, bf16[64,4096]{1,0:T(8,128)(2,1)S(1)}, u32[]{:S(2)}, u32[]{:S(2)}) %collective-permute-start.12) | collective-permute-done | bytes 524320 | tf_op jit(solution)/shard_map/ppermute | solution.py:50
  111.0 0.8 collective-permute-done.13.d
  112.6 3.0 %pair_sum.1 = (bf16[32,4096]{1,0:T(8,128)(2,1)}, bf16[32,4096]{1,0:T(8,128)(2,1)}, f32[64,4096]{1,0:T(8,128)}) custom-call(f32[64,4096]{1,0:T(8,128)} %get-tuple-element.72.a, bf16[64,4096]{1,0:T(8,128)(2,1)} %copy-done.11, f32[64,4096]{1,0:T(8,128)} %get-tuple-element.74.c, bf16[64,4096]{1,0:T(8,128)(2,1)} %copy-done.12), custom_call_target="tpu_custom_call" | custom-call | tf_op jit(solution)/shard_map/pair_sum/pallas_call | solution.py:177
  116.2 0.9 collective-permute-start.15
  117.1 2.5 %reorder.3 = (bf16[512,1024]{1,0:T(8,128)(2,1)}, bf16[256,1024]{1,0:T(8,128)(2,1)}) custom-call(s32[2]{0:T(128)} %pad_add_fusion.where_ref, bf16[512,1024]{1,0:T(8,128)(2,1)} %all-gather.7.cloned.1.call-done.x), custom_call_target="tpu_custom_call" | custom-call | tf_op jit(solution)/shard_map/reorder/pallas_call | solution.py:78
  119.5 9.8 %collective-permute-done.14.b = bf16[32,4096]{1,0:T(8,128)(2,1)S(1)} collective-permute-done((bf16[32,4096]{1,0:T(8,128)(2,1)}, bf16[32,4096]{1,0:T(8,128)(2,1)S(1)}, u32[]{:S(2)}, u32[]{:S(2)}) %collective-permute-start.14) | collective-permute-done | bytes 262176 | tf_op jit(solution)/shard_map/ppermute | solution.py:50
  129.3 0.9 collective-permute-done.15.c
  130.9 2.2 halves_sum.1
  133.2 1.1 collective-permute-start.17
  134.2 1.6 collective-permute-start.16
  135.8 22.2 %first_part.1 = (bf16[1024,7168]{1,0:T(8,128)(2,1)}, bf16[1024,7168]{1,0:T(8,128)(2,1)}, f32[512,1024]{1,0:T(8,128)}) custom-call(s32[2]{0:T(128)} %pad_add_fusion.where_ref, bf16[512,3072]{1,0:T(8,128)(2,1)} %all-gather.11.cloned.1.call-done.h, bf16[512,3072]{1,0:T(8,128)(2,1)} %pack.2.p0, bf16[512,3072]{1,0:T(8,128)(2,1)} %copy-done, ...), custom_call_target="tpu_custom_call" | custom-call | tf_op jit(solution)/shard_map/first_part/pallas_call | solution.py:279
  158.8 0.8 copy-done.10
  159.6 3.8 %pack.3.p0 = bf16[512,4096]{1,0:T(8,128)(2,1)} custom-call(bf16[128,4096]{1,0:T(8,128)(2,1)} %copy-done.1, bf16[128,4096]{1,0:T(8,128)(2,1)} %copy-done.4, bf16[128,4096]{1,0:T(8,128)(2,1)} %copy-done.3, bf16[64,4096]{1,0:T(8,128)(2,1)} %copy-done.10, bf16[64,4096]{1,0:T(8,128)(2,1)} %copy-done.9), custom_call_target="tpu_custom_call" | custom-call | tf_op jit(solution)/shard_map/pack/pallas_call | solution.py:385
  163.3 7.7 %collective-permute-done.18.p1 = bf16[512,4096]{1,0:T(8,128)(2,1)} collective-permute-done((bf16[512,4096]{1,0:T(8,128)(2,1)}, bf16[512,4096]{1,0:T(8,128)(2,1)}, u32[]{:S(2)}, u32[]{:S(2)}) %collective-permute-start.18) | collective-permute-done | bytes 4194336 | tf_op jit(solution)/shard_map/ppermute | solution.py:50
  171.0 1.9 all-gather.9.cloned.1.call-done.h
  172.9 18.2 %input_part.1 = (bf16[512,4096]{1,0:T(8,128)(2,1)}, bf16[512,4096]{1,0:T(8,128)(2,1)}, f32[128,1024]{1,0:T(8,128)}, bf16[128,1024]{1,0:T(8,128)(2,1)}, bf16[128,...) custom-call(s32[2]{0:T(128)} %pad_add_fusion.where_ref, bf16[512,4096]{1,0:T(8,128)(2,1)} %all-gather.9.cloned.1.call-done.h, ...), custom_call_target="tpu_custom_call" | custom-call | tf_op jit(solution)/shard_map/input_part/pallas_call | solution.py:329
  191.1 1.5 collective-permute-start.19
  192.6 2.4 %collective-permute-start.20 = (bf16[128,1024]{1,0:T(8,128)(2,1)}, bf16[128,1024]{1,0:T(8,128)(2,1)S(1)}, u32[]{:S(2)}, u32[]{:S(2)}) collective-permute-start(bf16[128,1024]{1,0:T(8,128)(2,1)} %get-tuple-element.98), channel_id=1, source_target_pairs={{0,16},{8,24},{16,0},{24,8},{1,17},{9,25},{17,1},{25,9},{2,18},{10... | collective-permute-start | bytes 786440 | tf_op jit(solution)/shard_map/ppermute | solution.py:54
  195.0 1.4 collective-permute-start.21
  196.5 19.9 %weight_part.1 = (bf16[1024,7168]{1,0:T(8,128)(2,1)}, bf16[1024,7168]{1,0:T(8,128)(2,1)}, bf16[7168,1024]{1,0:T(8,128)(2,1)}) custom-call(bf16[512,4096]{1,0:T(8,128)(2,1)} %get-tuple-element.91.a, bf16[512,4096]{1,0:T(8,128)(2,1)} %get-tuple-element.92.b, bf16[512,4096]{1,0:T(8,128)(2,1)} %pack.3.p0, ...), custom_call_target="tpu_custom_call", output_to_operand_aliasing={{0}: (6, {}), {1}: (7, {}), {2}: (8, {})} | custom-call | tf_op jit(solution)/shard_map/weight_part/pallas_call | solution.py:359
  217.9 2.1 sum_rows.1
  (81 shorter events, 9.5 us)
Async XLA Ops:
  7.2 7.5 %slice-start = ((bf16[64,7168]{1,0:T(8,128)(2,1)}), bf16[64,4096]{1,0:T(8,128)(2,1)S(1)}, s32[]{:S(2)}) async-start(bf16[64,7168]{1,0:T(8,128)(2,1)} %param.9), calls=%async_computation.4 | async-start | bytes 1048576 | tf_op jit(solution)/shard_map/slice | solution.py:412
  7.2 7.4 %slice-start.1 = ((bf16[64,7168]{1,0:T(8,128)(2,1)}), bf16[64,4096]{1,0:T(8,128)(2,1)S(1)}, s32[]{:S(2)}) async-start(bf16[64,7168]{1,0:T(8,128)(2,1)} %param.10), calls=%async_computation.5 | async-start | bytes 1048576 | tf_op jit(solution)/shard_map/slice | solution.py:412
  7.2 36.5 %all-gather.5.cloned.1.call-start = ((), (), s32[]{:S(2)}) async-start(), calls=%async_computation | async-start | bytes 1310720 | tf_op jit(solution)/shard_map/all_gather | solution.py:429
  7.2 36.5 %collective-permute-start.4 = (bf16[7168,1024]{1,0:T(8,128)(2,1)}, bf16[7168,1024]{1,0:T(8,128)(2,1)}, u32[]{:S(2)}, u32[]{:S(2)}) collective-permute-start(bf16[7168,1024]{1,0:T(8,128)(2,1)} %w.3), channel_id=1, source_target_pairs={{0,1},{1,0},{2,3},{3,2},{4,5},{5,4},{6,7},{7,6},{8,9},{9,8},{10,11... | collective-permute-start | bytes 44040200 | tf_op jit(solution)/shard_map/ppermute | solution.py:50
  7.9 109.1 %all-gather.7.cloned.1.call-start = ((), (), s32[]{:S(2)}) async-start(), calls=%async_computation.1 | async-start | bytes 1310720 | tf_op jit(solution)/shard_map/all_gather | solution.py:441
  10.1 50.3 %copy-start.2 = (bf16[128,3072]{1,0:T(8,128)(2,1)}, bf16[128,3072]{1,0:T(8,128)(2,1)S(1)}, u32[]{:S(2)}) copy-start(bf16[128,3072]{1,0:T(8,128)(2,1)S(1)} %pad_maximum_fusion.1.refs_0_) | copy-start | bytes 2359300
  10.1 20.6 %collective-permute-start.2 = (bf16[128,3072]{1,0:T(8,128)(2,1)S(1)}, bf16[128,3072]{1,0:T(8,128)(2,1)S(1)}, u32[]{:S(2)}, u32[]{:S(2)}) collective-permute-start(bf16[128,3072]{1,0:T(8,128)(2,1)S(1)} %pad_maximum_fusion.1.refs_0_), channel_id=1, source_target_pairs={{0,4},{1,5},{2,6},{3,7},{4,0},{5,1},{6,2},{7,3},{8,12},{9,13},{10,... | collective-permute-start | bytes 2359304 | tf_op jit(solution)/shard_map/ppermute | solution.py:50
  13.1 19.4 %collective-permute-start = (bf16[128,3072]{1,0:T(8,128)(2,1)S(1)}, bf16[128,3072]{1,0:T(8,128)(2,1)S(1)}, u32[]{:S(2)}, u32[]{:S(2)}) collective-permute-start(bf16[128,3072]{1,0:T(8,128)(2,1)S(1)} %pad_maximum_fusion.1.refs_0_), channel_id=1, source_target_pairs={{0,2},{1,3},{2,0},{3,1},{4,6},{5,7},{6,4},{7,5},{8,10},{9,11},{10,... | collective-permute-start | bytes 2359304 | tf_op jit(solution)/shard_map/ppermute | solution.py:50
  14.7 45.7 %copy-start.1 = (bf16[128,4096]{1,0:T(8,128)(2,1)}, bf16[128,4096]{1,0:T(8,128)(2,1)S(1)}, u32[]{:S(2)}) copy-start(bf16[128,4096]{1,0:T(8,128)(2,1)S(1)} %pad_maximum_fusion.refs_0_) | copy-start | bytes 3145732
  30.7 1.8 copy-start.7
  30.8 10.6 %collective-permute-start.3 = (bf16[64,3072]{1,0:T(8,128)(2,1)S(1)}, bf16[64,3072]{1,0:T(8,128)(2,1)S(1)}, u32[]{:S(2)}, u32[]{:S(2)}) collective-permute-start(bf16[64,3072]{1,0:T(8,128)(2,1)S(1)} %slice.29), channel_id=1, source_target_pairs={{0,2},{1,3},{2,0},{3,1},{4,6},{5,7},{6,4},{7,5},{8,10},{9,11},{10,... | collective-permute-start | bytes 1179656 | tf_op jit(solution)/shard_map/ppermute | solution.py:50
  32.6 1.0 copy-start.8
  33.6 10.1 %collective-permute-start.1 = (bf16[64,3072]{1,0:T(8,128)(2,1)}, bf16[64,3072]{1,0:T(8,128)(2,1)S(1)}, u32[]{:S(2)}, u32[]{:S(2)}) collective-permute-start(bf16[64,3072]{1,0:T(8,128)(2,1)} %slice.28), channel_id=1, source_target_pairs={{0,4},{1,5},{2,6},{3,7},{4,0},{5,1},{6,2},{7,3},{8,12},{9,13},{10,... | collective-permute-start | bytes 1179656 | tf_op jit(solution)/shard_map/ppermute | solution.py:50
  41.3 19.1 %copy-start.13 = (bf16[64,3072]{1,0:T(8,128)(2,1)}, bf16[64,3072]{1,0:T(8,128)(2,1)S(1)}, u32[]{:S(2)}) copy-start(bf16[64,3072]{1,0:T(8,128)(2,1)S(1)} %collective-permute-done.3.refs_4_) | copy-start | bytes 1179652
  43.7 2.7 %copy-start.14 = (bf16[64,3072]{1,0:T(8,128)(2,1)}, bf16[64,3072]{1,0:T(8,128)(2,1)S(1)}, u32[]{:S(2)}) copy-start(bf16[64,3072]{1,0:T(8,128)(2,1)S(1)} %collective-permute-done.1.refs_3_) | copy-start | bytes 1179652
  46.4 89.4 %all-gather.11.cloned.1.call-start = ((), (), s32[]{:S(2)}) async-start(), calls=%async_computation.3 | async-start | bytes 3538944 | tf_op jit(solution)/shard_map/all_gather | solution.py:451
  46.4 26.2 %collective-permute-start.7 = (bf16[128,4096]{1,0:T(8,128)(2,1)S(1)}, bf16[128,4096]{1,0:T(8,128)(2,1)S(1)}, u32[]{:S(2)}, u32[]{:S(2)}) collective-permute-start(bf16[128,4096]{1,0:T(8,128)(2,1)S(1)} %pad_maximum_fusion.refs_0_), channel_id=1, source_target_pairs={{0,4},{1,5},{2,6},{3,7},{4,0},{5,1},{6,2},{7,3},{8,12},{9,13},{10,... | collective-permute-start | bytes 3145736 | tf_op jit(solution)/shard_map/ppermute | solution.py:50
  48.0 26.1 %collective-permute-start.6 = (bf16[128,4096]{1,0:T(8,128)(2,1)S(1)}, bf16[128,4096]{1,0:T(8,128)(2,1)S(1)}, u32[]{:S(2)}, u32[]{:S(2)}) collective-permute-start(bf16[128,4096]{1,0:T(8,128)(2,1)S(1)} %pad_maximum_fusion.refs_0_), channel_id=1, source_target_pairs={{0,2},{1,3},{2,0},{3,1},{4,6},{5,7},{6,4},{7,5},{8,10},{9,11},{10,... | collective-permute-start | bytes 3145736 | tf_op jit(solution)/shard_map/ppermute | solution.py:50
  49.1 2.1 collective-permute-start.5
  51.2 0.8 copy-start.6
  60.4 27.4 %collective-permute-start.9 = (bf16[64,3072]{1,0:T(8,128)(2,1)}, bf16[64,3072]{1,0:T(8,128)(2,1)S(1)}, u32[]{:S(2)}, u32[]{:S(2)}) collective-permute-start(bf16[64,3072]{1,0:T(8,128)(2,1)} %get-tuple-element.66), channel_id=1, source_target_pairs={{0,2},{1,3},{2,0},{3,1},{4,6},{5,7},{6,4},{7,5},{8,10},{9,11},{10,... | collective-permute-start | bytes 1179656 | tf_op jit(solution)/shard_map/ppermute | solution.py:50
  61.5 26.4 %collective-permute-start.10 = (bf16[64,3072]{1,0:T(8,128)(2,1)}, bf16[64,3072]{1,0:T(8,128)(2,1)S(1)}, u32[]{:S(2)}, u32[]{:S(2)}) collective-permute-start(bf16[64,3072]{1,0:T(8,128)(2,1)} %get-tuple-element.67), channel_id=1, source_target_pairs={{0,4},{1,5},{2,6},{3,7},{4,0},{5,1},{6,2},{7,3},{8,12},{9,13},{10,... | collective-permute-start | bytes 1179656 | tf_op jit(solution)/shard_map/ppermute | solution.py:50
  62.2 25.7 %collective-permute-start.11 = (bf16[64,3072]{1,0:T(8,128)(2,1)}, bf16[64,3072]{1,0:T(8,128)(2,1)S(1)}, u32[]{:S(2)}, u32[]{:S(2)}) collective-permute-start(bf16[64,3072]{1,0:T(8,128)(2,1)} %get-tuple-element.68), channel_id=1, source_target_pairs={{0,6},{1,7},{2,4},{3,5},{4,2},{5,3},{6,0},{7,1},{8,14},{9,15},{10,... | collective-permute-start | bytes 1179656 | tf_op jit(solution)/shard_map/ppermute | solution.py:50
  72.6 21.4 %copy-start.3 = (bf16[128,4096]{1,0:T(8,128)(2,1)}, bf16[128,4096]{1,0:T(8,128)(2,1)S(1)}, u32[]{:S(2)}) copy-start(bf16[128,4096]{1,0:T(8,128)(2,1)S(1)} %collective-permute-done.7.refs_2_) | copy-start | bytes 3145732
  74.1 10.5 %copy-start.4 = (bf16[128,4096]{1,0:T(8,128)(2,1)}, bf16[128,4096]{1,0:T(8,128)(2,1)S(1)}, u32[]{:S(2)}) copy-start(bf16[128,4096]{1,0:T(8,128)(2,1)S(1)} %collective-permute-done.6.refs_1_) | copy-start | bytes 3145732
  84.6 9.4 %copy-start.5 = (bf16[128,4096]{1,0:T(8,128)(2,1)S(1)}, bf16[128,4096]{1,0:T(8,128)(2,1)}, u32[]{:S(2)}) copy-start(bf16[128,4096]{1,0:T(8,128)(2,1)} %copy-done.4) | copy-start | bytes 3145732
  87.9 0.8 copy-start.15
  87.9 0.9 copy-start.16
  88.8 0.7 copy-start.17
  91.9 81.0 %all-gather.9.cloned.1.call-start = ((), (), s32[]{:S(2)}) async-start(), calls=%async_computation.2 | async-start | bytes 4718592 | tf_op jit(solution)/shard_map/all_gather | solution.py:460
  92.1 5.9 %collective-permute-start.8 = (bf16[512,3072]{1,0:T(8,128)(2,1)}, bf16[512,3072]{1,0:T(8,128)(2,1)S(1)}, u32[]{:S(2)}, u32[]{:S(2)}) collective-permute-start(bf16[512,3072]{1,0:T(8,128)(2,1)} %pack.2.p0), channel_id=1, source_target_pairs={{0,1},{1,0},{2,3},{3,2},{4,5},{5,4},{6,7},{7,6},{8,9},{9,8},{10,11... | collective-permute-start | bytes 9437192 | tf_op jit(solution)/shard_map/ppermute | solution.py:50
  92.2 18.8 %collective-permute-start.12 = (bf16[64,4096]{1,0:T(8,128)(2,1)}, bf16[64,4096]{1,0:T(8,128)(2,1)S(1)}, u32[]{:S(2)}, u32[]{:S(2)}) collective-permute-start(bf16[64,4096]{1,0:T(8,128)(2,1)} %get-tuple-element.73), channel_id=1, source_target_pairs={{0,2},{1,3},{2,0},{3,1},{4,6},{5,7},{6,4},{7,5},{8,10},{9,11},{10,... | collective-permute-start | bytes 1572872 | tf_op jit(solution)/shard_map/ppermute | solution.py:50
  93.4 18.4 %collective-permute-start.13 = (bf16[64,4096]{1,0:T(8,128)(2,1)}, bf16[64,4096]{1,0:T(8,128)(2,1)S(1)}, u32[]{:S(2)}, u32[]{:S(2)}) collective-permute-start(bf16[64,4096]{1,0:T(8,128)(2,1)} %get-tuple-element.75), channel_id=1, source_target_pairs={{0,4},{1,5},{2,6},{3,7},{4,0},{5,1},{6,2},{7,3},{8,12},{9,13},{10,... | collective-permute-start | bytes 1572872 | tf_op jit(solution)/shard_map/ppermute | solution.py:50
  98.1 1.7 copy-start
  111.0 0.8 copy-start.11
  111.8 0.8 copy-start.12
  115.6 13.7 %collective-permute-start.14 = (bf16[32,4096]{1,0:T(8,128)(2,1)}, bf16[32,4096]{1,0:T(8,128)(2,1)S(1)}, u32[]{:S(2)}, u32[]{:S(2)}) collective-permute-start(bf16[32,4096]{1,0:T(8,128)(2,1)} %get-tuple-element.81), channel_id=1, source_target_pairs={{0,4},{1,5},{2,6},{3,7},{4,0},{5,1},{6,2},{7,3},{8,12},{9,13},{10,... | collective-permute-start | bytes 786440 | tf_op jit(solution)/shard_map/ppermute | solution.py:50
  116.2 14.0 %collective-permute-start.15 = (bf16[32,4096]{1,0:T(8,128)(2,1)}, bf16[32,4096]{1,0:T(8,128)(2,1)S(1)}, u32[]{:S(2)}, u32[]{:S(2)}) collective-permute-start(bf16[32,4096]{1,0:T(8,128)(2,1)} %get-tuple-element.82), channel_id=1, source_target_pairs={{0,2},{1,3},{2,0},{3,1},{4,6},{5,7},{6,4},{7,5},{8,10},{9,11},{10,... | collective-permute-start | bytes 786440 | tf_op jit(solution)/shard_map/ppermute | solution.py:50
  129.3 0.9 copy-start.21
  133.2 24.8 %collective-permute-start.17 = (bf16[64,4096]{1,0:T(8,128)(2,1)S(1)}, bf16[64,4096]{1,0:T(8,128)(2,1)S(1)}, u32[]{:S(2)}, u32[]{:S(2)}) collective-permute-start(bf16[64,4096]{1,0:T(8,128)(2,1)S(1)} %slice.31), channel_id=1, source_target_pairs={{0,2},{1,3},{2,0},{3,1},{4,6},{5,7},{6,4},{7,5},{8,10},{9,11},{10,... | collective-permute-start | bytes 1572872 | tf_op jit(solution)/shard_map/ppermute | solution.py:50
  134.2 23.8 %collective-permute-start.16 = (bf16[64,4096]{1,0:T(8,128)(2,1)S(1)}, bf16[64,4096]{1,0:T(8,128)(2,1)S(1)}, u32[]{:S(2)}, u32[]{:S(2)}) collective-permute-start(bf16[64,4096]{1,0:T(8,128)(2,1)S(1)} %slice.30), channel_id=1, source_target_pairs={{0,4},{1,5},{2,6},{3,7},{4,0},{5,1},{6,2},{7,3},{8,12},{9,13},{10,... | collective-permute-start | bytes 1572872 | tf_op jit(solution)/shard_map/ppermute | solution.py:50
  158.0 0.8 copy-start.9
  158.8 0.8 copy-start.10
  163.3 7.7 %collective-permute-start.18 = (bf16[512,4096]{1,0:T(8,128)(2,1)}, bf16[512,4096]{1,0:T(8,128)(2,1)}, u32[]{:S(2)}, u32[]{:S(2)}) collective-permute-start(bf16[512,4096]{1,0:T(8,128)(2,1)} %pack.3.p0), channel_id=1, source_target_pairs={{0,1},{1,0},{2,3},{3,2},{4,5},{5,4},{6,7},{7,6},{8,9},{9,8},{10,11... | collective-permute-start | bytes 12582920 | tf_op jit(solution)/shard_map/ppermute | solution.py:50
  191.1 25.3 %collective-permute-start.19 = (bf16[128,1024]{1,0:T(8,128)(2,1)}, bf16[128,1024]{1,0:T(8,128)(2,1)S(1)}, u32[]{:S(2)}, u32[]{:S(2)}) collective-permute-start(bf16[128,1024]{1,0:T(8,128)(2,1)} %get-tuple-element.97), channel_id=1, source_target_pairs={{0,8},{8,16},{16,24},{24,0},{1,9},{9,17},{17,25},{25,1},{2,10},{10... | collective-permute-start | bytes 786440 | tf_op jit(solution)/shard_map/ppermute | solution.py:54
  192.6 23.7 %collective-permute-start.20 = (bf16[128,1024]{1,0:T(8,128)(2,1)}, bf16[128,1024]{1,0:T(8,128)(2,1)S(1)}, u32[]{:S(2)}, u32[]{:S(2)}) collective-permute-start(bf16[128,1024]{1,0:T(8,128)(2,1)} %get-tuple-element.98), channel_id=1, source_target_pairs={{0,16},{8,24},{16,0},{24,8},{1,17},{9,25},{17,1},{25,9},{2,18},{10... | collective-permute-start | bytes 786440 | tf_op jit(solution)/shard_map/ppermute | solution.py:54
  195.0 21.3 %collective-permute-start.21 = (bf16[128,1024]{1,0:T(8,128)(2,1)}, bf16[128,1024]{1,0:T(8,128)(2,1)S(1)}, u32[]{:S(2)}, u32[]{:S(2)}) collective-permute-start(bf16[128,1024]{1,0:T(8,128)(2,1)} %get-tuple-element.99), channel_id=1, source_target_pairs={{0,24},{8,0},{16,8},{24,16},{1,25},{9,1},{17,9},{25,17},{2,26},{10... | collective-permute-start | bytes 786440 | tf_op jit(solution)/shard_map/ppermute | solution.py:54
  216.4 0.8 copy-start.19
  (3 other events, 2.1 us)
Sparse Core Ops, SparseCore 0:
  9.6 30.6 all-gather.4
  46.5 28.7 all-gather.6
  92.0 41.6 all-gather.10
  135.5 37.3 all-gather.8

commit v4 on v3

--- a/solution.py
+++ b/solution.py
@@ -451,12 +451,12 @@
     hidden0_all = lax.all_gather(hidden0, "col", axis=0, tiled=True)
     x1, y1 = after(x1, hidden0), after(y1, hidden0)
     over_y, over_x = x1[:part], y1[part:]
-    grad_down = down(0, None, (over_y, over_x))
-    far1 = [swap(over_y, 4), swap(over_x, 2)]
-    for_y, for_x, own1 = pair_sum(after(keep_x, grad_down), from_x, keep_y, from_y)
+    inputs_all, _ = reorder(where, after(inputs_all, (over_y, over_x)))
+    for_y, for_x, own1 = pair_sum(after(keep_x, inputs_all), from_x, keep_y, from_y)
     from_y, from_x = swap(for_y, 4), swap(for_x, 2)
-    inputs_all, _ = reorder(where, after(inputs_all, own1))
-    hidden1 = halves_sum(after(own1, inputs_all), from_y, from_x)
+    far1 = [swap(after(over_y, own1), 4), swap(after(over_x, own1), 2)]
+    grad_down = down(0, None, own1)
+    hidden1 = halves_sum(after(own1, grad_down), from_y, from_x)
     hidden1_all = lax.all_gather(hidden1, "col", axis=0, tiled=True)
     grad_gate, grad_up, total = first_part(
         where, hidden0_all, stored[0], after(inputs_all, hidden1), w_gate, w_up, cut, unit

time: 227 us -> 226 us (level)
  waiting for transfers between devices: 63.8 us -> 60 us
  local copies, waits for them, and re-layouts: 11.9 us -> 14.9 us
    ppermute x19, waiting for transfers between devices: 61.7 us -> 57.1 us  [swap(): return lax.ppermute(array, 'col', [(i, i ^ bit) for i in range(8)])]
    slice x2, local copies, waits for them, and re-layouts: 0.07 us -> 3.75 us  [on_square(): over_y, over_x = (x1[:part], y1[part:])]
    unnamed x46 -> x40, local copies, waits for them, and re-layouts: 8.97 us -> 9 us
  transfers between devices with their start and end apart: 26 -> 26, of which waited for: 13 -> 12; matrix products, arithmetic and copies ran while one was open for 2% -> 3% of each run, Pallas kernels for 38% -> 39%
where the time goes in v4:
time: 226 us; the launch traced here: 225 us
  Pallas kernels  110 us (49%)
  waiting for transfers between devices  60 us (27%)
  starting transfers between devices  25.8 us (11%)
  local copies, waits for them, and re-layouts  14.9 us (7%)
  between operations  14 us (6%)
    ppermute x19, waiting for transfers between devices, swap(): return lax.ppermute(array, 'col', [(i, i ^ bit) for i in range(8)])  57.1 us
    pallas_call x1, Pallas kernels, first_part(): pl.pallas_call(kernel, grid=(size // tile,), in_specs=[pl.BlockSpec(memor...  22.2 us
    ppermute x19, starting transfers between devices, swap(): return lax.ppermute(array, 'col', [(i, i ^ bit) for i in range(8)])  20 us
    pallas_call x1, Pallas kernels, weight_part(): pl.pallas_call(kernel, grid=(size // tile,), in_specs=[block] * 4 + [whol...  19.9 us
    pallas_call x1, Pallas kernels, input_part(): pl.pallas_call(kernel, grid=(steps,), in_specs=[pl.BlockSpec(memory_space...  18.2 us
    pallas_call x1, Pallas kernels, halved_hidden_grad(): pl.pallas_call(kernel, grid=(size // tile,), in_specs=[whole_block((token...  10.4 us
    unnamed x40, local copies, waits for them, and re-layouts  9 us
    pallas_call x1, Pallas kernels, grad_down_part(): pl.pallas_call(kernel, grid=(size // tile,), in_specs=[block] * 2 + [whol...  8.83 us
  transfers between devices with their start and end apart: 26, of which 12 were waited for; matrix products, arithmetic and copies ran while one was open for 3% of the time, Pallas kernels for 39%

profile of v4, /device:TPU:0, one launch (start us, length us, event | category | flops | bytes accessed | tf_op | source)
XLA Modules:
  0.0 225.0 jit_solution(494146286908065523)
XLA Ops:
  8.0 1.0 slice.24
  9.0 1.0 slice.25
  10.1 3.0 %collective-permute-start.2 = (bf16[128,3072]{1,0:T(8,128)(2,1)S(1)}, bf16[128,3072]{1,0:T(8,128)(2,1)S(1)}, u32[]{:S(2)}, u32[]{:S(2)}) collective-permute-start(bf16[128,3072]{1,0:T(8,128)(2,1)S(1)} %pad_maximum_fusion.1.refs_0_), channel_id=1, source_target_pairs={{0,4},{1,5},{2,6},{3,7},{4,0},{5,1},{6,2},{7,3},{8,12},{9,13},{10,... | collective-permute-start | bytes 2359304 | tf_op jit(solution)/shard_map/ppermute | solution.py:50
  13.1 1.5 collective-permute-start
  14.7 16.0 %collective-permute-done.2.refs_2_ = bf16[128,3072]{1,0:T(8,128)(2,1)S(1)} collective-permute-done((bf16[128,3072]{1,0:T(8,128)(2,1)S(1)}, bf16[128,3072]{1,0:T(8,128)(2,1)S(1)}, u32[]{:S(2)}, u32[]{:S(2)}) %collective-permute-start.2) | collective-permute-done | bytes 786464 | tf_op jit(solution)/shard_map/ppermute | solution.py:50
  30.8 1.8 collective-permute-start.3
  32.6 0.8 copy-done.7
  33.4 1.5 collective-permute-start.1
  35.6 5.8 %collective-permute-done.3.refs_4_ = bf16[64,3072]{1,0:T(8,128)(2,1)S(1)} collective-permute-done((bf16[64,3072]{1,0:T(8,128)(2,1)S(1)}, bf16[64,3072]{1,0:T(8,128)(2,1)S(1)}, u32[]{:S(2)}, u32[]{:S(2)}) %collective-permute-start.3) | collective-permute-done | bytes 393248 | tf_op jit(solution)/shard_map/ppermute | solution.py:50
  41.3 2.0 collective-permute-done.1.refs_3_
  43.3 2.6 %reorder.2 = (bf16[512,1024]{1,0:T(8,128)(2,1)}, bf16[256,1024]{1,0:T(8,128)(2,1)}) custom-call(s32[2]{0:T(128)} %pad_add_fusion.where_ref, bf16[512,1024]{1,0:T(8,128)(2,1)} %all-gather.5.cloned.1.call-done.x), custom_call_target="tpu_custom_call" | custom-call | tf_op jit(solution)/shard_map/reorder/pallas_call | solution.py:78
  46.0 1.6 collective-permute-start.7
  47.6 1.1 collective-permute-start.6
  48.7 2.1 collective-permute-done.5.y
  50.8 0.8 copy-done.5
  51.6 8.4 %partial_hidden_grad.1 = (f32[64,3072]{1,0:T(8,128)}, bf16[64,3072]{1,0:T(8,128)(2,1)}, bf16[64,3072]{1,0:T(8,128)(2,1)}, bf16[64,3072]{1,0:T(8,128)(2,1)}) custom-call(bf16[512,1024]{1,0:T(8,128)(2,1)} %get-tuple-element.81.x.y, bf16[256,1024]{1,0:T(8,128)(2,1)} %copy-done.5, bf16[7168,1024]{1,0:T(8,128)(2,1)} %w.3, bf16[7168,1024]{1,0:T(8,128)(2,1)} %collective-permute-done.4.v), custom_call_target="tpu_custom_call" | custom-call | tf_op jit(solution)/shard_map/partial_hidden_grad/pallas_call | solution.py:121
  60.1 1.1 collective-permute-start.8
  61.8 1.8 collective-permute-start.10
  63.6 8.6 %collective-permute-done.7.refs_2_ = bf16[128,4096]{1,0:T(8,128)(2,1)S(1)} collective-permute-done((bf16[128,4096]{1,0:T(8,128)(2,1)S(1)}, bf16[128,4096]{1,0:T(8,128)(2,1)S(1)}, u32[]{:S(2)}, u32[]{:S(2)}) %collective-permute-start.7) | collective-permute-done | bytes 1048608 | tf_op jit(solution)/shard_map/ppermute | solution.py:50
  72.2 1.5 collective-permute-done.6.refs_1_
  73.7 10.4 %halved_hidden_grad.1 = (bf16[64,4096]{1,0:T(8,128)(2,1)}, bf16[64,4096]{1,0:T(8,128)(2,1)}, f32[64,4096]{1,0:T(8,128)}, f32[64,4096]{1,0:T(8,128)}) custom-call(bf16[512,1024]{1,0:T(8,128)(2,1)} %get-tuple-element.81.x.y, bf16[256,1024]{1,0:T(8,128)(2,1)} %copy-done.5, bf16[7168,1024]{1,0:T(8,128)(2,1)} %w.3, bf16[7168,1024]{1,0:T(8,128)(2,1)} %collective-permute-done.4.v), custom_call_target="tpu_custom_call" | custom-call | tf_op jit(solution)/shard_map/halved_hidden_grad/pallas_call | solution.py:153
  84.2 3.2 %pack.2.p0 = bf16[512,3072]{1,0:T(8,128)(2,1)} custom-call(bf16[128,3072]{1,0:T(8,128)(2,1)} %copy-done.2, bf16[128,3072]{1,0:T(8,128)(2,1)} %copy-done.7, bf16[128,3072]{1,0:T(8,128)(2,1)} %copy-done.6, bf16[64,3072]{1,0:T(8,128)(2,1)} %copy-done.11, bf16[64,3072]{1,0:T(8,128)(2,1)} %copy-done.10), custom_call_target="tpu_custom_call" | custom-call | tf_op jit(solution)/shard_map/pack/pallas_call | solution.py:385
  89.1 2.4 %total_hidden_grad.1 = bf16[64,3072]{1,0:T(8,128)(2,1)} custom-call(f32[64,3072]{1,0:T(8,128)} %get-tuple-element.68.a, bf16[64,3072]{1,0:T(8,128)(2,1)} %copy-done.12, bf16[64,3072]{1,0:T(8,128)(2,1)} %copy-done.13, bf16[64,3072]{1,0:T(8,128)(2,1)} %copy-done.14), custom_call_target="tpu_custom_call" | custom-call | tf_op jit(solution)/shard_map/total_hidden_grad/pallas_call | solution.py:204
  91.8 1.1 collective-permute-start.11
  93.6 1.9 slice.30
  95.5 1.9 slice.31
  97.3 2.5 %reorder.3 = (bf16[512,1024]{1,0:T(8,128)(2,1)}, bf16[256,1024]{1,0:T(8,128)(2,1)}) custom-call(s32[2]{0:T(128)} %pad_add_fusion.where_ref, bf16[512,1024]{1,0:T(8,128)(2,1)} %all-gather.7.cloned.1.call-done.x), custom_call_target="tpu_custom_call" | custom-call | tf_op jit(solution)/shard_map/reorder/pallas_call | solution.py:78
  99.9 10.8 %collective-permute-done.11.b = bf16[64,4096]{1,0:T(8,128)(2,1)} collective-permute-done((bf16[64,4096]{1,0:T(8,128)(2,1)}, bf16[64,4096]{1,0:T(8,128)(2,1)}, u32[]{:S(2)}, u32[]{:S(2)}) %collective-permute-start.11) | collective-permute-done | bytes 524320 | tf_op jit(solution)/shard_map/ppermute | solution.py:50
  110.6 0.8 collective-permute-done.12.d
  111.4 3.0 %pair_sum.1 = (bf16[32,4096]{1,0:T(8,128)(2,1)}, bf16[32,4096]{1,0:T(8,128)(2,1)}, f32[64,4096]{1,0:T(8,128)}) custom-call(f32[64,4096]{1,0:T(8,128)} %get-tuple-element.76.a, bf16[64,4096]{1,0:T(8,128)(2,1)} %collective-permute-done.11.b, f32[64,4096]{1,0:T(8,128)} %get-tuple-element.78.c, bf16[64,4096]{1,0:T(8,128)(2,1)} %collective-permute-done.12.d), custom_call_target="tpu_custom_call" | custom-call | tf_op jit(solution)/shard_map/pair_sum/pallas_call | solution.py:177
  115.1 0.8 collective-permute-start.15
  115.9 1.7 copy-done
  117.7 8.8 %grad_down_part.1.rest_2_ = bf16[7168,1024]{1,0:T(8,128)(2,1)} custom-call(bf16[512,3072]{1,0:T(8,128)(2,1)} %pack.2.p0, bf16[512,3072]{1,0:T(8,128)(2,1)} %copy-done, bf16[512,1024]{1,0:T(8,128)(2,1)} %get-tuple-element.81.x.y), custom_call_target="tpu_custom_call" | custom-call | tf_op jit(solution)/shard_map/grad_down_part/pallas_call | solution.py:234
  126.5 1.3 collective-permute-done.14.b
  129.2 2.3 %halves_sum.1 = bf16[64,4096]{1,0:T(8,128)(2,1)} custom-call(f32[64,4096]{1,0:T(8,128)} %get-tuple-element.82.a, bf16[32,4096]{1,0:T(8,128)(2,1)} %copy-done.18, bf16[32,4096]{1,0:T(8,128)(2,1)} %copy-done.19), custom_call_target="tpu_custom_call" | custom-call | tf_op jit(solution)/shard_map/halves_sum/pallas_call | solution.py:192
  132.2 1.5 collective-permute-start.16
  133.7 22.2 %first_part.1 = (bf16[1024,7168]{1,0:T(8,128)(2,1)}, bf16[1024,7168]{1,0:T(8,128)(2,1)}, f32[512,1024]{1,0:T(8,128)}) custom-call(s32[2]{0:T(128)} %pad_add_fusion.where_ref, bf16[512,3072]{1,0:T(8,128)(2,1)} %all-gather.11.cloned.1.call-done.h, bf16[512,3072]{1,0:T(8,128)(2,1)} %pack.2.p0, bf16[512,3072]{1,0:T(8,128)(2,1)} %copy-done, ...), custom_call_target="tpu_custom_call" | custom-call | tf_op jit(solution)/shard_map/first_part/pallas_call | solution.py:279
  155.9 0.8 copy-done.8
  156.7 0.8 copy-done.9
  157.5 3.7 %pack.3.p0 = bf16[512,4096]{1,0:T(8,128)(2,1)} custom-call(bf16[128,4096]{1,0:T(8,128)(2,1)} %copy-done.1, bf16[128,4096]{1,0:T(8,128)(2,1)} %copy-done.4, bf16[128,4096]{1,0:T(8,128)(2,1)} %copy-done.3, bf16[64,4096]{1,0:T(8,128)(2,1)} %copy-done.9, bf16[64,4096]{1,0:T(8,128)(2,1)} %copy-done.8), custom_call_target="tpu_custom_call" | custom-call | tf_op jit(solution)/shard_map/pack/pallas_call | solution.py:385
  161.1 7.6 %collective-permute-done.18.p1 = bf16[512,4096]{1,0:T(8,128)(2,1)} collective-permute-done((bf16[512,4096]{1,0:T(8,128)(2,1)}, bf16[512,4096]{1,0:T(8,128)(2,1)}, u32[]{:S(2)}, u32[]{:S(2)}) %collective-permute-start.18) | collective-permute-done | bytes 4194336 | tf_op jit(solution)/shard_map/ppermute | solution.py:50
  168.8 2.7 %all-gather.9.cloned.1.call-done.h = bf16[512,4096]{1,0:T(8,128)(2,1)} async-done(((bf16[64,4096]{1,0:T(8,128)(2,1)}), bf16[512,4096]{1,0:T(8,128)(2,1)}) %all-gather.9.cloned.1.call-update) | async-done | bytes 4194320 | tf_op jit(solution)/shard_map/all_gather | solution.py:460
  171.4 18.2 %input_part.1 = (bf16[512,4096]{1,0:T(8,128)(2,1)}, bf16[512,4096]{1,0:T(8,128)(2,1)}, f32[128,1024]{1,0:T(8,128)}, bf16[128,1024]{1,0:T(8,128)(2,1)}, bf16[128,...) custom-call(s32[2]{0:T(128)} %pad_add_fusion.where_ref, bf16[512,4096]{1,0:T(8,128)(2,1)} %all-gather.9.cloned.1.call-done.h, ...), custom_call_target="tpu_custom_call" | custom-call | tf_op jit(solution)/shard_map/input_part/pallas_call | solution.py:329
  189.6 1.5 collective-permute-start.19
  191.2 2.4 %collective-permute-start.20 = (bf16[128,1024]{1,0:T(8,128)(2,1)}, bf16[128,1024]{1,0:T(8,128)(2,1)S(1)}, u32[]{:S(2)}, u32[]{:S(2)}) collective-permute-start(bf16[128,1024]{1,0:T(8,128)(2,1)} %get-tuple-element.102), channel_id=1, source_target_pairs={{0,16},{8,24},{16,0},{24,8},{1,17},{9,25},{17,1},{25,9},{2,18},{10... | collective-permute-start | bytes 786440 | tf_op jit(solution)/shard_map/ppermute | solution.py:54
  193.6 1.4 collective-permute-start.21
  195.0 19.9 %weight_part.1 = (bf16[1024,7168]{1,0:T(8,128)(2,1)}, bf16[1024,7168]{1,0:T(8,128)(2,1)}, bf16[7168,1024]{1,0:T(8,128)(2,1)}) custom-call(bf16[512,4096]{1,0:T(8,128)(2,1)} %get-tuple-element.95.a, bf16[512,4096]{1,0:T(8,128)(2,1)} %get-tuple-element.96.b, bf16[512,4096]{1,0:T(8,128)(2,1)} %pack.3.p0, ...), custom_call_target="tpu_custom_call", output_to_operand_aliasing={{0}: (6, {}), {1}: (7, {}), {2}: (8, {})} | custom-call | tf_op jit(solution)/shard_map/weight_part/pallas_call | solution.py:359
  216.4 2.1 sum_rows.1
  (75 shorter events, 9.2 us)
Async XLA Ops:
  7.2 7.5 %slice-start = ((bf16[64,7168]{1,0:T(8,128)(2,1)}), bf16[64,4096]{1,0:T(8,128)(2,1)S(1)}, s32[]{:S(2)}) async-start(bf16[64,7168]{1,0:T(8,128)(2,1)} %param.9), calls=%async_computation.4 | async-start | bytes 1048576 | tf_op jit(solution)/shard_map/slice | solution.py:412
  7.2 7.4 %slice-start.1 = ((bf16[64,7168]{1,0:T(8,128)(2,1)}), bf16[64,4096]{1,0:T(8,128)(2,1)S(1)}, s32[]{:S(2)}) async-start(bf16[64,7168]{1,0:T(8,128)(2,1)} %param.10), calls=%async_computation.5 | async-start | bytes 1048576 | tf_op jit(solution)/shard_map/slice | solution.py:412
  7.2 36.1 %all-gather.5.cloned.1.call-start = ((), (), s32[]{:S(2)}) async-start(), calls=%async_computation | async-start | bytes 1310720 | tf_op jit(solution)/shard_map/all_gather | solution.py:429
  7.2 36.1 %collective-permute-start.4 = (bf16[7168,1024]{1,0:T(8,128)(2,1)}, bf16[7168,1024]{1,0:T(8,128)(2,1)}, u32[]{:S(2)}, u32[]{:S(2)}) collective-permute-start(bf16[7168,1024]{1,0:T(8,128)(2,1)} %w.3), channel_id=1, source_target_pairs={{0,1},{1,0},{2,3},{3,2},{4,5},{5,4},{6,7},{7,6},{8,9},{9,8},{10,11... | collective-permute-start | bytes 44040200 | tf_op jit(solution)/shard_map/ppermute | solution.py:50
  7.9 89.4 %all-gather.7.cloned.1.call-start = ((), (), s32[]{:S(2)}) async-start(), calls=%async_computation.1 | async-start | bytes 1310720 | tf_op jit(solution)/shard_map/all_gather | solution.py:441
  10.1 49.9 %copy-start.2 = (bf16[128,3072]{1,0:T(8,128)(2,1)}, bf16[128,3072]{1,0:T(8,128)(2,1)S(1)}, u32[]{:S(2)}) copy-start(bf16[128,3072]{1,0:T(8,128)(2,1)S(1)} %pad_maximum_fusion.1.refs_0_) | copy-start | bytes 2359300
  10.1 20.6 %collective-permute-start.2 = (bf16[128,3072]{1,0:T(8,128)(2,1)S(1)}, bf16[128,3072]{1,0:T(8,128)(2,1)S(1)}, u32[]{:S(2)}, u32[]{:S(2)}) collective-permute-start(bf16[128,3072]{1,0:T(8,128)(2,1)S(1)} %pad_maximum_fusion.1.refs_0_), channel_id=1, source_target_pairs={{0,4},{1,5},{2,6},{3,7},{4,0},{5,1},{6,2},{7,3},{8,12},{9,13},{10,... | collective-permute-start | bytes 2359304 | tf_op jit(solution)/shard_map/ppermute | solution.py:50
  13.1 19.4 %collective-permute-start = (bf16[128,3072]{1,0:T(8,128)(2,1)S(1)}, bf16[128,3072]{1,0:T(8,128)(2,1)S(1)}, u32[]{:S(2)}, u32[]{:S(2)}) collective-permute-start(bf16[128,3072]{1,0:T(8,128)(2,1)S(1)} %pad_maximum_fusion.1.refs_0_), channel_id=1, source_target_pairs={{0,2},{1,3},{2,0},{3,1},{4,6},{5,7},{6,4},{7,5},{8,10},{9,11},{10,... | collective-permute-start | bytes 2359304 | tf_op jit(solution)/shard_map/ppermute | solution.py:50
  14.7 45.3 %copy-start.1 = (bf16[128,4096]{1,0:T(8,128)(2,1)}, bf16[128,4096]{1,0:T(8,128)(2,1)S(1)}, u32[]{:S(2)}) copy-start(bf16[128,4096]{1,0:T(8,128)(2,1)S(1)} %pad_maximum_fusion.refs_0_) | copy-start | bytes 3145732
  30.7 1.8 copy-start.6
  30.8 10.6 %collective-permute-start.3 = (bf16[64,3072]{1,0:T(8,128)(2,1)S(1)}, bf16[64,3072]{1,0:T(8,128)(2,1)S(1)}, u32[]{:S(2)}, u32[]{:S(2)}) collective-permute-start(bf16[64,3072]{1,0:T(8,128)(2,1)S(1)} %slice.29), channel_id=1, source_target_pairs={{0,2},{1,3},{2,0},{3,1},{4,6},{5,7},{6,4},{7,5},{8,10},{9,11},{10,... | collective-permute-start | bytes 1179656 | tf_op jit(solution)/shard_map/ppermute | solution.py:50
  32.6 0.9 copy-start.7
  33.4 9.9 %collective-permute-start.1 = (bf16[64,3072]{1,0:T(8,128)(2,1)S(1)}, bf16[64,3072]{1,0:T(8,128)(2,1)S(1)}, u32[]{:S(2)}, u32[]{:S(2)}) collective-permute-start(bf16[64,3072]{1,0:T(8,128)(2,1)S(1)} %slice.28), channel_id=1, source_target_pairs={{0,4},{1,5},{2,6},{3,7},{4,0},{5,1},{6,2},{7,3},{8,12},{9,13},{10,... | collective-permute-start | bytes 1179656 | tf_op jit(solution)/shard_map/ppermute | solution.py:50
  41.3 18.7 %copy-start.10 = (bf16[64,3072]{1,0:T(8,128)(2,1)}, bf16[64,3072]{1,0:T(8,128)(2,1)S(1)}, u32[]{:S(2)}) copy-start(bf16[64,3072]{1,0:T(8,128)(2,1)S(1)} %collective-permute-done.3.refs_4_) | copy-start | bytes 1179652
  43.3 16.7 %copy-start.11 = (bf16[64,3072]{1,0:T(8,128)(2,1)}, bf16[64,3072]{1,0:T(8,128)(2,1)S(1)}, u32[]{:S(2)}) copy-start(bf16[64,3072]{1,0:T(8,128)(2,1)S(1)} %collective-permute-done.1.refs_3_) | copy-start | bytes 1179652
  46.0 87.7 %all-gather.11.cloned.1.call-start = ((), (), s32[]{:S(2)}) async-start(), calls=%async_computation.3 | async-start | bytes 3538944 | tf_op jit(solution)/shard_map/all_gather | solution.py:451
  46.0 26.2 %collective-permute-start.7 = (bf16[128,4096]{1,0:T(8,128)(2,1)S(1)}, bf16[128,4096]{1,0:T(8,128)(2,1)S(1)}, u32[]{:S(2)}, u32[]{:S(2)}) collective-permute-start(bf16[128,4096]{1,0:T(8,128)(2,1)S(1)} %pad_maximum_fusion.refs_0_), channel_id=1, source_target_pairs={{0,4},{1,5},{2,6},{3,7},{4,0},{5,1},{6,2},{7,3},{8,12},{9,13},{10,... | collective-permute-start | bytes 3145736 | tf_op jit(solution)/shard_map/ppermute | solution.py:50
  47.6 26.1 %collective-permute-start.6 = (bf16[128,4096]{1,0:T(8,128)(2,1)S(1)}, bf16[128,4096]{1,0:T(8,128)(2,1)S(1)}, u32[]{:S(2)}, u32[]{:S(2)}) collective-permute-start(bf16[128,4096]{1,0:T(8,128)(2,1)S(1)} %pad_maximum_fusion.refs_0_), channel_id=1, source_target_pairs={{0,2},{1,3},{2,0},{3,1},{4,6},{5,7},{6,4},{7,5},{8,10},{9,11},{10,... | collective-permute-start | bytes 3145736 | tf_op jit(solution)/shard_map/ppermute | solution.py:50
  48.7 2.1 collective-permute-start.5
  50.8 0.8 copy-start.5
  60.1 27.3 %collective-permute-start.8 = (bf16[64,3072]{1,0:T(8,128)(2,1)}, bf16[64,3072]{1,0:T(8,128)(2,1)S(1)}, u32[]{:S(2)}, u32[]{:S(2)}) collective-permute-start(bf16[64,3072]{1,0:T(8,128)(2,1)} %get-tuple-element.69), channel_id=1, source_target_pairs={{0,2},{1,3},{2,0},{3,1},{4,6},{5,7},{6,4},{7,5},{8,10},{9,11},{10,... | collective-permute-start | bytes 1179656 | tf_op jit(solution)/shard_map/ppermute | solution.py:50
  61.1 26.3 %collective-permute-start.9 = (bf16[64,3072]{1,0:T(8,128)(2,1)}, bf16[64,3072]{1,0:T(8,128)(2,1)S(1)}, u32[]{:S(2)}, u32[]{:S(2)}) collective-permute-start(bf16[64,3072]{1,0:T(8,128)(2,1)} %get-tuple-element.70), channel_id=1, source_target_pairs={{0,4},{1,5},{2,6},{3,7},{4,0},{5,1},{6,2},{7,3},{8,12},{9,13},{10,... | collective-permute-start | bytes 1179656 | tf_op jit(solution)/shard_map/ppermute | solution.py:50
  61.8 25.6 %collective-permute-start.10 = (bf16[64,3072]{1,0:T(8,128)(2,1)}, bf16[64,3072]{1,0:T(8,128)(2,1)S(1)}, u32[]{:S(2)}, u32[]{:S(2)}) collective-permute-start(bf16[64,3072]{1,0:T(8,128)(2,1)} %get-tuple-element.71), channel_id=1, source_target_pairs={{0,6},{1,7},{2,4},{3,5},{4,2},{5,3},{6,0},{7,1},{8,14},{9,15},{10,... | collective-permute-start | bytes 1179656 | tf_op jit(solution)/shard_map/ppermute | solution.py:50
  72.2 12.0 %copy-start.3 = (bf16[128,4096]{1,0:T(8,128)(2,1)}, bf16[128,4096]{1,0:T(8,128)(2,1)S(1)}, u32[]{:S(2)}) copy-start(bf16[128,4096]{1,0:T(8,128)(2,1)S(1)} %collective-permute-done.7.refs_2_) | copy-start | bytes 3145732
  73.7 10.5 %copy-start.4 = (bf16[128,4096]{1,0:T(8,128)(2,1)}, bf16[128,4096]{1,0:T(8,128)(2,1)S(1)}, u32[]{:S(2)}) copy-start(bf16[128,4096]{1,0:T(8,128)(2,1)S(1)} %collective-permute-done.6.refs_1_) | copy-start | bytes 3145732
  87.4 0.7 copy-start.12
  87.4 0.9 copy-start.13
  88.3 0.8 copy-start.14
  91.5 80.0 %all-gather.9.cloned.1.call-start = ((), (), s32[]{:S(2)}) async-start(), calls=%async_computation.2 | async-start | bytes 4718592 | tf_op jit(solution)/shard_map/all_gather | solution.py:460
  91.7 24.2 %collective-permute-start.13 = (bf16[512,3072]{1,0:T(8,128)(2,1)}, bf16[512,3072]{1,0:T(8,128)(2,1)S(1)}, u32[]{:S(2)}, u32[]{:S(2)}) collective-permute-start(bf16[512,3072]{1,0:T(8,128)(2,1)} %pack.2.p0), channel_id=1, source_target_pairs={{0,1},{1,0},{2,3},{3,2},{4,5},{5,4},{6,7},{7,6},{8,9},{9,8},{10,11... | collective-permute-start | bytes 9437192 | tf_op jit(solution)/shard_map/ppermute | solution.py:50
  91.8 18.9 %collective-permute-start.11 = (bf16[64,4096]{1,0:T(8,128)(2,1)}, bf16[64,4096]{1,0:T(8,128)(2,1)}, u32[]{:S(2)}, u32[]{:S(2)}) collective-permute-start(bf16[64,4096]{1,0:T(8,128)(2,1)} %get-tuple-element.77), channel_id=1, source_target_pairs={{0,2},{1,3},{2,0},{3,1},{4,6},{5,7},{6,4},{7,5},{8,10},{9,11},{10,... | collective-permute-start | bytes 1572872 | tf_op jit(solution)/shard_map/ppermute | solution.py:50
  92.9 18.5 %collective-permute-start.12 = (bf16[64,4096]{1,0:T(8,128)(2,1)}, bf16[64,4096]{1,0:T(8,128)(2,1)}, u32[]{:S(2)}, u32[]{:S(2)}) collective-permute-start(bf16[64,4096]{1,0:T(8,128)(2,1)} %get-tuple-element.79), channel_id=1, source_target_pairs={{0,4},{1,5},{2,6},{3,7},{4,0},{5,1},{6,2},{7,3},{8,12},{9,13},{10,... | collective-permute-start | bytes 1572872 | tf_op jit(solution)/shard_map/ppermute | solution.py:50
  114.4 13.4 %collective-permute-start.14 = (bf16[32,4096]{1,0:T(8,128)(2,1)}, bf16[32,4096]{1,0:T(8,128)(2,1)S(1)}, u32[]{:S(2)}, u32[]{:S(2)}) collective-permute-start(bf16[32,4096]{1,0:T(8,128)(2,1)} %get-tuple-element.83), channel_id=1, source_target_pairs={{0,4},{1,5},{2,6},{3,7},{4,0},{5,1},{6,2},{7,3},{8,12},{9,13},{10,... | collective-permute-start | bytes 786440 | tf_op jit(solution)/shard_map/ppermute | solution.py:50
  115.1 13.2 %collective-permute-start.15 = (bf16[32,4096]{1,0:T(8,128)(2,1)}, bf16[32,4096]{1,0:T(8,128)(2,1)S(1)}, u32[]{:S(2)}, u32[]{:S(2)}) collective-permute-start(bf16[32,4096]{1,0:T(8,128)(2,1)} %get-tuple-element.84), channel_id=1, source_target_pairs={{0,2},{1,3},{2,0},{3,1},{4,6},{5,7},{6,4},{7,5},{8,10},{9,11},{10,... | collective-permute-start | bytes 786440 | tf_op jit(solution)/shard_map/ppermute | solution.py:50
  115.9 1.7 copy-start
  127.8 0.7 copy-start.18
  128.5 0.7 copy-start.19
  131.5 24.3 %collective-permute-start.17 = (bf16[64,4096]{1,0:T(8,128)(2,1)}, bf16[64,4096]{1,0:T(8,128)(2,1)S(1)}, u32[]{:S(2)}, u32[]{:S(2)}) collective-permute-start(bf16[64,4096]{1,0:T(8,128)(2,1)} %slice.31), channel_id=1, source_target_pairs={{0,2},{1,3},{2,0},{3,1},{4,6},{5,7},{6,4},{7,5},{8,10},{9,11},{10,... | collective-permute-start | bytes 1572872 | tf_op jit(solution)/shard_map/ppermute | solution.py:50
  132.2 23.7 %collective-permute-start.16 = (bf16[64,4096]{1,0:T(8,128)(2,1)}, bf16[64,4096]{1,0:T(8,128)(2,1)S(1)}, u32[]{:S(2)}, u32[]{:S(2)}) collective-permute-start(bf16[64,4096]{1,0:T(8,128)(2,1)} %slice.30), channel_id=1, source_target_pairs={{0,4},{1,5},{2,6},{3,7},{4,0},{5,1},{6,2},{7,3},{8,12},{9,13},{10,... | collective-permute-start | bytes 1572872 | tf_op jit(solution)/shard_map/ppermute | solution.py:50
  155.9 0.8 copy-start.8
  156.7 0.8 copy-start.9
  161.1 7.7 %collective-permute-start.18 = (bf16[512,4096]{1,0:T(8,128)(2,1)}, bf16[512,4096]{1,0:T(8,128)(2,1)}, u32[]{:S(2)}, u32[]{:S(2)}) collective-permute-start(bf16[512,4096]{1,0:T(8,128)(2,1)} %pack.3.p0), channel_id=1, source_target_pairs={{0,1},{1,0},{2,3},{3,2},{4,5},{5,4},{6,7},{7,6},{8,9},{9,8},{10,11... | collective-permute-start | bytes 12582920 | tf_op jit(solution)/shard_map/ppermute | solution.py:50
  189.6 25.3 %collective-permute-start.19 = (bf16[128,1024]{1,0:T(8,128)(2,1)}, bf16[128,1024]{1,0:T(8,128)(2,1)S(1)}, u32[]{:S(2)}, u32[]{:S(2)}) collective-permute-start(bf16[128,1024]{1,0:T(8,128)(2,1)} %get-tuple-element.101), channel_id=1, source_target_pairs={{0,8},{8,16},{16,24},{24,0},{1,9},{9,17},{17,25},{25,1},{2,10},{10... | collective-permute-start | bytes 786440 | tf_op jit(solution)/shard_map/ppermute | solution.py:54
  191.2 23.7 %collective-permute-start.20 = (bf16[128,1024]{1,0:T(8,128)(2,1)}, bf16[128,1024]{1,0:T(8,128)(2,1)S(1)}, u32[]{:S(2)}, u32[]{:S(2)}) collective-permute-start(bf16[128,1024]{1,0:T(8,128)(2,1)} %get-tuple-element.102), channel_id=1, source_target_pairs={{0,16},{8,24},{16,0},{24,8},{1,17},{9,25},{17,1},{25,9},{2,18},{10... | collective-permute-start | bytes 786440 | tf_op jit(solution)/shard_map/ppermute | solution.py:54
  193.6 21.3 %collective-permute-start.21 = (bf16[128,1024]{1,0:T(8,128)(2,1)}, bf16[128,1024]{1,0:T(8,128)(2,1)S(1)}, u32[]{:S(2)}, u32[]{:S(2)}) collective-permute-start(bf16[128,1024]{1,0:T(8,128)(2,1)} %get-tuple-element.103), channel_id=1, source_target_pairs={{0,24},{8,0},{16,8},{24,16},{1,25},{9,1},{17,9},{25,17},{2,26},{10... | collective-permute-start | bytes 786440 | tf_op jit(solution)/shard_map/ppermute | solution.py:54
  214.9 0.7 copy-start.15
  214.9 0.8 copy-start.16
  215.7 0.7 copy-start.17
Sparse Core Ops, SparseCore 0:
  9.6 30.6 all-gather.4
  46.1 28.7 all-gather.6
  91.6 40.9 all-gather.10
  134.3 37.1 all-gather.8

commit v5 on v4

--- a/solution.py
+++ b/solution.py
@@ -89,19 +89,10 @@
 
 
 def sum_rows(blocks):
-    def kernel(own, *refs):
-        *ins, out = refs
-        total = own[...]
-        for ref in ins:
-            total = total + ref[...].astype(F32)
-        out[...] = total.astype(BF16)
-
-    return pl.pallas_call(
-        kernel,
-        out_shape=jax.ShapeDtypeStruct(blocks[0].shape, BF16),
-        compiler_params=params(),
-        name="sum_rows",
-    )(*blocks)
+    total = blocks[0]
+    for block in blocks[1:]:
+        total = total + block.astype(F32)
+    return total.astype(BF16)
 
 
 def partial_hidden_grad(here, there, w_here, w_there, start, size, tile):
@@ -198,15 +189,7 @@
 
 
 def total_hidden_grad(own, *received):
-    def kernel(a, b, c, d, out):
-        out[...] = (a[...] + b[...].astype(F32) + c[...].astype(F32) + d[...].astype(F32)).astype(BF16)
-
-    return pl.pallas_call(
-        kernel,
-        out_shape=jax.ShapeDtypeStruct(own.shape, BF16),
-        compiler_params=params(),
-        name="total_hidden_grad",
-    )(own, *received)
+    return sum_rows([own, *received])
 
 
 def spread_whole(block, over_x_first):
@@ -468,7 +451,7 @@
     sums = [sums[0]] + [onward(block, rows, ahead) for ahead, block in enumerate(sums) if ahead]
     earlier = (grad_gate, grad_up, grad_down)
     grad_gate, grad_up, grad_down = weight_part(
-        gate_grad, up_grad, stored[1], inputs_all, grad_out_all, earlier, cut, unit
+        gate_grad, up_grad, stored[1], inputs_all, grad_out_all, earlier, cut, unit // 2
     )
     grad_inputs = sum_rows([after(sums[0], grad_up)] + sums[1:])
     return grad_inputs, grad_gate, grad_up, grad_down

time: 226 us -> 217 us (0.960)
  Pallas kernels: 110 us -> 105 us
  waiting for transfers between devices: 60 us -> 55.8 us
  local copies, waits for them, and re-layouts: 14.9 us -> 12.3 us
    pallas_call x2 -> x0, Pallas kernels: 4.46 us -> none  [the longest x1 2.38 us: total_hidden_grad(): pl.pallas_call(kernel, out_shape=jax.ShapeDtypeStruct(own.shape, BF16), c...]
    ppermute x19, waiting for transfers between devices: 57.1 us -> 52.9 us  [swap(): return lax.ppermute(array, 'col', [(i, i ^ bit) for i in range(8)])]
    unnamed x40 -> x28, local copies, waits for them, and re-layouts: 9 us -> 4.85 us
  transfers between devices with their start and end apart: 26 -> 26, of which waited for: 12 -> 11; matrix products, arithmetic and copies ran while one was open for 3% -> 4% of each run, Pallas kernels for 39% -> 40%
where the time goes in v5:
time: 217 us; the launch traced here: 215 us
  Pallas kernels  105 us (48%)
  waiting for transfers between devices  55.8 us (26%)
  starting transfers between devices  26 us (12%)
  between operations  13.9 us (6%)
  local copies, waits for them, and re-layouts  12.3 us (6%)
  other arithmetic  2.5 us (1%)
    ppermute x19, waiting for transfers between devices, swap(): return lax.ppermute(array, 'col', [(i, i ^ bit) for i in range(8)])  52.9 us
    pallas_call x1, Pallas kernels, first_part(): pl.pallas_call(kernel, grid=(size // tile,), in_specs=[pl.BlockSpec(memor...  22.1 us
    ppermute x19, starting transfers between devices, swap(): return lax.ppermute(array, 'col', [(i, i ^ bit) for i in range(8)])  20.3 us
    pallas_call x1, Pallas kernels, weight_part(): pl.pallas_call(kernel, grid=(size // tile,), in_specs=[block] * 4 + [whol...  19.1 us
    pallas_call x1, Pallas kernels, input_part(): pl.pallas_call(kernel, grid=(steps,), in_specs=[pl.BlockSpec(memory_space...  18.3 us
    pallas_call x1, Pallas kernels, halved_hidden_grad(): pl.pallas_call(kernel, grid=(size // tile,), in_specs=[whole_block((token...  10.4 us
    pallas_call x1, Pallas kernels, grad_down_part(): pl.pallas_call(kernel, grid=(size // tile,), in_specs=[block] * 2 + [whol...  8.85 us
    pallas_call x1, Pallas kernels, partial_hidden_grad(): pl.pallas_call(kernel, grid=(size // tile,), in_specs=[whole_block((token...  8.63 us
  transfers between devices with their start and end apart: 26, of which 11 were waited for; matrix products, arithmetic and copies ran while one was open for 4% of the time, Pallas kernels for 40%

profile of v5, /device:TPU:0, one launch (start us, length us, event | category | flops | bytes accessed | tf_op | source)
XLA Modules:
  0.0 215.2 jit_solution(9029972932689154845)
XLA Ops:
  8.0 1.0 slice.24
  9.0 1.0 slice.25
  10.1 3.0 %collective-permute-start.2 = (bf16[128,3072]{1,0:T(8,128)(2,1)S(1)}, bf16[128,3072]{1,0:T(8,128)(2,1)S(1)}, u32[]{:S(2)}, u32[]{:S(2)}) collective-permute-start(bf16[128,3072]{1,0:T(8,128)(2,1)S(1)} %pad_maximum_fusion.1.refs_0_), channel_id=1, source_target_pairs={{0,4},{1,5},{2,6},{3,7},{4,0},{5,1},{6,2},{7,3},{8,12},{9,13},{10,... | collective-permute-start | bytes 2359304 | tf_op jit(solution)/shard_map/ppermute | solution.py:50
  13.1 1.5 collective-permute-start
  14.7 16.0 %collective-permute-done.2.refs_2_ = bf16[128,3072]{1,0:T(8,128)(2,1)S(1)} collective-permute-done((bf16[128,3072]{1,0:T(8,128)(2,1)S(1)}, bf16[128,3072]{1,0:T(8,128)(2,1)S(1)}, u32[]{:S(2)}, u32[]{:S(2)}) %collective-permute-start.2) | collective-permute-done | bytes 786464 | tf_op jit(solution)/shard_map/ppermute | solution.py:50
  30.7 0.8 slice.29
  31.6 1.7 collective-permute-start.3
  33.3 0.8 slice.28
  34.1 1.5 collective-permute-start.1
  37.2 6.7 %collective-permute-done.3.refs_4_ = bf16[64,3072]{1,0:T(8,128)(2,1)S(1)} collective-permute-done((bf16[64,3072]{1,0:T(8,128)(2,1)}, bf16[64,3072]{1,0:T(8,128)(2,1)S(1)}, u32[]{:S(2)}, u32[]{:S(2)}) %collective-permute-start.3) | collective-permute-done | bytes 393248 | tf_op jit(solution)/shard_map/ppermute | solution.py:50
  43.8 2.7 %collective-permute-done.1.refs_3_ = bf16[64,3072]{1,0:T(8,128)(2,1)} collective-permute-done((bf16[64,3072]{1,0:T(8,128)(2,1)}, bf16[64,3072]{1,0:T(8,128)(2,1)}, u32[]{:S(2)}, u32[]{:S(2)}) %collective-permute-start.1) | collective-permute-done | bytes 393248 | tf_op jit(solution)/shard_map/ppermute | solution.py:50
  46.5 2.5 %reorder.2 = (bf16[512,1024]{1,0:T(8,128)(2,1)}, bf16[256,1024]{1,0:T(8,128)(2,1)}) custom-call(s32[2]{0:T(128)} %pad_add_fusion.where_ref, bf16[512,1024]{1,0:T(8,128)(2,1)} %all-gather.5.cloned.1.call-done.x), custom_call_target="tpu_custom_call" | custom-call | tf_op jit(solution)/shard_map/reorder/pallas_call | solution.py:78
  49.1 2.0 collective-permute-done.5.y
  51.1 0.8 copy-done.4
  51.9 8.6 %partial_hidden_grad.1 = (f32[64,3072]{1,0:T(8,128)}, bf16[64,3072]{1,0:T(8,128)(2,1)}, bf16[64,3072]{1,0:T(8,128)(2,1)}, bf16[64,3072]{1,0:T(8,128)(2,1)}) custom-call(bf16[512,1024]{1,0:T(8,128)(2,1)} %get-tuple-element.81.x.y, bf16[256,1024]{1,0:T(8,128)(2,1)} %copy-done.4, bf16[7168,1024]{1,0:T(8,128)(2,1)} %w.3, bf16[7168,1024]{1,0:T(8,128)(2,1)} %collective-permute-done.4.v), custom_call_target="tpu_custom_call" | custom-call | tf_op jit(solution)/shard_map/partial_hidden_grad/pallas_call | solution.py:112
  60.9 1.7 collective-permute-start.9
  62.6 1.5 collective-permute-start.10
  64.1 4.7 %collective-permute-done.7.refs_2_ = bf16[128,4096]{1,0:T(8,128)(2,1)S(1)} collective-permute-done((bf16[128,4096]{1,0:T(8,128)(2,1)S(1)}, bf16[128,4096]{1,0:T(8,128)(2,1)S(1)}, u32[]{:S(2)}, u32[]{:S(2)}) %collective-permute-start.7) | collective-permute-done | bytes 1048608 | tf_op jit(solution)/shard_map/ppermute | solution.py:50
  68.9 10.4 %halved_hidden_grad.1 = (bf16[64,4096]{1,0:T(8,128)(2,1)}, bf16[64,4096]{1,0:T(8,128)(2,1)}, f32[64,4096]{1,0:T(8,128)}, f32[64,4096]{1,0:T(8,128)}) custom-call(bf16[512,1024]{1,0:T(8,128)(2,1)} %get-tuple-element.81.x.y, bf16[256,1024]{1,0:T(8,128)(2,1)} %copy-done.4, bf16[7168,1024]{1,0:T(8,128)(2,1)} %w.3, bf16[7168,1024]{1,0:T(8,128)(2,1)} %collective-permute-done.4.v), custom_call_target="tpu_custom_call" | custom-call | tf_op jit(solution)/shard_map/halved_hidden_grad/pallas_call | solution.py:144
  79.3 3.2 %pack.2.p0 = bf16[512,3072]{1,0:T(8,128)(2,1)} custom-call(bf16[128,3072]{1,0:T(8,128)(2,1)} %copy-done.2, bf16[128,3072]{1,0:T(8,128)(2,1)} %copy-done.6, bf16[128,3072]{1,0:T(8,128)(2,1)} %copy-done.5, bf16[64,3072]{1,0:T(8,128)(2,1)} %collective-permute-done.1.refs_3_, bf16[64,3072]{1,0:T(8,128)(2,1)} %copy-done.11), custom_call_target="tpu_custom_call" | custom-call | tf_op jit(solution)/shard_map/pack/pallas_call | solution.py:368
  82.6 1.0 collective-permute-done.9
  83.5 0.9 add_convert_fusion
  84.8 0.7 collective-permute-start.11
  85.5 1.4 collective-permute-start.12
  86.9 1.9 slice.30
  88.8 1.9 slice.31
  90.7 2.5 %reorder.3 = (bf16[512,1024]{1,0:T(8,128)(2,1)}, bf16[256,1024]{1,0:T(8,128)(2,1)}) custom-call(s32[2]{0:T(128)} %pad_add_fusion.where_ref, bf16[512,1024]{1,0:T(8,128)(2,1)} %all-gather.7.cloned.1.call-done.x), custom_call_target="tpu_custom_call" | custom-call | tf_op jit(solution)/shard_map/reorder/pallas_call | solution.py:78
  93.2 10.5 %collective-permute-done.11.b = bf16[64,4096]{1,0:T(8,128)(2,1)} collective-permute-done((bf16[64,4096]{1,0:T(8,128)(2,1)}, bf16[64,4096]{1,0:T(8,128)(2,1)}, u32[]{:S(2)}, u32[]{:S(2)}) %collective-permute-start.11) | collective-permute-done | bytes 524320 | tf_op jit(solution)/shard_map/ppermute | solution.py:50
  104.0 3.0 %pair_sum.1 = (bf16[32,4096]{1,0:T(8,128)(2,1)}, bf16[32,4096]{1,0:T(8,128)(2,1)}, f32[64,4096]{1,0:T(8,128)}) custom-call(f32[64,4096]{1,0:T(8,128)} %get-tuple-element.76.a, bf16[64,4096]{1,0:T(8,128)(2,1)} %collective-permute-done.11.b, f32[64,4096]{1,0:T(8,128)} %get-tuple-element.78.c, bf16[64,4096]{1,0:T(8,128)(2,1)} %collective-permute-done.12.d), custom_call_target="tpu_custom_call" | custom-call | tf_op jit(solution)/shard_map/pair_sum/pallas_call | solution.py:168
  107.0 1.4 collective-permute-start.14
  108.5 1.5 collective-permute-start.15
  109.9 1.7 copy-done
  111.7 8.8 %grad_down_part.1.rest_2_ = bf16[7168,1024]{1,0:T(8,128)(2,1)} custom-call(bf16[512,3072]{1,0:T(8,128)(2,1)} %pack.2.p0, bf16[512,3072]{1,0:T(8,128)(2,1)} %copy-done, bf16[512,1024]{1,0:T(8,128)(2,1)} %get-tuple-element.81.x.y), custom_call_target="tpu_custom_call" | custom-call | tf_op jit(solution)/shard_map/grad_down_part/pallas_call | solution.py:217
  120.5 1.3 collective-permute-done.15.c
  122.6 2.3 %halves_sum.1 = bf16[64,4096]{1,0:T(8,128)(2,1)} custom-call(f32[64,4096]{1,0:T(8,128)} %get-tuple-element.82.a, bf16[32,4096]{1,0:T(8,128)(2,1)} %copy-done.12, bf16[32,4096]{1,0:T(8,128)(2,1)} %copy-done.13), custom_call_target="tpu_custom_call" | custom-call | tf_op jit(solution)/shard_map/halves_sum/pallas_call | solution.py:183
  124.9 2.4 %collective-permute-start.17 = (bf16[64,4096]{1,0:T(8,128)(2,1)}, bf16[64,4096]{1,0:T(8,128)(2,1)S(1)}, u32[]{:S(2)}, u32[]{:S(2)}) collective-permute-start(bf16[64,4096]{1,0:T(8,128)(2,1)} %slice.31), channel_id=1, source_target_pairs={{0,2},{1,3},{2,0},{3,1},{4,6},{5,7},{6,4},{7,5},{8,10},{9,11},{10,... | collective-permute-start | bytes 1572872 | tf_op jit(solution)/shard_map/ppermute | solution.py:50
  127.3 22.1 %first_part.1 = (bf16[1024,7168]{1,0:T(8,128)(2,1)}, bf16[1024,7168]{1,0:T(8,128)(2,1)}, f32[512,1024]{1,0:T(8,128)}) custom-call(s32[2]{0:T(128)} %pad_add_fusion.where_ref, bf16[512,3072]{1,0:T(8,128)(2,1)} %all-gather.11.cloned.1.call-done.h, bf16[512,3072]{1,0:T(8,128)(2,1)} %pack.2.p0, bf16[512,3072]{1,0:T(8,128)(2,1)} %copy-done, ...), custom_call_target="tpu_custom_call" | custom-call | tf_op jit(solution)/shard_map/first_part/pallas_call | solution.py:262
  149.5 0.8 copy-done.9
  150.2 0.8 copy-done.10
  151.0 3.6 %pack.3.p0 = bf16[512,4096]{1,0:T(8,128)(2,1)} custom-call(bf16[128,4096]{1,0:T(8,128)(2,1)} %copy-done.1, bf16[128,4096]{1,0:T(8,128)(2,1)} %collective-permute-done.6.refs_1_, bf16[128,4096]{1,0:T(8,128)(2,1)} %copy-done.3, bf16[64,4096]{1,0:T(8,128)(2,1)} %copy-done.10, bf16[64,4096]{1,0:T(8,128)(2,1)} %copy-done.9), custom_call_target="tpu_custom_call" | custom-call | tf_op jit(solution)/shard_map/pack/pallas_call | solution.py:368
  154.7 7.6 %collective-permute-done.18.p1 = bf16[512,4096]{1,0:T(8,128)(2,1)} collective-permute-done((bf16[512,4096]{1,0:T(8,128)(2,1)}, bf16[512,4096]{1,0:T(8,128)(2,1)}, u32[]{:S(2)}, u32[]{:S(2)}) %collective-permute-start.18) | collective-permute-done | bytes 4194336 | tf_op jit(solution)/shard_map/ppermute | solution.py:50
  162.3 2.7 %all-gather.9.cloned.1.call-done.h = bf16[512,4096]{1,0:T(8,128)(2,1)} async-done(((bf16[64,4096]{1,0:T(8,128)(2,1)}), bf16[512,4096]{1,0:T(8,128)(2,1)}) %all-gather.9.cloned.1.call-update) | async-done | bytes 4194320 | tf_op jit(solution)/shard_map/all_gather | solution.py:443
  165.0 18.3 %input_part.1 = (bf16[512,4096]{1,0:T(8,128)(2,1)}, bf16[512,4096]{1,0:T(8,128)(2,1)}, f32[128,1024]{1,0:T(8,128)}, bf16[128,1024]{1,0:T(8,128)(2,1)}, bf16[128,...) custom-call(s32[2]{0:T(128)} %pad_add_fusion.where_ref, bf16[512,4096]{1,0:T(8,128)(2,1)} %all-gather.9.cloned.1.call-done.h, ...), custom_call_target="tpu_custom_call" | custom-call | tf_op jit(solution)/shard_map/input_part/pallas_call | solution.py:312
  183.3 1.5 collective-permute-start.19
  184.8 2.4 %collective-permute-start.20 = (bf16[128,1024]{1,0:T(8,128)(2,1)}, bf16[128,1024]{1,0:T(8,128)(2,1)S(1)}, u32[]{:S(2)}, u32[]{:S(2)}) collective-permute-start(bf16[128,1024]{1,0:T(8,128)(2,1)} %get-tuple-element.102), channel_id=1, source_target_pairs={{0,16},{8,24},{16,0},{24,8},{1,17},{9,25},{17,1},{25,9},{2,18},{10... | collective-permute-start | bytes 786440 | tf_op jit(solution)/shard_map/ppermute | solution.py:54
  187.2 1.4 collective-permute-start.21
  188.7 19.1 %weight_part.1 = (bf16[1024,7168]{1,0:T(8,128)(2,1)}, bf16[1024,7168]{1,0:T(8,128)(2,1)}, bf16[7168,1024]{1,0:T(8,128)(2,1)}) custom-call(bf16[512,4096]{1,0:T(8,128)(2,1)} %get-tuple-element.95.a, bf16[512,4096]{1,0:T(8,128)(2,1)} %get-tuple-element.96.b, bf16[512,4096]{1,0:T(8,128)(2,1)} %pack.3.p0, ...), custom_call_target="tpu_custom_call", output_to_operand_aliasing={{0}: (6, {}), {1}: (7, {}), {2}: (8, {})} | custom-call | tf_op jit(solution)/shard_map/weight_part/pallas_call | solution.py:342
  207.9 0.8 add_convert_fusion.1
  (63 shorter events, 4.3 us)
Async XLA Ops:
  7.2 7.5 %slice-start = ((bf16[64,7168]{1,0:T(8,128)(2,1)}), bf16[64,4096]{1,0:T(8,128)(2,1)S(1)}, s32[]{:S(2)}) async-start(bf16[64,7168]{1,0:T(8,128)(2,1)} %param.9), calls=%async_computation.4 | async-start | bytes 1048576 | tf_op jit(solution)/shard_map/slice | solution.py:395
  7.2 7.4 %slice-start.1 = ((bf16[64,7168]{1,0:T(8,128)(2,1)}), bf16[64,4096]{1,0:T(8,128)(2,1)S(1)}, s32[]{:S(2)}) async-start(bf16[64,7168]{1,0:T(8,128)(2,1)} %param.10), calls=%async_computation.5 | async-start | bytes 1048576 | tf_op jit(solution)/shard_map/slice | solution.py:395
  7.2 39.3 %all-gather.5.cloned.1.call-start = ((), (), s32[]{:S(2)}) async-start(), calls=%async_computation | async-start | bytes 1310720 | tf_op jit(solution)/shard_map/all_gather | solution.py:412
  7.2 39.3 %collective-permute-start.4 = (bf16[7168,1024]{1,0:T(8,128)(2,1)}, bf16[7168,1024]{1,0:T(8,128)(2,1)}, u32[]{:S(2)}, u32[]{:S(2)}) collective-permute-start(bf16[7168,1024]{1,0:T(8,128)(2,1)} %w.3), channel_id=1, source_target_pairs={{0,1},{1,0},{2,3},{3,2},{4,5},{5,4},{6,7},{7,6},{8,9},{9,8},{10,11... | collective-permute-start | bytes 44040200 | tf_op jit(solution)/shard_map/ppermute | solution.py:50
  7.9 82.7 %all-gather.7.cloned.1.call-start = ((), (), s32[]{:S(2)}) async-start(), calls=%async_computation.1 | async-start | bytes 1310720 | tf_op jit(solution)/shard_map/all_gather | solution.py:424
  10.1 50.5 %copy-start.2 = (bf16[128,3072]{1,0:T(8,128)(2,1)}, bf16[128,3072]{1,0:T(8,128)(2,1)S(1)}, u32[]{:S(2)}) copy-start(bf16[128,3072]{1,0:T(8,128)(2,1)S(1)} %pad_maximum_fusion.1.refs_0_) | copy-start | bytes 2359300
  10.1 20.6 %collective-permute-start.2 = (bf16[128,3072]{1,0:T(8,128)(2,1)S(1)}, bf16[128,3072]{1,0:T(8,128)(2,1)S(1)}, u32[]{:S(2)}, u32[]{:S(2)}) collective-permute-start(bf16[128,3072]{1,0:T(8,128)(2,1)S(1)} %pad_maximum_fusion.1.refs_0_), channel_id=1, source_target_pairs={{0,4},{1,5},{2,6},{3,7},{4,0},{5,1},{6,2},{7,3},{8,12},{9,13},{10,... | collective-permute-start | bytes 2359304 | tf_op jit(solution)/shard_map/ppermute | solution.py:50
  13.1 20.2 %collective-permute-start = (bf16[128,3072]{1,0:T(8,128)(2,1)S(1)}, bf16[128,3072]{1,0:T(8,128)(2,1)S(1)}, u32[]{:S(2)}, u32[]{:S(2)}) collective-permute-start(bf16[128,3072]{1,0:T(8,128)(2,1)S(1)} %pad_maximum_fusion.1.refs_0_), channel_id=1, source_target_pairs={{0,2},{1,3},{2,0},{3,1},{4,6},{5,7},{6,4},{7,5},{8,10},{9,11},{10,... | collective-permute-start | bytes 2359304 | tf_op jit(solution)/shard_map/ppermute | solution.py:50
  14.7 45.8 %copy-start.1 = (bf16[128,4096]{1,0:T(8,128)(2,1)}, bf16[128,4096]{1,0:T(8,128)(2,1)S(1)}, u32[]{:S(2)}) copy-start(bf16[128,4096]{1,0:T(8,128)(2,1)S(1)} %pad_maximum_fusion.refs_0_) | copy-start | bytes 3145732
  30.7 4.9 %copy-start.5 = (bf16[128,3072]{1,0:T(8,128)(2,1)}, bf16[128,3072]{1,0:T(8,128)(2,1)S(1)}, u32[]{:S(2)}) copy-start(bf16[128,3072]{1,0:T(8,128)(2,1)S(1)} %collective-permute-done.2.refs_2_) | copy-start | bytes 2359300
  31.6 12.3 %collective-permute-start.3 = (bf16[64,3072]{1,0:T(8,128)(2,1)}, bf16[64,3072]{1,0:T(8,128)(2,1)S(1)}, u32[]{:S(2)}, u32[]{:S(2)}) collective-permute-start(bf16[64,3072]{1,0:T(8,128)(2,1)} %slice.29), channel_id=1, source_target_pairs={{0,2},{1,3},{2,0},{3,1},{4,6},{5,7},{6,4},{7,5},{8,10},{9,11},{10,... | collective-permute-start | bytes 1179656 | tf_op jit(solution)/shard_map/ppermute | solution.py:50
  33.3 2.9 %copy-start.6 = (bf16[128,3072]{1,0:T(8,128)(2,1)}, bf16[128,3072]{1,0:T(8,128)(2,1)S(1)}, u32[]{:S(2)}) copy-start(bf16[128,3072]{1,0:T(8,128)(2,1)S(1)} %collective-permute-done.refs_1_) | copy-start | bytes 2359300
  34.1 12.4 %collective-permute-start.1 = (bf16[64,3072]{1,0:T(8,128)(2,1)}, bf16[64,3072]{1,0:T(8,128)(2,1)}, u32[]{:S(2)}, u32[]{:S(2)}) collective-permute-start(bf16[64,3072]{1,0:T(8,128)(2,1)} %slice.28), channel_id=1, source_target_pairs={{0,4},{1,5},{2,6},{3,7},{4,0},{5,1},{6,2},{7,3},{8,12},{9,13},{10,... | collective-permute-start | bytes 1179656 | tf_op jit(solution)/shard_map/ppermute | solution.py:50
  35.6 33.2 %collective-permute-start.7 = (bf16[128,4096]{1,0:T(8,128)(2,1)S(1)}, bf16[128,4096]{1,0:T(8,128)(2,1)S(1)}, u32[]{:S(2)}, u32[]{:S(2)}) collective-permute-start(bf16[128,4096]{1,0:T(8,128)(2,1)S(1)} %pad_maximum_fusion.refs_0_), channel_id=1, source_target_pairs={{0,4},{1,5},{2,6},{3,7},{4,0},{5,1},{6,2},{7,3},{8,12},{9,13},{10,... | collective-permute-start | bytes 3145736 | tf_op jit(solution)/shard_map/ppermute | solution.py:50
  36.1 32.7 %collective-permute-start.6 = (bf16[128,4096]{1,0:T(8,128)(2,1)S(1)}, bf16[128,4096]{1,0:T(8,128)(2,1)}, u32[]{:S(2)}, u32[]{:S(2)}) collective-permute-start(bf16[128,4096]{1,0:T(8,128)(2,1)S(1)} %pad_maximum_fusion.refs_0_), channel_id=1, source_target_pairs={{0,2},{1,3},{2,0},{3,1},{4,6},{5,7},{6,4},{7,5},{8,10},{9,11},{10,... | collective-permute-start | bytes 3145736 | tf_op jit(solution)/shard_map/ppermute | solution.py:50
  43.8 5.1 %copy-start.11 = (bf16[64,3072]{1,0:T(8,128)(2,1)}, bf16[64,3072]{1,0:T(8,128)(2,1)S(1)}, u32[]{:S(2)}) copy-start(bf16[64,3072]{1,0:T(8,128)(2,1)S(1)} %collective-permute-done.3.refs_4_) | copy-start | bytes 1179652
  49.0 2.1 collective-permute-start.5
  49.0 78.3 %all-gather.11.cloned.1.call-start = ((), (), s32[]{:S(2)}) async-start(), calls=%async_computation.3 | async-start | bytes 3538944 | tf_op jit(solution)/shard_map/all_gather | solution.py:434
  51.1 0.8 copy-start.4
  60.6 22.0 %collective-permute-start.8 = (bf16[64,3072]{1,0:T(8,128)(2,1)}, bf16[64,3072]{1,0:T(8,128)(2,1)S(1)}, u32[]{:S(2)}, u32[]{:S(2)}) collective-permute-start(bf16[64,3072]{1,0:T(8,128)(2,1)} %get-tuple-element.69), channel_id=1, source_target_pairs={{0,2},{1,3},{2,0},{3,1},{4,6},{5,7},{6,4},{7,5},{8,10},{9,11},{10,... | collective-permute-start | bytes 1179656 | tf_op jit(solution)/shard_map/ppermute | solution.py:50
  60.9 22.6 %collective-permute-start.9 = (bf16[64,3072]{1,0:T(8,128)(2,1)}, bf16[64,3072]{1,0:T(8,128)(2,1)S(1)}, u32[]{:S(2)}, u32[]{:S(2)}) collective-permute-start(bf16[64,3072]{1,0:T(8,128)(2,1)} %get-tuple-element.70), channel_id=1, source_target_pairs={{0,4},{1,5},{2,6},{3,7},{4,0},{5,1},{6,2},{7,3},{8,12},{9,13},{10,... | collective-permute-start | bytes 1179656 | tf_op jit(solution)/shard_map/ppermute | solution.py:50
  62.6 20.9 %collective-permute-start.10 = (bf16[64,3072]{1,0:T(8,128)(2,1)}, bf16[64,3072]{1,0:T(8,128)(2,1)S(1)}, u32[]{:S(2)}, u32[]{:S(2)}) collective-permute-start(bf16[64,3072]{1,0:T(8,128)(2,1)} %get-tuple-element.71), channel_id=1, source_target_pairs={{0,6},{1,7},{2,4},{3,5},{4,2},{5,3},{6,0},{7,1},{8,14},{9,15},{10,... | collective-permute-start | bytes 1179656 | tf_op jit(solution)/shard_map/ppermute | solution.py:50
  68.9 10.4 %copy-start.3 = (bf16[128,4096]{1,0:T(8,128)(2,1)}, bf16[128,4096]{1,0:T(8,128)(2,1)S(1)}, u32[]{:S(2)}) copy-start(bf16[128,4096]{1,0:T(8,128)(2,1)S(1)} %collective-permute-done.7.refs_2_) | copy-start | bytes 3145732
  79.3 4.2 %copy-start.7 = (f32[64,3072]{1,0:T(8,128)S(1)}, f32[64,3072]{1,0:T(8,128)}, u32[]{:S(2)}) copy-start(f32[64,3072]{1,0:T(8,128)} %get-tuple-element.68) | copy-start | bytes 2359300
  84.5 80.5 %all-gather.9.cloned.1.call-start = ((), (), s32[]{:S(2)}) async-start(), calls=%async_computation.2 | async-start | bytes 4718592 | tf_op jit(solution)/shard_map/all_gather | solution.py:443
  84.7 25.2 %collective-permute-start.13 = (bf16[512,3072]{1,0:T(8,128)(2,1)}, bf16[512,3072]{1,0:T(8,128)(2,1)S(1)}, u32[]{:S(2)}, u32[]{:S(2)}) collective-permute-start(bf16[512,3072]{1,0:T(8,128)(2,1)} %pack.2.p0), channel_id=1, source_target_pairs={{0,1},{1,0},{2,3},{3,2},{4,5},{5,4},{6,7},{7,6},{8,9},{9,8},{10,11... | collective-permute-start | bytes 9437192 | tf_op jit(solution)/shard_map/ppermute | solution.py:50
  84.8 18.9 %collective-permute-start.11 = (bf16[64,4096]{1,0:T(8,128)(2,1)}, bf16[64,4096]{1,0:T(8,128)(2,1)}, u32[]{:S(2)}, u32[]{:S(2)}) collective-permute-start(bf16[64,4096]{1,0:T(8,128)(2,1)} %get-tuple-element.77), channel_id=1, source_target_pairs={{0,2},{1,3},{2,0},{3,1},{4,6},{5,7},{6,4},{7,5},{8,10},{9,11},{10,... | collective-permute-start | bytes 1572872 | tf_op jit(solution)/shard_map/ppermute | solution.py:50
  85.5 18.5 %collective-permute-start.12 = (bf16[64,4096]{1,0:T(8,128)(2,1)}, bf16[64,4096]{1,0:T(8,128)(2,1)}, u32[]{:S(2)}, u32[]{:S(2)}) collective-permute-start(bf16[64,4096]{1,0:T(8,128)(2,1)} %get-tuple-element.79), channel_id=1, source_target_pairs={{0,4},{1,5},{2,6},{3,7},{4,0},{5,1},{6,2},{7,3},{8,12},{9,13},{10,... | collective-permute-start | bytes 1572872 | tf_op jit(solution)/shard_map/ppermute | solution.py:50
  107.0 13.5 %collective-permute-start.14 = (bf16[32,4096]{1,0:T(8,128)(2,1)}, bf16[32,4096]{1,0:T(8,128)(2,1)S(1)}, u32[]{:S(2)}, u32[]{:S(2)}) collective-permute-start(bf16[32,4096]{1,0:T(8,128)(2,1)} %get-tuple-element.83), channel_id=1, source_target_pairs={{0,4},{1,5},{2,6},{3,7},{4,0},{5,1},{6,2},{7,3},{8,12},{9,13},{10,... | collective-permute-start | bytes 786440 | tf_op jit(solution)/shard_map/ppermute | solution.py:50
  108.5 13.4 %collective-permute-start.15 = (bf16[32,4096]{1,0:T(8,128)(2,1)}, bf16[32,4096]{1,0:T(8,128)(2,1)S(1)}, u32[]{:S(2)}, u32[]{:S(2)}) collective-permute-start(bf16[32,4096]{1,0:T(8,128)(2,1)} %get-tuple-element.84), channel_id=1, source_target_pairs={{0,2},{1,3},{2,0},{3,1},{4,6},{5,7},{6,4},{7,5},{8,10},{9,11},{10,... | collective-permute-start | bytes 786440 | tf_op jit(solution)/shard_map/ppermute | solution.py:50
  109.9 1.7 copy-start
  120.5 1.4 copy-start.12
  121.9 0.7 copy-start.13
  124.9 24.6 %collective-permute-start.17 = (bf16[64,4096]{1,0:T(8,128)(2,1)}, bf16[64,4096]{1,0:T(8,128)(2,1)S(1)}, u32[]{:S(2)}, u32[]{:S(2)}) collective-permute-start(bf16[64,4096]{1,0:T(8,128)(2,1)} %slice.31), channel_id=1, source_target_pairs={{0,2},{1,3},{2,0},{3,1},{4,6},{5,7},{6,4},{7,5},{8,10},{9,11},{10,... | collective-permute-start | bytes 1572872 | tf_op jit(solution)/shard_map/ppermute | solution.py:50
  127.3 22.2 %collective-permute-start.16 = (bf16[64,4096]{1,0:T(8,128)(2,1)}, bf16[64,4096]{1,0:T(8,128)(2,1)S(1)}, u32[]{:S(2)}, u32[]{:S(2)}) collective-permute-start(bf16[64,4096]{1,0:T(8,128)(2,1)} %slice.30), channel_id=1, source_target_pairs={{0,4},{1,5},{2,6},{3,7},{4,0},{5,1},{6,2},{7,3},{8,12},{9,13},{10,... | collective-permute-start | bytes 1572872 | tf_op jit(solution)/shard_map/ppermute | solution.py:50
  149.4 0.8 copy-start.9
  150.2 0.8 copy-start.10
  154.7 7.6 %collective-permute-start.18 = (bf16[512,4096]{1,0:T(8,128)(2,1)}, bf16[512,4096]{1,0:T(8,128)(2,1)}, u32[]{:S(2)}, u32[]{:S(2)}) collective-permute-start(bf16[512,4096]{1,0:T(8,128)(2,1)} %pack.3.p0), channel_id=1, source_target_pairs={{0,1},{1,0},{2,3},{3,2},{4,5},{5,4},{6,7},{7,6},{8,9},{9,8},{10,11... | collective-permute-start | bytes 12582920 | tf_op jit(solution)/shard_map/ppermute | solution.py:50
  183.3 24.5 %collective-permute-start.19 = (bf16[128,1024]{1,0:T(8,128)(2,1)}, bf16[128,1024]{1,0:T(8,128)(2,1)S(1)}, u32[]{:S(2)}, u32[]{:S(2)}) collective-permute-start(bf16[128,1024]{1,0:T(8,128)(2,1)} %get-tuple-element.101), channel_id=1, source_target_pairs={{0,8},{8,16},{16,24},{24,0},{1,9},{9,17},{17,25},{25,1},{2,10},{10... | collective-permute-start | bytes 786440 | tf_op jit(solution)/shard_map/ppermute | solution.py:54
  184.8 23.0 %collective-permute-start.20 = (bf16[128,1024]{1,0:T(8,128)(2,1)}, bf16[128,1024]{1,0:T(8,128)(2,1)S(1)}, u32[]{:S(2)}, u32[]{:S(2)}) collective-permute-start(bf16[128,1024]{1,0:T(8,128)(2,1)} %get-tuple-element.102), channel_id=1, source_target_pairs={{0,16},{8,24},{16,0},{24,8},{1,17},{9,25},{17,1},{25,9},{2,18},{10... | collective-permute-start | bytes 786440 | tf_op jit(solution)/shard_map/ppermute | solution.py:54
  187.2 20.6 %collective-permute-start.21 = (bf16[128,1024]{1,0:T(8,128)(2,1)}, bf16[128,1024]{1,0:T(8,128)(2,1)S(1)}, u32[]{:S(2)}, u32[]{:S(2)}) collective-permute-start(bf16[128,1024]{1,0:T(8,128)(2,1)} %get-tuple-element.103), channel_id=1, source_target_pairs={{0,24},{8,0},{16,8},{24,16},{1,25},{9,1},{17,9},{25,17},{2,26},{10... | collective-permute-start | bytes 786440 | tf_op jit(solution)/shard_map/ppermute | solution.py:54
  188.7 19.2 %copy-start.8 = (f32[128,1024]{1,0:T(8,128)S(1)}, f32[128,1024]{1,0:T(8,128)}, u32[]{:S(2)}) copy-start(f32[128,1024]{1,0:T(8,128)} %get-tuple-element.100) | copy-start | bytes 1572868
Sparse Core Ops, SparseCore 0:
  9.6 30.6 all-gather.4
  49.1 28.3 all-gather.6
  84.6 41.2 all-gather.10
  127.6 37.2 all-gather.8
